TPU v7x, 32 devices: a whole 2x2x4 slice. The times are simulated.
32 devices in a mesh: ctx: 8 (over z, y), fsdp: 4 (over x, core).
Axes of the slice: x: 2, y: 2, z: 4, core: 2. Of those that a mesh axis runs over, the one named last changes fastest.
Arguments:
- inputs: bfloat16 [2, 2048, 1024], P(None, ('ctx', 'fsdp')), may hold values from -6 to 6
- attn_gain: bfloat16 [1024], P('fsdp'), may hold values from 0.5 to 1.5
- attn_proj: bfloat16 [1024, 3072], P('fsdp'), may hold values from -0.1875 to 0.1875
- attn_out: bfloat16 [1024, 1024], P('fsdp'), may hold values from -6 to 6
- mlp_gain: bfloat16 [1024], P('fsdp'), may hold values from 0.5 to 1.5
- mlp_in: bfloat16 [1024, 5248], P('fsdp'), may hold values from -0.1875 to 0.1875
- mlp_out: bfloat16 [2624, 1024], P('fsdp'), may hold values from -0.125 to 0.125
- cotangent: bfloat16 [2, 2048, 1024], P(None, ('ctx', 'fsdp')), may hold values from -6 to 6
Outputs:
- outputs: bfloat16 [2, 2048, 1024], P(None, ('ctx', 'fsdp'))
- input_grad: float32 [2, 2048, 1024], P(None, ('ctx', 'fsdp'))
- attn_gain_grad: float32 [1024], P('fsdp')
- attn_proj_grad: float32 [1024, 3072], P('fsdp')
- attn_out_grad: float32 [1024, 1024], P('fsdp')
- mlp_gain_grad: float32 [1024], P('fsdp')
- mlp_in_grad: float32 [1024, 5248], P('fsdp')
- mlp_out_grad: float32 [2624, 1024], P('fsdp')
All inputs are finite; a program needn't handle non-finite values.
Results may differ from a plain program's by a relative error of at most 0.02.
Values may be sent and summed in bfloat16 or wider, within the bound.
A program may use at most 768 MiB of HBM per device.

v0:
```python
import functools

import jax
import jax.numpy as jnp
from jax import lax
from jax.experimental import pallas as pl
from jax.experimental.pallas import tpu as pltpu
from jax.sharding import PartitionSpec as P

HEADS = 16
HEAD_DIM = 64


eps = 1e-05
rope_base = 160000.0


def layer_norm(values, norm_gain):
    center = jnp.mean(values, axis=-1, keepdims=True)
    centred = values - center
    spread = jnp.mean(centred * centred, axis=-1, keepdims=True)
    return centred * lax.rsqrt(spread + eps) * norm_gain


def rotate(values, cos_table, sin_table):
    halfway = values.shape[-1] // 2
    turned = jnp.concatenate([-values[..., halfway:], values[..., :halfway]], axis=-1)
    return values * cos_table + turned * sin_table


def unrotate(gradient, cos_table, sin_table):
    halfway = gradient.shape[-1] // 2
    sined = gradient * sin_table
    return gradient * cos_table + jnp.concatenate(
        [sined[..., halfway:], -sined[..., :halfway]], axis=-1
    )


def angles(positions, head_size):
    exponent = jnp.arange(0, head_size, 2, dtype=jnp.float32) / head_size
    inverse = rope_base ** (-exponent)
    phases = positions.astype(jnp.float32)[:, None] * inverse[None, :]
    phases = jnp.concatenate([phases, phases], axis=-1)
    return (jnp.cos(phases)[:, None, :], jnp.sin(phases)[:, None, :])


def gated_unit(lifted):
    hidden_units = lifted.shape[-1] // 2
    return jax.nn.gelu(lifted[..., :hidden_units], approximate=False) * lifted[..., hidden_units:]


def as_heads(flat_rows, head_size):
    return flat_rows.reshape(flat_rows.shape[0], flat_rows.shape[1], -1, head_size)


def empty_state(seq_count, head_count, query_rows, head_size):
    return (
        jnp.full((seq_count, head_count, query_rows), -jnp.inf, jnp.float32),
        jnp.zeros((seq_count, head_count, query_rows), jnp.float32),
        jnp.zeros((seq_count, head_count, query_rows, head_size), jnp.float32),
    )


def forward_step(queries, scaling, state_now, shard_part):
    running_max, denominator, weighted = state_now
    key_part = as_heads(shard_part[0], queries.shape[3])
    value_part = as_heads(shard_part[1], queries.shape[3])
    scores = (
        jnp.einsum("sqhd,skhd->shqk", queries, key_part, preferred_element_type=jnp.float32)
        * scaling
    )
    new_max = jnp.max(scores, axis=-1)
    fading = jnp.exp(running_max - new_max)
    weights = jnp.exp(scores - new_max[..., None])
    denominator = denominator * fading + jnp.sum(weights, axis=-1)
    weighted = weighted * fading[..., None] + jnp.einsum(
        "shqk,skhd->shqd",
        weights.astype(jnp.bfloat16),
        value_part,
        preferred_element_type=jnp.float32,
    )
    return (new_max, denominator, weighted)


def query_step(queries, grad_out, log_total, inner_heads, scaling, shard_part):
    key_part = as_heads(shard_part[0], queries.shape[3])
    value_part = as_heads(shard_part[1], queries.shape[3])
    scores = (
        jnp.einsum("sqhd,skhd->shqk", queries, key_part, preferred_element_type=jnp.float32)
        * scaling
    )
    weights = jnp.exp(scores - log_total[..., None])
    weight_grad = jnp.einsum(
        "sqhd,skhd->shqk", grad_out, value_part, preferred_element_type=jnp.float32
    )
    score_grad = (weights * (weight_grad - inner_heads[..., None])).astype(jnp.bfloat16)
    return jnp.einsum("shqk,skhd->sqhd", score_grad, key_part, preferred_element_type=jnp.float32)


def key_step(key_heads, value_heads, scaling, shard_part):
    head_size = key_heads.shape[3]
    query_part = as_heads(shard_part[0].astype(jnp.bfloat16), head_size)
    grad_part = as_heads(shard_part[1].astype(jnp.bfloat16), head_size)
    log_part = shard_part[2].transpose(0, 2, 1)
    inner_part = shard_part[3].transpose(0, 2, 1)
    scores = (
        jnp.einsum("sqhd,skhd->shqk", query_part, key_heads, preferred_element_type=jnp.float32)
        * scaling
    )
    weights = jnp.exp(scores - log_part[..., None])
    value_grad = jnp.einsum(
        "shqk,sqhd->skhd",
        weights.astype(jnp.bfloat16),
        grad_part,
        preferred_element_type=jnp.float32,
    )
    weight_grad = jnp.einsum(
        "sqhd,skhd->shqk", grad_part, value_heads, preferred_element_type=jnp.float32
    )
    score_grad = (weights * (weight_grad - inner_part[..., None])).astype(jnp.bfloat16)
    key_grad = jnp.einsum(
        "shqk,sqhd->skhd", score_grad, query_part, preferred_element_type=jnp.float32
    )
    return (key_grad, value_grad)


MESH_ID = pl.DeviceIdType.MESH


def exchange_kernel(ctx_count, fsdp_count, x_ref, o_ref, send_sem, recv_sem, own_sem):
    count = ctx_count * fsdp_count
    me = lax.axis_index("ctx") * fsdp_count + lax.axis_index("fsdp")
    barrier = pltpu.get_barrier_semaphore()

    def target(step):
        place = lax.rem(me + step, count)
        return place, (place // fsdp_count, lax.rem(place, fsdp_count))

    def copy_to(step):
        place, device = target(step)
        return pltpu.make_async_remote_copy(
            src_ref=x_ref.at[place],
            dst_ref=o_ref.at[me],
            send_sem=send_sem.at[step],
            recv_sem=recv_sem.at[step],
            device_id=device,
            device_id_type=MESH_ID,
        )

    @pl.loop(1, count)
    def _(step):
        pl.semaphore_signal(barrier, inc=1, device_id=target(step)[1], device_id_type=MESH_ID)

    pl.semaphore_wait(barrier, count - 1)
    own = pltpu.make_async_copy(x_ref.at[me], o_ref.at[me], own_sem)
    own.start()

    @pl.loop(1, count)
    def _(step):
        copy_to(step).start()

    own.wait()

    @pl.loop(1, count)
    def _(step):
        copy_to(step).wait()


def exchange(blocks, ctx_count, fsdp_count, collective_id):
    count = ctx_count * fsdp_count
    return pl.pallas_call(
        functools.partial(exchange_kernel, ctx_count, fsdp_count),
        out_shape=jax.ShapeDtypeStruct(blocks.shape, blocks.dtype),
        in_specs=[pl.BlockSpec(memory_space=pl.ANY)],
        out_specs=pl.BlockSpec(memory_space=pl.ANY),
        scratch_shapes=[
            pltpu.SemaphoreType.DMA((count,)),
            pltpu.SemaphoreType.DMA((count,)),
            pltpu.SemaphoreType.DMA,
        ],
        compiler_params=pltpu.CompilerParams(collective_id=collective_id, has_side_effects=True),
    )(blocks)


def gather_kernel(spread, chunks, x_ref, o_ref, send_sem, recv_sem, own_sem):
    ctx, place = lax.axis_index("ctx"), lax.axis_index("fsdp")
    across = lax.rem(place + 2, 4)
    beside = place + 1 - 2 * lax.rem(place, 2)
    half = lax.rem(ctx, 2)
    other_ctx = ctx + 1 - 2 * half
    sibling, partner, neighbour = (ctx, beside), (ctx, across), (other_ctx, place)
    width = x_ref.shape[-1] // (2 * chunks if spread else chunks)
    mine = half * chunks if spread else 0
    theirs = (1 - half) * chunks

    def columns(index):
        return pl.ds(pl.multiple_of(index * width, 128), width)

    def send(src, dst, sem, device):
        return pltpu.make_async_remote_copy(
            src_ref=src,
            dst_ref=dst,
            send_sem=send_sem.at[sem],
            recv_sem=recv_sem.at[sem],
            device_id=device,
            device_id_type=MESH_ID,
        )

    def piece(index):
        return o_ref.at[across, :, columns(index)]

    barrier = pltpu.get_barrier_semaphore()
    partners = (sibling, partner, neighbour) if spread else (sibling, partner)
    for device in partners:
        pl.semaphore_signal(barrier, inc=1, device_id=device, device_id_type=MESH_ID)
    pl.semaphore_wait(barrier, len(partners))
    crossing = [
        send(
            x_ref.at[:, columns(mine + c)],
            o_ref.at[place, :, columns(mine + c)],
            c,
            partner,
        )
        for c in range(chunks)
    ]
    for copy in crossing:
        copy.start()
    started = list(crossing)
    whole = send(x_ref, o_ref.at[place], chunks, sibling)
    whole.start()
    own = pltpu.make_async_copy(x_ref, o_ref.at[place], own_sem)
    own.start()
    turned = []
    for c in range(chunks):
        crossing[c].wait_recv()
        if spread:
            turn = send(piece(mine + c), piece(mine + c), chunks + 1 + c, neighbour)
            turn.start()
            turned.append(turn)
        hand = send(piece(mine + c), piece(mine + c), 2 * chunks + 1 + c, sibling)
        hand.start()
        started.append(hand)
    handed = started[chunks:]
    for c in range(len(turned)):
        turned[c].wait_recv()
        hand = send(piece(theirs + c), piece(theirs + c), 3 * chunks + 1 + c, sibling)
        hand.start()
        handed.append(hand)
    whole.wait_recv()
    own.wait()
    for hand in handed:
        hand.wait_recv()
    for copy in crossing + turned + handed + [whole]:
        copy.wait_send()


def gather(block, spread, chunks, collective_id):
    rows, width = block.shape
    count = 4 * chunks + 1
    return pl.pallas_call(
        functools.partial(gather_kernel, spread, chunks),
        out_shape=jax.ShapeDtypeStruct((4, rows, width), block.dtype),
        in_specs=[pl.BlockSpec(memory_space=pl.ANY)],
        out_specs=pl.BlockSpec(memory_space=pl.ANY),
        scratch_shapes=[
            pltpu.SemaphoreType.DMA((count,)),
            pltpu.SemaphoreType.DMA((count,)),
            pltpu.SemaphoreType.DMA,
        ],
        compiler_params=pltpu.CompilerParams(collective_id=collective_id, has_side_effects=True),
    )(block).reshape(4 * rows, width)


TILE = 16
SLICE = 1536


def total_kernel(pair, lone, x_ref, o_ref, y_got, z_got, z_sent, e_got, send_sem, recv_sem):
    ctx, place = lax.axis_index("ctx"), lax.axis_index("fsdp")
    y = lax.rem(ctx, 2)
    z = ctx // 2
    firsts, lasts = 2 * pair, 2 * lone
    every = firsts + lasts

    def send(src, dst, sem, to_ctx):
        return pltpu.make_async_remote_copy(
            src_ref=src,
            dst_ref=dst,
            send_sem=send_sem.at[sem],
            recv_sem=recv_sem.at[sem],
            device_id=(to_ctx, place),
            device_id_type=MESH_ID,
        )

    y_side = ctx + 1 - 2 * y

    def rows(item, side):
        if item < firsts:
            return pl.ds(pl.multiple_of((side * firsts + item) * TILE, TILE), TILE)
        return pl.ds((firsts + item) * TILE, TILE)

    def end_of(item):
        return item // pair if item < firsts else (item - firsts) // lone

    def turn_of(item):
        return item % pair if item < firsts else (item - firsts) % lone

    def add(store, store_rows, terms):
        @pl.loop(0, x_ref.shape[1] // SLICE)
        def _(i):
            columns = pl.ds(pl.multiple_of(i * SLICE, SLICE), SLICE)
            total = terms[0][0][terms[0][1], columns].astype(jnp.float32)
            for ref, place_rows in terms[1:]:
                total += ref[place_rows, columns].astype(jnp.float32)
            store[store_rows, columns] = total.astype(jnp.bfloat16)

    def slot(item):
        return pl.ds(item * TILE, TILE)

    def pair_copy(item):
        return send(x_ref.at[rows(item, 1 - y), :], y_got.at[slot(item), :], item, y_side)

    def up_copy(item, to_z):
        return send(z_sent.at[slot(item), :], z_got.at[slot(item), :], firsts + item, 2 * to_z + y)

    def end_copy(item):
        return send(
            z_sent.at[slot(item), :],
            e_got.at[slot(item - firsts), :],
            firsts + every + item - firsts,
            y_side,
        )

    def down_copy(item, to_z):
        here = rows(item, y)
        return send(
            o_ref.at[here, :], o_ref.at[here, :], firsts + every + lasts + item, 2 * to_z + y
        )

    def back_copy(item):
        here = rows(item, y)
        return send(
            o_ref.at[here, :], o_ref.at[here, :], firsts + 2 * every + lasts + item, y_side
        )

    barrier = pltpu.get_barrier_semaphore()
    pl.semaphore_signal(barrier, inc=1, device_id=(y_side, place), device_id_type=MESH_ID)

    @pl.when(z > 0)
    def _():
        pl.semaphore_signal(barrier, inc=1, device_id=(ctx - 2, place), device_id_type=MESH_ID)

    @pl.when(z < 3)
    def _():
        pl.semaphore_signal(barrier, inc=1, device_id=(ctx + 2, place), device_id_type=MESH_ID)

    @pl.when((z == 0) | (z == 3))
    def _():
        pl.semaphore_wait(barrier, 2)

    @pl.when((z > 0) & (z < 3))
    def _():
        pl.semaphore_wait(barrier, 3)

    for turn in range(pair):
        for end in range(2):
            pair_copy(end * pair + turn).start()

    def steps(my_z):
        depth = lambda item: 3 - my_z if end_of(item) == 0 else my_z
        toward = lambda item: my_z - 1 if end_of(item) == 0 else my_z + 1
        away = lambda item: my_z + 1 if end_of(item) == 0 else my_z - 1
        events = []
        for item in range(every):
            wait = 1 if item < firsts else 0
            late = 0 if item < firsts else 1
            at = 2 * turn_of(item) + depth(item) + wait
            events.append((at, item, "up"))
            if depth(item) == 3 and late:
                events.append((at + 1, item, "meet"))
            if depth(item) < 3:
                events.append(
                    (2 * turn_of(item) + 3 + wait + late + 3 - depth(item), item, "down")
                )
        pending = []

        def start(copy):
            copy.start()
            pending.append(copy)

        def finish(item):
            if depth(item) > 0:
                start(down_copy(item, away(item)))
            if item < firsts:
                start(back_copy(item))

        for _, item, kind in sorted(events):
            if kind == "up":
                terms = [(x_ref, rows(item, y))]
                if item < firsts:
                    pair_copy(item).wait_recv()
                    terms.append((y_got, slot(item)))
                if depth(item) > 0:
                    up_copy(item, away(item)).wait_recv()
                    terms.append((z_got, slot(item)))
                if depth(item) == 3 and item < firsts:
                    add(o_ref, rows(item, y), terms)
                    finish(item)
                else:
                    add(z_sent, slot(item), terms)
                    if depth(item) == 3:
                        start(end_copy(item))
                    else:
                        start(up_copy(item, toward(item)))
            elif kind == "meet":
                end_copy(item).wait_recv()
                add(
                    o_ref,
                    rows(item, y),
                    [(z_sent, slot(item)), (e_got, slot(item - firsts))],
                )
                finish(item)
            else:
                down_copy(item, toward(item)).wait_recv()
                finish(item)
        for copy in pending:
            copy.wait_send()

    for my_z in range(4):
        pl.when(z == my_z)(functools.partial(steps, my_z))

    for item in range(firsts):
        pair_copy(item).wait_send()
        send(
            o_ref.at[rows(item, y), :],
            o_ref.at[rows(item, 1 - y), :],
            firsts + 2 * every + lasts + item,
            y_side,
        ).wait_recv()


def total_over_ctx(grads, collective_id):
    rows, width = grads.shape
    chunks = rows // TILE
    pair, lone = chunks // 8, chunks // 4
    items = 2 * pair + 2 * lone
    sems = 4 * pair + 2 * items + 2 * lone
    low = lambda count: pltpu.VMEM((count * TILE, width), jnp.bfloat16)
    return pl.pallas_call(
        functools.partial(total_kernel, pair, lone),
        out_shape=jax.ShapeDtypeStruct((rows, width), jnp.bfloat16),
        in_specs=[pl.BlockSpec(memory_space=pltpu.VMEM)],
        out_specs=pl.BlockSpec(memory_space=pltpu.VMEM),
        scratch_shapes=[
            low(2 * pair),
            low(items),
            low(items),
            low(2 * lone),
            pltpu.SemaphoreType.DMA((sems,)),
            pltpu.SemaphoreType.DMA((sems,)),
        ],
        compiler_params=pltpu.CompilerParams(
            collective_id=collective_id,
            has_side_effects=True,
            vmem_limit_bytes=48 * 1024 * 1024,
        ),
    )(grads)


def pack(blocks):
    half = blocks.shape[-2] // 2
    return jnp.concatenate([blocks[..., :half, :], blocks[..., half:, :]], axis=-1)


def unpack(blocks):
    half = blocks.shape[-1] // 2
    return jnp.concatenate([blocks[..., :half], blocks[..., half:]], axis=-2)


CONTRACT_LAST = (((1,), (1,)), ((), ()))
CONTRACT_FIRST = (((0,), (0,)), ((), ()))


def attend_kernel(q_ref, k_ref, v_ref, context_ref, log_ref):
    scores = lax.dot_general(
        q_ref[...], k_ref[...], CONTRACT_LAST, preferred_element_type=jnp.float32
    )
    top = jnp.max(scores, axis=-1, keepdims=True)
    weights = jnp.exp(scores - top)
    total = jnp.sum(weights, axis=-1, keepdims=True)
    weighted = jnp.dot(
        weights.astype(jnp.bfloat16), v_ref[...], preferred_element_type=jnp.float32
    )
    context_ref[...] = weighted / total
    log_ref[...] = top + jnp.log(total)


def attend(queries, key_rows, value_rows, block):
    rows, size = queries.shape
    return pl.pallas_call(
        attend_kernel,
        grid=(rows // block,),
        out_shape=(
            jax.ShapeDtypeStruct((rows, size), jnp.float32),
            jax.ShapeDtypeStruct((rows, 1), jnp.float32),
        ),
        in_specs=[
            pl.BlockSpec((block, size), lambda i: (i, 0)),
            pl.BlockSpec((rows, size), lambda i: (0, 0)),
            pl.BlockSpec((rows, size), lambda i: (0, 0)),
        ],
        out_specs=(
            pl.BlockSpec((block, size), lambda i: (i, 0)),
            pl.BlockSpec((block, 1), lambda i: (i, 0)),
        ),
        compiler_params=pltpu.CompilerParams(vmem_limit_bytes=48 * 1024 * 1024),
    )(queries, key_rows, value_rows)


def attend_back_kernel(
    q_ref, k_ref, v_ref, context_ref, log_ref, grad_ref, dq_ref, dk_ref, dv_ref
):
    @pl.when(pl.program_id(0) == 0)
    def _():
        dk_ref[...] = jnp.zeros_like(dk_ref)
        dv_ref[...] = jnp.zeros_like(dv_ref)

    grad = grad_ref[...]
    inner = jnp.sum(grad.astype(jnp.float32) * context_ref[...], axis=-1, keepdims=True)
    scores = lax.dot_general(
        q_ref[...], k_ref[...], CONTRACT_LAST, preferred_element_type=jnp.float32
    )
    probs = jnp.exp(scores - log_ref[...])
    prob_grad = lax.dot_general(
        grad, v_ref[...], CONTRACT_LAST, preferred_element_type=jnp.float32
    )
    score_grad = (probs * (prob_grad - inner)).astype(jnp.bfloat16)
    dv_ref[...] += lax.dot_general(
        probs.astype(jnp.bfloat16), grad, CONTRACT_FIRST, preferred_element_type=jnp.float32
    )
    dk_ref[...] += lax.dot_general(
        score_grad, q_ref[...], CONTRACT_FIRST, preferred_element_type=jnp.float32
    )
    dq_ref[...] = jnp.dot(score_grad, k_ref[...], preferred_element_type=jnp.float32)


def attend_back(queries, key_rows, value_rows, context, log_total, grad, block):
    rows, size = queries.shape
    part = pl.BlockSpec((block, size), lambda i: (i, 0))
    whole = pl.BlockSpec((rows, size), lambda i: (0, 0))
    return pl.pallas_call(
        attend_back_kernel,
        grid=(rows // block,),
        out_shape=(jax.ShapeDtypeStruct((rows, size), jnp.float32),) * 3,
        in_specs=[
            part,
            whole,
            whole,
            part,
            pl.BlockSpec((block, 1), lambda i: (i, 0)),
            part,
        ],
        out_specs=(part, whole, whole),
        compiler_params=pltpu.CompilerParams(vmem_limit_bytes=48 * 1024 * 1024),
    )(queries, key_rows, value_rows, context, log_total, grad)


def by_head_forward(mixed_rows, cos_table, sin_table, scaling):
    seq_count, row_count, _, head_count, head_size = mixed_rows.shape
    ctx_count, fsdp_count = lax.axis_size("ctx"), lax.axis_size("fsdp")
    count = ctx_count * fsdp_count
    queries = rotate(mixed_rows[:, :, 0], cos_table, sin_table).astype(jnp.bfloat16) * scaling
    key_rows = rotate(mixed_rows[:, :, 1], cos_table, sin_table).astype(jnp.bfloat16)
    value_rows = mixed_rows[:, :, 2].astype(jnp.bfloat16)
    to_head = lambda rows: rows.transpose(0, 2, 1, 3).reshape(count, row_count, head_size)
    sent = jnp.concatenate(
        [
            jnp.concatenate([to_head(queries), to_head(key_rows)], axis=-1),
            pack(to_head(value_rows)),
        ],
        axis=1,
    )
    got = exchange(sent, ctx_count, fsdp_count, 1)
    flat = lambda rows: rows.reshape(count * row_count, head_size)
    queries = flat(got[:, :row_count, :head_size])
    key_rows = flat(got[:, :row_count, head_size:])
    value_rows = flat(unpack(got[:, row_count:]))
    context, log_total = attend(queries, key_rows, value_rows, 256)
    back = exchange(
        pack(context.astype(jnp.bfloat16).reshape(count, row_count, head_size)),
        ctx_count,
        fsdp_count,
        2,
    )
    context_low = (
        unpack(back)
        .reshape(seq_count, head_count, row_count, head_size)
        .transpose(0, 2, 1, 3)
        .reshape(seq_count * row_count, head_count * head_size)
    )
    return context_low, (queries, key_rows, value_rows, context, log_total)


def by_head_back(context_grad, saved, scaling, after):
    seq_count, row_count, head_count, head_size = context_grad.shape
    ctx_count, fsdp_count = lax.axis_size("ctx"), lax.axis_size("fsdp")
    count = ctx_count * fsdp_count
    queries, key_rows, value_rows, context, log_total = saved
    sent = pack(context_grad.transpose(0, 2, 1, 3).reshape(count, row_count, head_size))
    grad = unpack(exchange(sent, ctx_count, fsdp_count, 3)).reshape(count * row_count, head_size)
    query_grad, key_grad, value_grad = attend_back(
        queries, key_rows, value_rows, context, log_total, grad, 256
    )
    cos_all, sin_all = angles(jnp.arange(count * row_count, dtype=jnp.int32), head_size)
    cos_all, sin_all = cos_all[:, 0], sin_all[:, 0]
    query_pre = unrotate(query_grad * scaling, cos_all, sin_all).astype(jnp.bfloat16)
    key_pre = unrotate(key_grad, cos_all, sin_all).astype(jnp.bfloat16)
    split = lambda rows: rows.reshape(count, row_count, head_size)
    sent = jnp.concatenate(
        [
            jnp.concatenate([split(query_pre), split(key_pre)], axis=-1),
            pack(split(value_grad.astype(jnp.bfloat16))),
        ],
        axis=1,
    )
    sent, after = lax.optimization_barrier((sent, after))
    got = exchange(sent, ctx_count, fsdp_count, 4)
    parts = jnp.stack(
        [got[:, :row_count, :head_size], got[:, :row_count, head_size:], unpack(got[:, row_count:])]
    )
    return (
        parts.reshape(3, seq_count, head_count, row_count, head_size)
        .transpose(1, 3, 0, 2, 4)
        .reshape(seq_count * row_count, 3 * head_count * head_size)
    ), after


def by_block_forward(mixed_rows, cos_table, sin_table, scaling):
    seq_count, row_count, _, head_count, head_size = mixed_rows.shape
    width = head_count * head_size
    queries = rotate(mixed_rows[:, :, 0], cos_table, sin_table).astype(jnp.bfloat16)
    key_flat = (
        rotate(mixed_rows[:, :, 1], cos_table, sin_table)
        .astype(jnp.bfloat16)
        .reshape(seq_count, row_count, width)
    )
    value_flat = mixed_rows[:, :, 2].astype(jnp.bfloat16).reshape(seq_count, row_count, width)
    key_block, value_block = (
        lax.all_gather(key_flat, "fsdp", axis=1, tiled=True),
        lax.all_gather(value_flat, "fsdp", axis=1, tiled=True),
    )
    start_state = empty_state(seq_count, head_count, row_count, head_size)
    running_max, denominator, weighted = forward_step(
        queries,
        scaling,
        start_state,
        (
            lax.all_gather(key_block, "ctx", axis=1, tiled=True),
            lax.all_gather(value_block, "ctx", axis=1, tiled=True),
        ),
    )
    context = (weighted / denominator[..., None]).transpose(0, 2, 1, 3)
    log_total = running_max + jnp.log(denominator)
    context_low = context.reshape(seq_count * row_count, width).astype(jnp.bfloat16)
    return context_low, (queries, key_block, value_block, context, log_total, cos_table, sin_table)


def by_block_back(context_grad, saved, scaling, after):
    seq_count, row_count, head_count, head_size = context_grad.shape
    width = head_count * head_size
    queries, key_block, value_block, context, log_total, cos_table, sin_table = saved
    inner = jnp.sum(context_grad.astype(jnp.float32) * context, axis=-1)
    inner_heads = inner.transpose(0, 2, 1)
    log_rows = log_total.transpose(0, 2, 1)
    query_grad = query_step(
        queries,
        context_grad,
        log_total,
        inner_heads,
        scaling,
        (
            lax.all_gather(key_block, "ctx", axis=1, tiled=True),
            lax.all_gather(value_block, "ctx", axis=1, tiled=True),
        ),
    )
    block_len = key_block.shape[1]
    query_wide = queries.reshape(seq_count, row_count, width).astype(jnp.float32)
    grad_wide = context_grad.reshape(seq_count, row_count, width).astype(jnp.float32)
    key_grad, value_grad = key_step(
        as_heads(key_block, head_size),
        as_heads(value_block, head_size),
        scaling,
        (
            lax.all_gather(query_wide, "ctx", axis=1, tiled=True),
            lax.all_gather(grad_wide, "ctx", axis=1, tiled=True),
            lax.all_gather(log_rows, "ctx", axis=1, tiled=True),
            lax.all_gather(inner, "ctx", axis=1, tiled=True),
        ),
    )
    own = lambda grad: lax.psum_scatter(
        grad.reshape(seq_count, block_len, width), "fsdp", scatter_dimension=1, tiled=True
    ).reshape(seq_count, row_count, head_count, head_size)
    query_pre = unrotate(query_grad * scaling, cos_table, sin_table)
    key_pre = unrotate(own(key_grad) * scaling, cos_table, sin_table)
    return (
        jnp.stack([query_pre, key_pre, own(value_grad)], axis=2)
        .reshape(seq_count * row_count, 3 * width)
        .astype(jnp.bfloat16)
    ), after


def group_rows(rows):
    return lax.all_gather(rows, "fsdp", axis=0, tiled=True)


def group_columns(arrays):
    count = lax.axis_size("fsdp")
    widths = [rows.shape[1] // count for rows in arrays]
    sent = jnp.stack(
        [
            jnp.concatenate(
                [rows[:, f * width : (f + 1) * width] for rows, width in zip(arrays, widths)],
                axis=1,
            )
            for f in range(count)
        ]
    )
    got = lax.all_to_all(sent, "fsdp", split_axis=0, concat_axis=0, tiled=True)
    got = got.reshape(-1, sum(widths))
    edges = [sum(widths[:i]) for i in range(len(widths) + 1)]
    return [got[:, edges[i] : edges[i + 1]] for i in range(len(widths))]


def weight_grad(left, right):
    return jnp.einsum("tw,tf->wf", left, right, preferred_element_type=jnp.float32)


def on_device(inputs, attn_gain, attn_proj, attn_out, mlp_gain, mlp_in, mlp_out, cotangent):
    seq_count, row_count, model_width = inputs.shape
    head_size = HEAD_DIM
    head_count = HEADS
    scaling = head_size ** (-0.5)
    fsdp_count = lax.axis_size("fsdp")
    fsdp_place = lax.axis_index("fsdp")
    device_count = lax.axis_size("ctx") * fsdp_count
    one_head_each = device_count == seq_count * head_count
    start_row = (lax.axis_index("ctx") * fsdp_count + fsdp_place) * row_count
    cos_table, sin_table = angles(start_row + jnp.arange(row_count, dtype=jnp.int32), head_size)
    tokens = seq_count * row_count
    gain_width = own_rows = attn_gain.shape[0]
    gains = lax.all_gather(jnp.stack([attn_gain, mlp_gain]), "fsdp", axis=1, tiled=True).astype(
        jnp.float32
    )
    gain_one, gain_two = gains[0], gains[1]
    ctx_count = lax.axis_size("ctx")
    small = one_head_each and fsdp_count == 4 and ctx_count == 8
    proj_full, out_full, lift_full, down_full = (
        gather(attn_proj, True, 3, 6)
        if small
        else lax.all_gather(attn_proj, "fsdp", axis=0, tiled=True),
        lax.all_gather(attn_out, "fsdp", axis=0, tiled=True),
        lax.all_gather(mlp_in, "fsdp", axis=0, tiled=True),
        lax.all_gather(mlp_out, "fsdp", axis=0, tiled=True),
    )
    states = inputs.astype(jnp.float32)
    normed, norm_back_one = jax.vjp(layer_norm, states, gain_one)
    normed_low = normed.astype(jnp.bfloat16).reshape(tokens, model_width)
    mixed_rows = jnp.dot(normed_low, proj_full, preferred_element_type=jnp.float32).reshape(
        seq_count, row_count, 3, head_count, head_size
    )
    attention, attention_back = (
        (by_head_forward, by_head_back) if one_head_each else (by_block_forward, by_block_back)
    )
    context_low, saved = attention(mixed_rows, cos_table, sin_table, scaling)
    branch = jnp.dot(context_low, out_full, preferred_element_type=jnp.float32).reshape(
        seq_count, row_count, model_width
    )
    middle = states + branch
    normed_two, norm_back_two = jax.vjp(layer_norm, middle, gain_two)
    normed_two_low = normed_two.astype(jnp.bfloat16).reshape(tokens, model_width)
    lifted = jnp.dot(normed_two_low, lift_full, preferred_element_type=jnp.float32)
    gate_out, gated_back = jax.vjp(gated_unit, lifted)
    gate_low = gate_out.astype(jnp.bfloat16)
    outputs = (
        middle
        + jnp.dot(gate_low, down_full, preferred_element_type=jnp.float32).reshape(
            seq_count, row_count, model_width
        )
    ).astype(jnp.bfloat16)
    seed_rows = cotangent.reshape(tokens, model_width)
    gate_grad = jnp.einsum("td,fd->tf", seed_rows, down_full, preferred_element_type=jnp.float32)
    lifted_grad = gated_back(gate_grad)[0].astype(jnp.bfloat16)
    normed_two_grad = jnp.einsum(
        "tf,wf->tw", lifted_grad, lift_full, preferred_element_type=jnp.float32
    ).reshape(seq_count, row_count, model_width)
    middle_part, gain_two_grad = norm_back_two(normed_two_grad)
    middle_grad = cotangent.astype(jnp.float32) + middle_part
    middle_low = middle_grad.reshape(tokens, model_width).astype(jnp.bfloat16)
    context_grad = (
        jnp.einsum("tv,wv->tw", middle_low, out_full, preferred_element_type=jnp.float32)
        .astype(jnp.bfloat16)
        .reshape(seq_count, row_count, head_count, head_size)
    )
    normed_two_part, gate_part, context_part, normed_part = group_columns(
        (normed_two_low, gate_low, context_low, normed_low)
    )
    seed_group = group_rows(seed_rows)
    joined = group_rows(jnp.concatenate([lifted_grad, middle_low], axis=1))
    lift_grad = weight_grad(normed_two_part, joined[:, : lifted_grad.shape[1]])
    out_grad = weight_grad(context_part, joined[:, lifted_grad.shape[1] :])
    down_grad = weight_grad(gate_part, seed_group)
    first_grads = tuple(grad.astype(jnp.bfloat16) for grad in (lift_grad, down_grad, out_grad))
    mixed_grad, first_grads = attention_back(context_grad, saved, scaling, first_grads)
    normed_grad = jnp.einsum(
        "tm,wm->tw", mixed_grad, proj_full, preferred_element_type=jnp.float32
    ).reshape(seq_count, row_count, model_width)
    state_part, gain_one_grad = norm_back_one(normed_grad)
    input_grad = middle_grad + state_part
    mixed_group = gather(mixed_grad, False, 4, 7) if small else group_rows(mixed_grad)
    proj_grad = weight_grad(normed_part, mixed_group).astype(jnp.bfloat16)
    grads = (*first_grads, proj_grad)
    if small:
        sheet = [grad.reshape(own_rows, -1) for grad in grads]
        widths = [grad.shape[1] for grad in sheet]
        spare = -sum(widths) % SLICE
        sheet = jnp.concatenate(
            [sheet[0], sheet[2], sheet[3], sheet[1], jnp.zeros((own_rows, spare), jnp.bfloat16)],
            axis=1,
        )
        sums = total_over_ctx(sheet, 8)
        edges = [0, widths[0], widths[0] + widths[2], widths[0] + widths[2] + widths[3]]
        lift_sum, out_sum, proj_sum, down_sum = (
            sums[:, edges[0] : edges[1]],
            sums[:, edges[1] : edges[2]],
            sums[:, edges[2] : edges[3]],
            sums[:, edges[3] : edges[3] + widths[1]].reshape(mlp_out.shape),
        )
    else:
        lift_sum, down_sum, out_sum, proj_sum = lax.psum(grads, "ctx")
    lift_sum, down_sum, out_sum, proj_sum = (
        total.astype(jnp.float32) for total in (lift_sum, down_sum, out_sum, proj_sum)
    )
    gain_grads = jnp.stack([gain_one_grad, gain_two_grad])
    if small:
        shares = gain_grads.reshape(2, fsdp_count, gain_width).transpose(1, 0, 2)
        shares = jnp.concatenate([shares, jnp.zeros((fsdp_count, 6, gain_width))], axis=1)
        shares = jnp.concatenate([shares] * ctx_count, axis=0)
        gain_own = jnp.sum(exchange(shares, ctx_count, fsdp_count, 5), axis=0)
    else:
        gain_sums = lax.psum(gain_grads, ("ctx", "fsdp"))
        gain_own = lax.dynamic_slice_in_dim(gain_sums, fsdp_place * gain_width, gain_width, axis=1)
    return (
        outputs,
        input_grad,
        gain_own[0],
        proj_sum,
        out_sum,
        gain_own[1],
        lift_sum,
        down_sum,
    )


def solution(mesh):
    in_specs = (
        P(None, ("ctx", "fsdp"), None),
        P("fsdp"),
        P("fsdp", None),
        P("fsdp", None),
        P("fsdp"),
        P("fsdp", None),
        P("fsdp", None),
        P(None, ("ctx", "fsdp"), None),
    )
    out_specs = (
        P(None, ("ctx", "fsdp"), None),
        P(None, ("ctx", "fsdp"), None),
        P("fsdp"),
        P("fsdp", None),
        P("fsdp", None),
        P("fsdp"),
        P("fsdp", None),
        P("fsdp", None),
    )
    return jax.shard_map(
        on_device, mesh=mesh, in_specs=in_specs, out_specs=out_specs, check_vma=False
    )
```

profile of v0, /device:TPU:0, one launch (start us, length us, event | category | flops | bytes accessed | tf_op | source)
XLA Modules:
  0.0 570.1 jit_solution(15463182366156632771)
XLA Ops:
  11.0 6.0 %all_gather.18 = bf16[2,1024]{1,0:T(2,128)(2,1)S(1)} all-gather(bf16[2,256]{1,0:T(2,128)(2,1)S(1)} %pad_maximum_fusion.10), channel_id=1, replica_groups=mesh['ctx'=8,'fsdp'=4] {'fsdp'}, dimensions={1}, use_global_device_ids=true | all-gather | bytes 5120 | tf_op jit(solution)/shard_map/all_gather | solution.py:751
  17.0 51.1 %shard_map.143 = bf16[4,256,3072]{2,1,0:T(8,128)(2,1)} custom-call(bf16[256,3072]{1,0:T(8,128)(2,1)} %x_ref.1), custom_call_target="tpu_custom_call" | custom-call | tf_op jit(solution)/shard_map/pallas_call | solution.py:260
  68.1 8.7 %copy.56 = bf16[1024,3072]{0,1:T(8,128)(2,1)} copy(bf16[1024,3072]{1,0:T(8,128)(2,1)} %bitcast.117) | data formatting | bytes 12582912 | tf_op jit(solution)/shard_map/reshape | solution.py:271
  77.0 4.5 fusion.43
  95.1 18.5 %shard_map.144 = bf16[32,96,128]{2,1,0:T(8,128)(2,1)} custom-call(bf16[32,96,128]{2,1,0:T(8,128)(2,1)} %maximum_maximum_fusion.x_ref), custom_call_target="tpu_custom_call" | custom-call | tf_op jit(solution)/shard_map/pallas_call | solution.py:171
  115.3 8.5 %shard_map.145 = (f32[2048,64]{1,0:T(8,128)S(1)}, f32[2048,1]{1,0:T(8,128)S(1)}) custom-call(bf16[2048,64]{1,0:T(8,128)(2,1)S(1)} %bitcast.114, bf16[2048,64]{1,0:T(8,128)(2,1)S(1)} %bitcast.112, bf16[2048,64]{1,0:T(8,128)(2,1)S(1)} %bitcast.110), custom_call_target="tpu_custom_call" | custom-call | tf_op jit(solution)/shard_map/pallas_call | solution.py:500
  125.8 15.9 %shard_map.146 = bf16[32,32,128]{2,1,0:T(8,128)(2,1)} custom-call(bf16[32,32,128]{2,1,0:T(8,128)(2,1)} %pad_maximum_fusion.7.x_ref), custom_call_target="tpu_custom_call" | custom-call | tf_op jit(solution)/shard_map/pallas_call | solution.py:171
  146.8 7.3 %fusion.70 = f32[128,5248]{1,0:T(8,128)} fusion(bf16[128,1024]{1,0:T(8,128)(2,1)S(1)} %bitcast.122, bf16[1024,5248]{1,0:T(8,128)(2,1)} %all-gather.8.cloned.1.call-done), kind=kOutput, calls=%fused_computation.149 | convolution fusion | flops 1375731712 | bytes 13697024 | tf_op jit(solution)/shard_map/dot_general | solution.py:781
  154.1 17.1 %all-gather.10.cloned.1.call-done = bf16[2624,1024]{1,0:T(8,128)(2,1)} async-done(((bf16[656,1024]{1,0:T(8,128)(2,1)}), bf16[2624,1024]{1,0:T(8,128)(2,1)}) %all-gather.10.cloned.1.call-update) | async-done | bytes 5373968 | tf_op jit(solution)/shard_map/all_gather | solution.py:763
  171.2 7.0 %fusion.38 = (f32[128,2624]{1,0:T(8,128)S(1)}, f32[128,2624]{1,0:T(8,128)S(1)}, f32[128,2624]{1,0:T(8,128)S(1)}) fusion(f32[128,5248]{1,0:T(8,128)} %fusion.70, bf16[128,1024]{1,0:T(8,128)(2,1)S(1)} %bitcast.127, bf16[2624,1024]{1,0:T(8,128)(2,1)} %all-gather.10.cloned.1.call-done), kind=kOutput, calls=%fused_computation.93 | convolution fusion | flops 709697536 | bytes 11010048 | tf_op jit(solution)/shard_map/td,fd->tf/dot_general | solution.py:791
  212.9 4.5 all-to-all-start
  222.9 33.2 %shard_map.147 = bf16[32,32,128]{2,1,0:T(8,128)(2,1)} custom-call(bf16[32,32,128]{2,1,0:T(8,128)(2,1)} %pad_maximum_fusion.8.x_ref), custom_call_target="tpu_custom_call" | custom-call | tf_op jit(solution)/shard_map/pallas_call | solution.py:171
  257.5 14.1 %shard_map.148 = (f32[2048,64]{1,0:T(8,128)S(1)}, f32[2048,64]{1,0:T(8,128)S(1)}, f32[2048,64]{1,0:T(8,128)S(1)}) custom-call(bf16[2048,64]{1,0:T(8,128)(2,1)S(1)} %bitcast.115, bf16[2048,64]{1,0:T(8,128)(2,1)S(1)} %bitcast.113, bf16[2048,64]{1,0:T(8,128)(2,1)S(1)} %bitcast.111, f32[2048,64]{1,0:T(8,128)} %copy-done, f32[2048,1]{1,0:T(8,128)} %copy-done.1, ...), custom_call_target="tpu_custom_call" | custom-call | tf_op jit(solution)/shard_map/pallas_call | solution.py:551
  275.9 4.8 fusion.18
  294.0 5.6 convolution_convert_fusion
  299.6 18.2 %shard_map.149 = bf16[32,96,128]{2,1,0:T(8,128)(2,1)} custom-call(bf16[32,96,128]{2,1,0:T(8,128)(2,1)} %maximum_maximum_fusion.1.x_ref), custom_call_target="tpu_custom_call" | custom-call | tf_op jit(solution)/shard_map/pallas_call | solution.py:171
  323.2 26.6 %shard_map.151 = bf16[4,128,3072]{2,1,0:T(8,128)(2,1)} custom-call(bf16[128,3072]{1,0:T(8,128)(2,1)} %reshape.266.x_ref), custom_call_target="tpu_custom_call" | custom-call | tf_op jit(solution)/shard_map/pallas_call | solution.py:260
  352.9 4.2 reshape.268
  357.7 11.4 %concatenate.113.x_ref = bf16[256,12288]{1,0:T(8,128)(2,1)} concatenate(bf16[256,5248]{1,0:T(8,128)(2,1)} %convolution_convert_fusion, bf16[256,1024]{1,0:T(8,128)(2,1)} %convolution_convert_fusion.3, bf16[256,3072]{1,0:T(8,128)(2,1)S(1)} %convolution_convert_fusion.1, bf16[256,2624]{1,0:T(8,128)(2,1)} %reshape.268, bf16[256,320]{1,0:T(8,128)(2,1)} %broadcast_in_dim.28), dimensions={1} | concatenate | bytes 12582912 | tf_op jit(solution)/shard_map/concatenate | solution.py:826
  369.1 158.1 %shard_map.152 = bf16[256,12288]{1,0:T(8,128)(2,1)} custom-call(bf16[256,12288]{1,0:T(8,128)(2,1)} %concatenate.113.x_ref), custom_call_target="tpu_custom_call" | custom-call | tf_op jit(solution)/shard_map/pallas_call | solution.py:449
  530.2 4.5 slice_convert_fusion
  541.4 4.3 reshape.269
  545.6 5.1 fusion.33
  551.9 8.8 %shard_map.150 = f32[32,8,256]{2,1,0:T(8,128)} custom-call(f32[32,8,256]{2,1,0:T(8,128)} %copy-done.23), custom_call_target="tpu_custom_call" | custom-call | tf_op jit(solution)/shard_map/pallas_call | solution.py:171
  (187 shorter events, 107.6 us)
Async XLA Ops:
  7.2 137.1 %all-gather.6.cloned.1.call-start = ((), (), s32[]{:S(2)}) async-start(), calls=%async_computation.1 | async-start | bytes 2621440 | tf_op jit(solution)/shard_map/all_gather | solution.py:761
  7.9 138.9 %all-gather.8.cloned.1.call-start = ((), (), s32[]{:S(2)}) async-start(), calls=%async_computation.2 | async-start | bytes 13434880 | tf_op jit(solution)/shard_map/all_gather | solution.py:762
  8.7 162.6 %all-gather.10.cloned.1.call-start = ((), (), s32[]{:S(2)}) async-start(), calls=%async_computation.3 | async-start | bytes 6717440 | tf_op jit(solution)/shard_map/all_gather | solution.py:763
  9.4 278.5 %all-gather.14.cloned.1.call-start = ((), (), s32[]{:S(2)}) async-start(), calls=%async_computation.5 | async-start | bytes 1310720 | tf_op jit(solution)/shard_map/all_gather | solution.py:713
  10.0 281.6 %all-gather.12.cloned.1.call-start = ((), (), s32[]{:S(2)}) async-start(), calls=%async_computation.4 | async-start | bytes 8028160 | tf_op jit(solution)/shard_map/all_gather | solution.py:713
  10.1 73.7 %copy-start.28 = (f32[32]{0:T(128)}, f32[32]{0:T(128)S(1)}, u32[]{:S(2)}) copy-start(f32[32]{0:T(128)S(1)} %negate_power_fusion) | copy-start | bytes 388
  77.0 4.5 copy-start.21
  146.8 24.4 %copy-start.16 = (bf16[2,64,1024]{2,1,0:T(8,128)(2,1)S(1)}, bf16[2,64,1024]{2,1,0:T(8,128)(2,1)}, u32[]{:S(2)}) copy-start(bf16[2,64,1024]{2,1,0:T(8,128)(2,1)} %param.15) | copy-start | bytes 786436
  171.2 7.0 %copy-start.6 = (f32[128,5248]{1,0:T(8,128)S(1)}, f32[128,5248]{1,0:T(8,128)}, u32[]{:S(2)}) copy-start(f32[128,5248]{1,0:T(8,128)} %fusion.70) | copy-start | bytes 8060932
  178.2 4.6 copy-start.2
  179.1 7.6 %copy-start.10 = (bf16[128,2624]{1,0:T(8,128)(2,1)}, bf16[128,2624]{1,0:T(8,128)(2,1)S(1)}, u32[]{:S(2)}) copy-start(bf16[128,2624]{1,0:T(8,128)(2,1)S(1)} %get-tuple-element.33) | copy-start | bytes 2015236
  182.8 3.6 copy-start.4
  191.3 3.2 copy-start.5
  192.6 3.2 copy-start.24
  195.8 2.1 copy-start.22
  195.8 2.8 copy-start.29
  197.2 2.5 copy-start.11
  212.9 4.5 copy-start.15
  212.9 73.4 %all-to-all-start = ((bf16[4,128,1424]{1,2,0:T(8,128)(2,1)}), bf16[4,128,1424]{1,2,0:T(8,128)(2,1)}, u32[]{:S(2)}, u32[]{:S(2)}) async-start(bf16[4,128,1424]{1,2,0:T(8,128)(2,1)} %copy.66), calls=%async_computation | async-start | bytes 2916352 | tf_op jit(solution)/shard_map/all_to_all | solution.py:728
  287.8 6.2 %copy-start.20 = (bf16[512,1424]{0,1:T(8,128)(2,1)}, bf16[512,1424]{0,1:T(8,128)(2,1)S(1)}, u32[]{:S(2)}) copy-start(bf16[512,1424]{0,1:T(8,128)(2,1)S(1)} %copy_bitcast_fusion) | copy-start | bytes 4374532
  545.6 5.1 copy-start.27
  550.7 11.6 %copy-start.7 = (f32[2,64,1024]{2,1,0:T(8,128)S(1)}, f32[2,64,1024]{2,1,0:T(8,128)}, u32[]{:S(2)}) copy-start(f32[2,64,1024]{2,1,0:T(8,128)} %get-tuple-element.62) | copy-start | bytes 1572868
  550.7 11.5 %copy-start.17 = (bf16[2,64,1024]{2,1,0:T(8,128)(2,1)S(1)}, bf16[2,64,1024]{2,1,0:T(8,128)(2,1)}, u32[]{:S(2)}) copy-start(bf16[2,64,1024]{2,1,0:T(8,128)(2,1)} %param.15) | copy-start | bytes 786436
  550.7 11.5 %copy-start.25 = (f32[2,64]{1,0:T(2,128)S(1)}, f32[2,64]{1,0:T(2,128)}, u32[]{:S(2)}) copy-start(f32[2,64]{1,0:T(2,128)} %copy-done.24) | copy-start | bytes 1540
  (14 other events, 17.0 us)
Sparse Core Ops, SparseCore 0:
  9.6 36.5 all-gather.5
  47.7 80.1 all-gather.7
  129.5 41.7 all-gather.9
  172.6 17.0 all-gather.13
  196.0 65.9 all-gather.11
where the time goes:
time: 578 us; the launch traced here: 570 us
  Pallas kernels  353 us (61%)
  local copies, waits for them, and re-layouts  70.5 us (12%)
  matrix products  50.9 us (9%)
  other arithmetic  50.5 us (9%)
  waiting for transfers between devices  19.8 us (3%)
  between operations  14.8 us (3%)
  blocking collectives  5.97 us (1%)
    pallas_call x1, Pallas kernels, total_over_ctx(): pl.pallas_call(functools.partial(total_kernel, pair, lone), out_shape=jax...  158 us
    pallas_call x5, Pallas kernels, exchange(): pl.pallas_call(functools.partial(exchange_kernel, ctx_count, fsdp_count),...  94.6 us
    pallas_call x2, Pallas kernels, gather(): pl.pallas_call(functools.partial(gather_kernel, spread, chunks), out_shap...  77.7 us
    all_gather x1, waiting for transfers between devices, on_device(): lax.all_gather(mlp_out, 'fsdp', axis=0, tiled=True)  17.1 us
    dot_general x4, matrix products, weight_grad(): jnp.einsum('tw,tf->wf', left, right, preferred_element_type=jnp.float32)  14.7 us
    pallas_call x1, Pallas kernels, attend_back(): pl.pallas_call(attend_back_kernel, grid=(rows // block,), out_shape=(jax....  14.1 us
    convert_element_type x4, other arithmetic, on_device(): total.astype(jnp.float32)  13.1 us
  transfers between devices with their start and end apart: 6, of which 1 were waited for; matrix products, arithmetic and copies ran while one was open for 18% of the time, Pallas kernels for 25%

commit v1 on v0

--- a/solution.py
+++ b/solution.py
@@ -623,7 +623,8 @@
         ],
         axis=1,
     )
-    sent, after = lax.optimization_barrier((sent, after))
+    if after:
+        sent, after = lax.optimization_barrier((sent, after))
     got = exchange(sent, ctx_count, fsdp_count, 4)
     parts = jnp.stack(
         [got[:, :row_count, :head_size], got[:, :row_count, head_size:], unpack(got[:, row_count:])]
@@ -733,6 +734,83 @@
 
 def weight_grad(left, right):
     return jnp.einsum("tw,tf->wf", left, right, preferred_element_type=jnp.float32)
+
+
+AXES = ("ctx", "fsdp")
+
+
+def routes(move):
+    pairs = []
+    for z in range(4):
+        for y in range(2):
+            for x in range(2):
+                for core in range(2):
+                    to = move(z, y, x, core)
+                    if to is not None:
+                        source = ((z * 2 + y) * 2 + x) * 2 + core
+                        pairs.append((source, ((to[0] * 2 + to[1]) * 2 + to[2]) * 2 + to[3]))
+    return pairs
+
+
+TO_X = routes(lambda z, y, x, core: (z, y, 1 - x, core))
+TO_Y = routes(lambda z, y, x, core: (z, 1 - y, x, core))
+TO_CORE = routes(lambda z, y, x, core: (z, y, x, 1 - core))
+INWARD = routes(lambda z, y, x, core: {0: (1, y, x, core), 3: (2, y, x, core)}.get(z))
+MIDDLE = routes(lambda z, y, x, core: {1: (2, y, x, core), 2: (1, y, x, core)}.get(z))
+OUTWARD = routes(lambda z, y, x, core: {1: (0, y, x, core), 2: (3, y, x, core)}.get(z))
+
+
+def over(array, route):
+    return lax.ppermute(array, AXES, route)
+
+
+def half_of(array, index):
+    width = array.shape[1] // 2
+    return jnp.where(index == 0, array[:, :width], array[:, width:])
+
+
+def plane_left(parts, x):
+    own = jnp.concatenate([half_of(part, x) for part in parts], axis=1)
+    away = jnp.concatenate([half_of(part, 1 - x) for part in parts], axis=1)
+    over_x = over(away, TO_X)
+    return jnp.concatenate([own, over_x, over(own, TO_Y), over(over_x, TO_Y)], axis=0)
+
+
+def plane_right(part, y, width):
+    first, last = part[:, :width], part[:, part.shape[1] - width :]
+    own = jnp.where(y == 0, first, last)
+    over_y = over(jnp.where(y == 0, last, first), TO_Y)
+    return jnp.concatenate([own, over(own, TO_X), over_y, over(over_y, TO_X)], axis=0)
+
+
+def core_sum(left, right, core):
+    both = weight_grad(left, right).astype(jnp.bfloat16)
+    both = both.reshape(2, both.shape[0] // 2, both.shape[1])
+    away = jnp.where(core == 0, both[1], both[0])
+    own = jnp.where(core == 0, both[0], both[1])
+    return added(own, over(away, TO_CORE))
+
+
+def added(one, other):
+    total = (one.astype(jnp.float32) + other.astype(jnp.float32)).astype(jnp.bfloat16)
+    return lax.optimization_barrier(total)
+
+
+def line_sum(part, z):
+    part = added(part, over(part, INWARD))
+    total = added(part, over(part, MIDDLE))
+    outer = over(total, OUTWARD)
+    return lax.optimization_barrier(jnp.where((z == 0) | (z == 3), outer, total))
+
+
+def ctx_sum(part, z, y, full, pieces):
+    width = part.shape[1] // pieces
+    sums = [line_sum(part[:, i * width : (i + 1) * width], z) for i in range(pieces)]
+    swapped = [over(total, TO_Y) for total in sums]
+    own, other = jnp.concatenate(sums, axis=1), jnp.concatenate(swapped, axis=1)
+    low, high = jnp.where(y == 0, own, other), jnp.where(y == 0, other, own)
+    skip = 2 * part.shape[1] - full
+    return jnp.concatenate([low, high[:, skip:]], axis=1).astype(jnp.float32)
 
 
 def on_device(inputs, attn_gain, attn_proj, attn_out, mlp_gain, mlp_in, mlp_out, cotangent):
@@ -801,54 +879,52 @@
         .astype(jnp.bfloat16)
         .reshape(seq_count, row_count, head_count, head_size)
     )
-    normed_two_part, gate_part, context_part, normed_part = group_columns(
-        (normed_two_low, gate_low, context_low, normed_low)
-    )
-    seed_group = group_rows(seed_rows)
-    joined = group_rows(jnp.concatenate([lifted_grad, middle_low], axis=1))
-    lift_grad = weight_grad(normed_two_part, joined[:, : lifted_grad.shape[1]])
-    out_grad = weight_grad(context_part, joined[:, lifted_grad.shape[1] :])
-    down_grad = weight_grad(gate_part, seed_group)
-    first_grads = tuple(grad.astype(jnp.bfloat16) for grad in (lift_grad, down_grad, out_grad))
-    mixed_grad, first_grads = attention_back(context_grad, saved, scaling, first_grads)
+    norms = normed_two_low, context_low, normed_low
+    if small:
+        z, y = lax.axis_index("ctx") // 2, lax.axis_index("ctx") % 2
+        x, core = fsdp_place // 2, fsdp_place % 2
+        left = plane_left(norms, x)
+        gate_left = plane_left((gate_low,), x)
+        seed_right = plane_right(seed_rows, y, model_width // 2)
+        lifted_width = lifted_grad.shape[1]
+        lift_half = -(-lifted_width // 256) * 128
+        lift_right = plane_right(lifted_grad, y, lift_half)
+        middle_right = plane_right(middle_low, y, model_width // 2)
+        each = left.shape[1] // 3
+        down_part = core_sum(gate_left, seed_right, core)
+        lift_part = core_sum(left[:, :each], lift_right, core)
+        out_part = core_sum(left[:, each : 2 * each], middle_right, core)
+        down_sum = ctx_sum(down_part, z, y, model_width, 1)
+        lift_sum = ctx_sum(lift_part, z, y, lifted_width, 3)
+        out_sum = ctx_sum(out_part, z, y, model_width, 1)
+        mixed_grad, _ = attention_back(context_grad, saved, scaling, ())
+        mixed_right = plane_right(mixed_grad, y, mixed_grad.shape[1] // 2)
+        proj_part = core_sum(left[:, 2 * each :], mixed_right, core)
+        proj_sum = ctx_sum(proj_part, z, y, mixed_grad.shape[1], 2)
+    else:
+        normed_two_part, gate_part, context_part, normed_part = group_columns(
+            (normed_two_low, gate_low, context_low, normed_low)
+        )
+        seed_group = group_rows(seed_rows)
+        joined = group_rows(jnp.concatenate([lifted_grad, middle_low], axis=1))
+        lift_grad = weight_grad(normed_two_part, joined[:, : lifted_grad.shape[1]])
+        out_grad = weight_grad(context_part, joined[:, lifted_grad.shape[1] :])
+        down_grad = weight_grad(gate_part, seed_group)
+        first_grads = tuple(grad.astype(jnp.bfloat16) for grad in (lift_grad, down_grad, out_grad))
+        mixed_grad, first_grads = attention_back(context_grad, saved, scaling, first_grads)
+        mixed_group = group_rows(mixed_grad)
+        proj_grad = weight_grad(normed_part, mixed_group).astype(jnp.bfloat16)
+        lift_sum, down_sum, out_sum, proj_sum = (
+            total.astype(jnp.float32) for total in lax.psum((*first_grads, proj_grad), "ctx")
+        )
     normed_grad = jnp.einsum(
         "tm,wm->tw", mixed_grad, proj_full, preferred_element_type=jnp.float32
     ).reshape(seq_count, row_count, model_width)
     state_part, gain_one_grad = norm_back_one(normed_grad)
     input_grad = middle_grad + state_part
-    mixed_group = gather(mixed_grad, False, 4, 7) if small else group_rows(mixed_grad)
-    proj_grad = weight_grad(normed_part, mixed_group).astype(jnp.bfloat16)
-    grads = (*first_grads, proj_grad)
-    if small:
-        sheet = [grad.reshape(own_rows, -1) for grad in grads]
-        widths = [grad.shape[1] for grad in sheet]
-        spare = -sum(widths) % SLICE
-        sheet = jnp.concatenate(
-            [sheet[0], sheet[2], sheet[3], sheet[1], jnp.zeros((own_rows, spare), jnp.bfloat16)],
-            axis=1,
-        )
-        sums = total_over_ctx(sheet, 8)
-        edges = [0, widths[0], widths[0] + widths[2], widths[0] + widths[2] + widths[3]]
-        lift_sum, out_sum, proj_sum, down_sum = (
-            sums[:, edges[0] : edges[1]],
-            sums[:, edges[1] : edges[2]],
-            sums[:, edges[2] : edges[3]],
-            sums[:, edges[3] : edges[3] + widths[1]].reshape(mlp_out.shape),
-        )
-    else:
-        lift_sum, down_sum, out_sum, proj_sum = lax.psum(grads, "ctx")
-    lift_sum, down_sum, out_sum, proj_sum = (
-        total.astype(jnp.float32) for total in (lift_sum, down_sum, out_sum, proj_sum)
-    )
     gain_grads = jnp.stack([gain_one_grad, gain_two_grad])
-    if small:
-        shares = gain_grads.reshape(2, fsdp_count, gain_width).transpose(1, 0, 2)
-        shares = jnp.concatenate([shares, jnp.zeros((fsdp_count, 6, gain_width))], axis=1)
-        shares = jnp.concatenate([shares] * ctx_count, axis=0)
-        gain_own = jnp.sum(exchange(shares, ctx_count, fsdp_count, 5), axis=0)
-    else:
-        gain_sums = lax.psum(gain_grads, ("ctx", "fsdp"))
-        gain_own = lax.dynamic_slice_in_dim(gain_sums, fsdp_place * gain_width, gain_width, axis=1)
+    gain_sums = lax.psum(gain_grads, ("ctx", "fsdp"))
+    gain_own = lax.dynamic_slice_in_dim(gain_sums, fsdp_place * gain_width, gain_width, axis=1)
     return (
         outputs,
         input_grad,

time: 578 us -> 582 us (level)
  Pallas kernels: 353 us -> 141 us
  waiting for transfers between devices: 19.8 us -> 172 us
  starting transfers between devices: 4.64 us -> 63.2 us
  blocking collectives: 5.97 us -> 54 us
  local copies, waits for them, and re-layouts: 70.5 us -> 35.1 us
  matrix products: 50.9 us -> 43.2 us
    ppermute x0 -> x50, waiting for transfers between devices: none -> 170 us  [over(): return lax.ppermute(array, AXES, route)]
    pallas_call x1 -> x0, Pallas kernels: 158 us -> none  [total_over_ctx(): pl.pallas_call(functools.partial(total_kernel, pair, lone), out_shape=jax...]
    ppermute x0 -> x50, starting transfers between devices: none -> 63.1 us  [over(): return lax.ppermute(array, AXES, route)]
    psum x0 -> x1, blocking collectives: none -> 49 us  [on_device(): gain_sums = lax.psum(gain_grads, ('ctx', 'fsdp'))]
    pallas_call x5 -> x4, Pallas kernels: 94.6 us -> 66.2 us  [exchange(): pl.pallas_call(functools.partial(exchange_kernel, ctx_count, fsdp_count),...]
    pallas_call x2 -> x1, Pallas kernels: 77.7 us -> 52 us  [gather(): pl.pallas_call(functools.partial(gather_kernel, spread, chunks), out_shap...]
    concatenate x6 -> x2, local copies, waits for them, and re-layouts: 18.3 us -> 0.08 us  [ctx_sum(): jnp.concatenate(swapped, axis=1)]
    all_gather x1, waiting for transfers between devices: 17.1 us -> 0.01 us  [on_device(): lax.all_gather(mlp_out, 'fsdp', axis=0, tiled=True)]
  transfers between devices with their start and end apart: 6 -> 53, of which waited for: 1 -> 23; matrix products, arithmetic and copies ran while one was open for 18% -> 20% of each run, Pallas kernels for 25% -> 25%
where the time goes in v1:
time: 582 us; the launch traced here: 573 us
  waiting for transfers between devices  172 us (30%)
  Pallas kernels  141 us (24%)
  starting transfers between devices  63.2 us (11%)
  blocking collectives  54 us (9%)
  other arithmetic  49.6 us (9%)
  matrix products  43.2 us (7%)
  local copies, waits for them, and re-layouts  35.1 us (6%)
  between operations  15.4 us (3%)
    ppermute x50, waiting for transfers between devices, over(): return lax.ppermute(array, AXES, route)  170 us
    pallas_call x4, Pallas kernels, exchange(): pl.pallas_call(functools.partial(exchange_kernel, ctx_count, fsdp_count),...  66.2 us
    ppermute x50, starting transfers between devices, over(): return lax.ppermute(array, AXES, route)  63.1 us
    pallas_call x1, Pallas kernels, gather(): pl.pallas_call(functools.partial(gather_kernel, spread, chunks), out_shap...  52 us
    psum x1, blocking collectives, on_device(): gain_sums = lax.psum(gain_grads, ('ctx', 'fsdp'))  49 us
    pallas_call x1, Pallas kernels, attend_back(): pl.pallas_call(attend_back_kernel, grid=(rows // block,), out_shape=(jax....  14.1 us
  transfers between devices with their start and end apart: 53, of which 23 were waited for; matrix products, arithmetic and copies ran while one was open for 20% of the time, Pallas kernels for 25%

profile of v1, /device:TPU:0, one launch (start us, length us, event | category | flops | bytes accessed | tf_op | source)
XLA Modules:
  0.0 573.4 jit_solution(2538936252163251148)
XLA Ops:
  9.4 52.0 %shard_map.143 = bf16[4,256,3072]{2,1,0:T(8,128)(2,1)} custom-call(bf16[256,3072]{1,0:T(8,128)(2,1)} %x_ref.1), custom_call_target="tpu_custom_call" | custom-call | tf_op jit(solution)/shard_map/pallas_call | solution.py:260
  61.5 8.7 %copy.26 = bf16[1024,3072]{0,1:T(8,128)(2,1)} copy(bf16[1024,3072]{1,0:T(8,128)(2,1)} %bitcast.104) | data formatting | bytes 12582912 | tf_op jit(solution)/shard_map/reshape | solution.py:271
  90.8 18.6 %shard_map.144 = bf16[32,96,128]{2,1,0:T(8,128)(2,1)} custom-call(bf16[32,96,128]{2,1,0:T(8,128)(2,1)} %maximum_maximum_fusion.x_ref), custom_call_target="tpu_custom_call" | custom-call | tf_op jit(solution)/shard_map/pallas_call | solution.py:171
  111.0 8.5 %shard_map.145 = (f32[2048,64]{1,0:T(8,128)S(1)}, f32[2048,1]{1,0:T(8,128)S(1)}) custom-call(bf16[2048,64]{1,0:T(8,128)(2,1)S(1)} %bitcast.101, bf16[2048,64]{1,0:T(8,128)(2,1)S(1)} %bitcast.99, bf16[2048,64]{1,0:T(8,128)(2,1)S(1)} %bitcast.97), custom_call_target="tpu_custom_call" | custom-call | tf_op jit(solution)/shard_map/pallas_call | solution.py:500
  121.5 15.6 %shard_map.146 = bf16[32,32,128]{2,1,0:T(8,128)(2,1)} custom-call(bf16[32,32,128]{2,1,0:T(8,128)(2,1)} %pad_maximum_fusion.10.x_ref), custom_call_target="tpu_custom_call" | custom-call | tf_op jit(solution)/shard_map/pallas_call | solution.py:171
  148.7 15.3 %collective-permute-done = bf16[128,1536]{1,0:T(8,128)(2,1)} collective-permute-done((bf16[128,1536]{1,0:T(8,128)(2,1)S(1)}, bf16[128,1536]{1,0:T(8,128)(2,1)}, u32[]{:S(2)}, u32[]{:S(2)}) %collective-permute-start) | collective-permute-done | bytes 393248 | tf_op jit(solution)/shard_map/ppermute | solution.py:764
  167.2 7.6 %collective-permute-done.2 = bf16[128,1536]{1,0:T(8,128)(2,1)S(1)} collective-permute-done((bf16[128,1536]{1,0:T(8,128)(2,1)}, bf16[128,1536]{1,0:T(8,128)(2,1)S(1)}, u32[]{:S(2)}, u32[]{:S(2)}) %collective-permute-start.2) | collective-permute-done | bytes 393248 | tf_op jit(solution)/shard_map/ppermute | solution.py:764
  177.2 7.3 %fusion.104 = f32[128,5248]{1,0:T(8,128)} fusion(bf16[128,1024]{1,0:T(8,128)(2,1)} %bitcast.111, bf16[1024,5248]{1,0:T(8,128)(2,1)} %all-gather.6.cloned.1.call-done), kind=kOutput, calls=%fused_computation.237 | convolution fusion | flops 1375731712 | bytes 13697024 | tf_op jit(solution)/shard_map/dot_general | solution.py:859
  184.5 7.1 %fusion.73 = (f32[128,2624]{1,0:T(8,128)S(1)}, f32[128,2624]{1,0:T(8,128)S(1)}, f32[128,2624]{1,0:T(8,128)S(1)}) fusion(f32[128,5248]{1,0:T(8,128)} %fusion.104, bf16[128,1024]{1,0:T(8,128)(2,1)} %bitcast.114, bf16[2624,1024]{1,0:T(8,128)(2,1)} %all-gather.8.cloned.1.call-done), kind=kOutput, calls=%fused_computation.162 | convolution fusion | flops 709697536 | bytes 11010048 | tf_op jit(solution)/shard_map/td,fd->tf/dot_general | solution.py:869
  213.6 11.5 %shard_map.147 = bf16[32,32,128]{2,1,0:T(8,128)(2,1)} custom-call(bf16[32,32,128]{2,1,0:T(8,128)(2,1)} %pad_maximum_fusion.11.x_ref), custom_call_target="tpu_custom_call" | custom-call | tf_op jit(solution)/shard_map/pallas_call | solution.py:171
  226.4 14.1 %shard_map.148 = (f32[2048,64]{1,0:T(8,128)S(1)}, f32[2048,64]{1,0:T(8,128)S(1)}, f32[2048,64]{1,0:T(8,128)S(1)}) custom-call(bf16[2048,64]{1,0:T(8,128)(2,1)S(1)} %bitcast.102, bf16[2048,64]{1,0:T(8,128)(2,1)S(1)} %bitcast.100, bf16[2048,64]{1,0:T(8,128)(2,1)S(1)} %bitcast.98, f32[2048,64]{1,0:T(8,128)} %copy-done, f32[2048,1]{1,0:T(8,128)} %copy-done.1, ...), custom_call_target="tpu_custom_call" | custom-call | tf_op jit(solution)/shard_map/pallas_call | solution.py:551
  255.3 20.5 %shard_map.149 = bf16[32,96,128]{2,1,0:T(8,128)(2,1)} custom-call(bf16[32,96,128]{2,1,0:T(8,128)(2,1)} %maximum_maximum_fusion.1.x_ref), custom_call_target="tpu_custom_call" | custom-call | tf_op jit(solution)/shard_map/pallas_call | solution.py:171
  300.1 9.7 %collective-permute-done.17 = bf16[128,512]{1,0:T(8,128)(2,1)S(1)} collective-permute-done((bf16[128,512]{1,0:T(8,128)(2,1)S(1)}, bf16[128,512]{1,0:T(8,128)(2,1)S(1)}, u32[]{:S(2)}, u32[]{:S(2)}) %collective-permute-start.17) | collective-permute-done | bytes 131104 | tf_op jit(solution)/shard_map/ppermute | solution.py:764
  312.4 49.0 %psum.7 = f32[2,1024]{1,0:T(2,128)S(1)} all-reduce(f32[2,1024]{1,0:T(2,128)S(1)} %pad_maximum_fusion.13), channel_id=1, replica_groups=mesh['ctx'=8,'fsdp'=4] {'ctx','fsdp'}, use_global_device_ids=true, to_apply=%region_10.11 | all-reduce | flops 2048 | bytes 16384 | tf_op jit(solution)/shard_map/psum | solution.py:926
  385.0 8.4 %collective-permute-done.24 = bf16[128,2688]{1,0:T(8,128)(2,1)S(1)} collective-permute-done((bf16[128,2688]{1,0:T(8,128)(2,1)}, bf16[128,2688]{1,0:T(8,128)(2,1)S(1)}, u32[]{:S(2)}, u32[]{:S(2)}) %collective-permute-start.24) | collective-permute-done | bytes 688160 | tf_op jit(solution)/shard_map/ppermute | solution.py:764
  395.3 10.2 %collective-permute-done.5 = bf16[128,1536]{1,0:T(8,128)(2,1)S(1)} collective-permute-done((bf16[128,1536]{1,0:T(8,128)(2,1)}, bf16[128,1536]{1,0:T(8,128)(2,1)S(1)}, u32[]{:S(2)}, u32[]{:S(2)}) %collective-permute-start.5) | collective-permute-done | bytes 393248 | tf_op jit(solution)/shard_map/ppermute | solution.py:764
  409.1 6.8 %collective-permute-done.21 = bf16[256,512]{1,0:T(8,128)(2,1)S(1)} collective-permute-done((bf16[256,512]{1,0:T(8,128)(2,1)S(1)}, bf16[256,512]{1,0:T(8,128)(2,1)S(1)}, u32[]{:S(2)}, u32[]{:S(2)}) %collective-permute-start.21) | collective-permute-done | bytes 262176 | tf_op jit(solution)/shard_map/ppermute | solution.py:764
  425.3 18.3 %collective-permute-done.10 = bf16[256,768]{1,0:T(8,128)(2,1)S(1)} collective-permute-done((bf16[256,768]{1,0:T(8,128)(2,1)S(1)}, bf16[256,768]{1,0:T(8,128)(2,1)S(1)}, u32[]{:S(2)}, u32[]{:S(2)}) %collective-permute-start.10) | collective-permute-done | bytes 393248 | tf_op jit(solution)/shard_map/ppermute | solution.py:764
  455.8 17.0 %collective-permute-done.9 = bf16[256,768]{1,0:T(8,128)(2,1)S(1)} collective-permute-done((bf16[256,768]{1,0:T(8,128)(2,1)S(1)}, bf16[256,768]{1,0:T(8,128)(2,1)S(1)}, u32[]{:S(2)}, u32[]{:S(2)}) %collective-permute-start.9) | collective-permute-done | bytes 393248 | tf_op jit(solution)/shard_map/ppermute | solution.py:764
  473.8 7.3 %collective-permute-done.12 = bf16[256,768]{1,0:T(8,128)(2,1)S(1)} collective-permute-done((bf16[256,768]{1,0:T(8,128)(2,1)S(1)}, bf16[256,768]{1,0:T(8,128)(2,1)S(1)}, u32[]{:S(2)}, u32[]{:S(2)}) %collective-permute-start.12) | collective-permute-done | bytes 393248 | tf_op jit(solution)/shard_map/ppermute | solution.py:764
  481.9 6.5 %collective-permute-start.27 = (bf16[256,896]{1,0:T(8,128)(2,1)S(1)}, bf16[256,896]{1,0:T(8,128)(2,1)S(1)}, u32[]{:S(2)}, u32[]{:S(2)}) collective-permute-start(bf16[256,896]{1,0:T(8,128)(2,1)S(1)} %get-tuple-element.35), channel_id=1, source_target_pairs={{0,8},{1,9},{2,10},{3,11},{4,12},{5,13},{6,14},{7,15},{24,16},{25,... | collective-permute-start | bytes 1376264 | tf_op jit(solution)/shard_map/ppermute | solution.py:764
  499.2 7.8 %collective-permute-done.30 = bf16[256,896]{1,0:T(8,128)(2,1)S(1)} collective-permute-done((bf16[256,896]{1,0:T(8,128)(2,1)S(1)}, bf16[256,896]{1,0:T(8,128)(2,1)S(1)}, u32[]{:S(2)}, u32[]{:S(2)}) %collective-permute-start.30) | collective-permute-done | bytes 458784 | tf_op jit(solution)/shard_map/ppermute | solution.py:764
  521.7 17.7 %collective-permute-done.29 = bf16[256,896]{1,0:T(8,128)(2,1)S(1)} collective-permute-done((bf16[256,896]{1,0:T(8,128)(2,1)S(1)}, bf16[256,896]{1,0:T(8,128)(2,1)S(1)}, u32[]{:S(2)}, u32[]{:S(2)}) %collective-permute-start.29) | collective-permute-done | bytes 458784 | tf_op jit(solution)/shard_map/ppermute | solution.py:764
  539.8 8.0 %collective-permute-done.32 = bf16[256,896]{1,0:T(8,128)(2,1)S(1)} collective-permute-done((bf16[256,896]{1,0:T(8,128)(2,1)S(1)}, bf16[256,896]{1,0:T(8,128)(2,1)S(1)}, u32[]{:S(2)}, u32[]{:S(2)}) %collective-permute-start.32) | collective-permute-done | bytes 458784 | tf_op jit(solution)/shard_map/ppermute | solution.py:764
  (313 shorter events, 204.5 us)
Async XLA Ops:
  7.2 132.6 %all-gather.4.cloned.1.call-start = ((), (), s32[]{:S(2)}) async-start(), calls=%async_computation | async-start | bytes 2621440 | tf_op jit(solution)/shard_map/all_gather | solution.py:839
  7.9 169.3 %all-gather.6.cloned.1.call-start = ((), (), s32[]{:S(2)}) async-start(), calls=%async_computation.1 | async-start | bytes 13434880 | tf_op jit(solution)/shard_map/all_gather | solution.py:840
  8.7 175.9 %all-gather.8.cloned.1.call-start = ((), (), s32[]{:S(2)}) async-start(), calls=%async_computation.2 | async-start | bytes 6717440 | tf_op jit(solution)/shard_map/all_gather | solution.py:841
  146.3 215.1 %collective-permute-start.43 = (bf16[128,512]{1,0:T(8,128)(2,1)}, bf16[128,512]{1,0:T(8,128)(2,1)}, u32[]{:S(2)}, u32[]{:S(2)}) collective-permute-start(bf16[128,512]{1,0:T(8,128)(2,1)} %get-tuple-element.81), channel_id=1, source_target_pairs={{0,4},{1,5},{2,6},{3,7},{4,0},{5,1},{6,2},{7,3},{8,12},{9,13},{10,... | collective-permute-start | bytes 393224 | tf_op jit(solution)/shard_map/ppermute | solution.py:764
  148.3 216.1 %collective-permute-start.42 = (bf16[128,512]{1,0:T(8,128)(2,1)}, bf16[128,512]{1,0:T(8,128)(2,1)}, u32[]{:S(2)}, u32[]{:S(2)}) collective-permute-start(bf16[128,512]{1,0:T(8,128)(2,1)} %get-tuple-element.80), channel_id=1, source_target_pairs={{0,2},{1,3},{2,0},{3,1},{4,6},{5,7},{6,4},{7,5},{8,10},{9,11},{10,... | collective-permute-start | bytes 393224 | tf_op jit(solution)/shard_map/ppermute | solution.py:764
  295.8 67.9 %collective-permute-start.39 = (bf16[128,1312]{1,0:T(8,128)(2,1)}, bf16[128,1312]{1,0:T(8,128)(2,1)}, u32[]{:S(2)}, u32[]{:S(2)}) collective-permute-start(bf16[128,1312]{1,0:T(8,128)(2,1)} %get-tuple-element.67), channel_id=1, source_target_pairs={{0,2},{1,3},{2,0},{3,1},{4,6},{5,7},{6,4},{7,5},{8,10},{9,11},{10,... | collective-permute-start | bytes 1007624 | tf_op jit(solution)/shard_map/ppermute | solution.py:764
  311.0 55.3 %collective-permute-start.18 = (bf16[256,512]{1,0:T(8,128)(2,1)}, bf16[256,512]{1,0:T(8,128)(2,1)S(1)}, u32[]{:S(2)}, u32[]{:S(2)}) collective-permute-start(bf16[256,512]{1,0:T(8,128)(2,1)} %broadcast_select_fusion.20), channel_id=1, source_target_pairs={{0,1},{1,0},{2,3},{3,2},{4,5},{5,4},{6,7},{7,6},{8,9},{9,8},{10,11... | collective-permute-start | bytes 786440 | tf_op jit(solution)/shard_map/ppermute | solution.py:764
  312.1 63.1 %collective-permute-start.4 = (bf16[128,1536]{1,0:T(8,128)(2,1)}, bf16[128,1536]{1,0:T(8,128)(2,1)}, u32[]{:S(2)}, u32[]{:S(2)}) collective-permute-start(bf16[128,1536]{1,0:T(8,128)(2,1)} %get-tuple-element.57), channel_id=1, source_target_pairs={{0,4},{1,5},{2,6},{3,7},{4,0},{5,1},{6,2},{7,3},{8,12},{9,13},{10,... | collective-permute-start | bytes 1179656 | tf_op jit(solution)/shard_map/ppermute | solution.py:764
  366.3 27.1 %collective-permute-start.24 = (bf16[128,2688]{1,0:T(8,128)(2,1)}, bf16[128,2688]{1,0:T(8,128)(2,1)S(1)}, u32[]{:S(2)}, u32[]{:S(2)}) collective-permute-start(bf16[128,2688]{1,0:T(8,128)(2,1)} %get-tuple-element.41), channel_id=1, source_target_pairs={{0,4},{1,5},{2,6},{3,7},{4,0},{5,1},{6,2},{7,3},{8,12},{9,13},{10,... | collective-permute-start | bytes 2064392 | tf_op jit(solution)/shard_map/ppermute | solution.py:764
  369.8 24.9 %collective-permute-start.3 = (bf16[128,1536]{1,0:T(8,128)(2,1)}, bf16[128,1536]{1,0:T(8,128)(2,1)S(1)}, u32[]{:S(2)}, u32[]{:S(2)}) collective-permute-start(bf16[128,1536]{1,0:T(8,128)(2,1)} %get-tuple-element.56), channel_id=1, source_target_pairs={{0,2},{1,3},{2,0},{3,1},{4,6},{5,7},{6,4},{7,5},{8,10},{9,11},{10,... | collective-permute-start | bytes 1179656 | tf_op jit(solution)/shard_map/ppermute | solution.py:764
  373.3 46.7 %collective-permute-start.23 = (bf16[128,2688]{1,0:T(8,128)(2,1)}, bf16[128,2688]{1,0:T(8,128)(2,1)S(1)}, u32[]{:S(2)}, u32[]{:S(2)}) collective-permute-start(bf16[128,2688]{1,0:T(8,128)(2,1)} %get-tuple-element.40), channel_id=1, source_target_pairs={{0,2},{1,3},{2,0},{3,1},{4,6},{5,7},{6,4},{7,5},{8,10},{9,11},{10,... | collective-permute-start | bytes 2064392 | tf_op jit(solution)/shard_map/ppermute | solution.py:764
  375.2 30.4 %collective-permute-start.5 = (bf16[128,1536]{1,0:T(8,128)(2,1)}, bf16[128,1536]{1,0:T(8,128)(2,1)S(1)}, u32[]{:S(2)}, u32[]{:S(2)}) collective-permute-start(bf16[128,1536]{1,0:T(8,128)(2,1)} %collective-permute-done.4), channel_id=1, source_target_pairs={{0,2},{1,3},{2,0},{3,1},{4,6},{5,7},{6,4},{7,5},{8,10},{9,11},{10,... | collective-permute-start | bytes 1179656 | tf_op jit(solution)/shard_map/ppermute | solution.py:764
  393.4 24.8 %collective-permute-start.45 = (bf16[656,512]{1,0:T(8,128)(2,1)S(1)}, bf16[656,512]{1,0:T(8,128)(2,1)S(1)}, u32[]{:S(2)}, u32[]{:S(2)}) collective-permute-start(bf16[656,512]{1,0:T(8,128)(2,1)S(1)} %broadcast_select_fusion.7), channel_id=1, source_target_pairs={{0,1},{1,0},{2,3},{3,2},{4,5},{5,4},{6,7},{7,6},{8,9},{9,8},{10,11... | collective-permute-start | bytes 2015240 | tf_op jit(solution)/shard_map/ppermute | solution.py:764
  393.5 26.5 %collective-permute-start.25 = (bf16[128,2688]{1,0:T(8,128)(2,1)S(1)}, bf16[128,2688]{1,0:T(8,128)(2,1)S(1)}, u32[]{:S(2)}, u32[]{:S(2)}) collective-permute-start(bf16[128,2688]{1,0:T(8,128)(2,1)S(1)} %collective-permute-done.24), channel_id=1, source_target_pairs={{0,2},{1,3},{2,0},{3,1},{4,6},{5,7},{6,4},{7,5},{8,10},{9,11},{10,... | collective-permute-start | bytes 2064392 | tf_op jit(solution)/shard_map/ppermute | solution.py:764
  416.0 34.3 %collective-permute-start.22 = (bf16[256,512]{1,0:T(8,128)(2,1)S(1)}, bf16[256,512]{1,0:T(8,128)(2,1)S(1)}, u32[]{:S(2)}, u32[]{:S(2)}) collective-permute-start(bf16[256,512]{1,0:T(8,128)(2,1)S(1)} %broadcast_select_fusion.21), channel_id=1, source_target_pairs={{0,4},{1,5},{2,6},{3,7},{4,0},{5,1},{6,2},{7,3},{8,12},{9,13},{10,... | collective-permute-start | bytes 786440 | tf_op jit(solution)/shard_map/ppermute | solution.py:764
  418.5 30.9 %collective-permute-start.46 = (bf16[656,512]{1,0:T(8,128)(2,1)S(1)}, bf16[656,512]{1,0:T(8,128)(2,1)S(1)}, u32[]{:S(2)}, u32[]{:S(2)}) collective-permute-start(bf16[656,512]{1,0:T(8,128)(2,1)S(1)} %add_convert_fusion.5), channel_id=1, source_target_pairs={{0,8},{1,9},{2,10},{3,11},{4,12},{5,13},{6,14},{7,15},{24,16},{25,... | collective-permute-start | bytes 2015240 | tf_op jit(solution)/shard_map/ppermute | solution.py:764
  423.8 24.0 %collective-permute-start.7 = (bf16[256,768]{1,0:T(8,128)(2,1)S(1)}, bf16[256,768]{1,0:T(8,128)(2,1)S(1)}, u32[]{:S(2)}, u32[]{:S(2)}) collective-permute-start(bf16[256,768]{1,0:T(8,128)(2,1)S(1)} %get-tuple-element.55), channel_id=1, source_target_pairs={{0,8},{1,9},{2,10},{3,11},{4,12},{5,13},{6,14},{7,15},{24,16},{25,... | collective-permute-start | bytes 1179656 | tf_op jit(solution)/shard_map/ppermute | solution.py:764
  425.3 55.9 %collective-permute-start.26 = (bf16[256,2688]{1,0:T(8,128)(2,1)S(1)}, bf16[256,2688]{1,0:T(8,128)(2,1)S(1)}, u32[]{:S(2)}, u32[]{:S(2)}) collective-permute-start(bf16[256,2688]{1,0:T(8,128)(2,1)S(1)} %broadcast_select_fusion), channel_id=1, source_target_pairs={{0,1},{1,0},{2,3},{3,2},{4,5},{5,4},{6,7},{7,6},{8,9},{9,8},{10,11... | collective-permute-start | bytes 4128776 | tf_op jit(solution)/shard_map/ppermute | solution.py:764
  453.0 28.1 %collective-permute-start.12 = (bf16[256,768]{1,0:T(8,128)(2,1)S(1)}, bf16[256,768]{1,0:T(8,128)(2,1)S(1)}, u32[]{:S(2)}, u32[]{:S(2)}) collective-permute-start(bf16[256,768]{1,0:T(8,128)(2,1)S(1)} %add_convert_fusion.12), channel_id=1, source_target_pairs={{8,0},{9,1},{10,2},{11,3},{12,4},{13,5},{14,6},{15,7},{16,24},{17,... | collective-permute-start | bytes 1179656 | tf_op jit(solution)/shard_map/ppermute | solution.py:764
  454.5 62.0 %collective-permute-start.48 = (bf16[656,512]{1,0:T(8,128)(2,1)S(1)}, bf16[656,512]{1,0:T(8,128)(2,1)S(1)}, u32[]{:S(2)}, u32[]{:S(2)}) collective-permute-start(bf16[656,512]{1,0:T(8,128)(2,1)S(1)} %add_convert_fusion.3), channel_id=1, source_target_pairs={{8,0},{9,1},{10,2},{11,3},{12,4},{13,5},{14,6},{15,7},{16,24},{17,... | collective-permute-start | bytes 2015240 | tf_op jit(solution)/shard_map/ppermute | solution.py:764
  489.8 22.2 %collective-permute-start.33 = (bf16[256,896]{1,0:T(8,128)(2,1)S(1)}, bf16[256,896]{1,0:T(8,128)(2,1)S(1)}, u32[]{:S(2)}, u32[]{:S(2)}) collective-permute-start(bf16[256,896]{1,0:T(8,128)(2,1)S(1)} %get-tuple-element.36), channel_id=1, source_target_pairs={{0,8},{1,9},{2,10},{3,11},{4,12},{5,13},{6,14},{7,15},{24,16},{25,... | collective-permute-start | bytes 1376264 | tf_op jit(solution)/shard_map/ppermute | solution.py:764
  516.5 37.2 %collective-permute-start.49 = (bf16[656,512]{1,0:T(8,128)(2,1)S(1)}, bf16[656,512]{1,0:T(8,128)(2,1)S(1)}, u32[]{:S(2)}, u32[]{:S(2)}) collective-permute-start(bf16[656,512]{1,0:T(8,128)(2,1)S(1)} %broadcast_select_fusion.8), channel_id=1, source_target_pairs={{0,4},{1,5},{2,6},{3,7},{4,0},{5,1},{6,2},{7,3},{8,12},{9,13},{10,... | collective-permute-start | bytes 2015240 | tf_op jit(solution)/shard_map/ppermute | solution.py:764
  519.0 28.8 %collective-permute-start.32 = (bf16[256,896]{1,0:T(8,128)(2,1)S(1)}, bf16[256,896]{1,0:T(8,128)(2,1)S(1)}, u32[]{:S(2)}, u32[]{:S(2)}) collective-permute-start(bf16[256,896]{1,0:T(8,128)(2,1)S(1)} %add_convert_fusion.8), channel_id=1, source_target_pairs={{8,0},{9,1},{10,2},{11,3},{12,4},{13,5},{14,6},{15,7},{16,24},{17,... | collective-permute-start | bytes 1376264 | tf_op jit(solution)/shard_map/ppermute | solution.py:764
  520.4 32.3 %collective-permute-start.35 = (bf16[256,896]{1,0:T(8,128)(2,1)S(1)}, bf16[256,896]{1,0:T(8,128)(2,1)S(1)}, u32[]{:S(2)}, u32[]{:S(2)}) collective-permute-start(bf16[256,896]{1,0:T(8,128)(2,1)S(1)} %add_convert_fusion.6), channel_id=1, source_target_pairs={{8,0},{9,1},{10,2},{11,3},{12,4},{13,5},{14,6},{15,7},{16,24},{17,... | collective-permute-start | bytes 1376264 | tf_op jit(solution)/shard_map/ppermute | solution.py:764
  (67 other events, 544.7 us)
Sparse Core Ops, SparseCore 0:
  9.6 34.5 all-gather.3
  45.7 80.4 all-gather.5
  127.8 52.4 all-gather.7

commit v2 on v0

--- a/solution.py
+++ b/solution.py
@@ -271,202 +271,6 @@
     )(block).reshape(4 * rows, width)
 
 
-TILE = 16
-SLICE = 1536
-
-
-def total_kernel(pair, lone, x_ref, o_ref, y_got, z_got, z_sent, e_got, send_sem, recv_sem):
-    ctx, place = lax.axis_index("ctx"), lax.axis_index("fsdp")
-    y = lax.rem(ctx, 2)
-    z = ctx // 2
-    firsts, lasts = 2 * pair, 2 * lone
-    every = firsts + lasts
-
-    def send(src, dst, sem, to_ctx):
-        return pltpu.make_async_remote_copy(
-            src_ref=src,
-            dst_ref=dst,
-            send_sem=send_sem.at[sem],
-            recv_sem=recv_sem.at[sem],
-            device_id=(to_ctx, place),
-            device_id_type=MESH_ID,
-        )
-
-    y_side = ctx + 1 - 2 * y
-
-    def rows(item, side):
-        if item < firsts:
-            return pl.ds(pl.multiple_of((side * firsts + item) * TILE, TILE), TILE)
-        return pl.ds((firsts + item) * TILE, TILE)
-
-    def end_of(item):
-        return item // pair if item < firsts else (item - firsts) // lone
-
-    def turn_of(item):
-        return item % pair if item < firsts else (item - firsts) % lone
-
-    def add(store, store_rows, terms):
-        @pl.loop(0, x_ref.shape[1] // SLICE)
-        def _(i):
-            columns = pl.ds(pl.multiple_of(i * SLICE, SLICE), SLICE)
-            total = terms[0][0][terms[0][1], columns].astype(jnp.float32)
-            for ref, place_rows in terms[1:]:
-                total += ref[place_rows, columns].astype(jnp.float32)
-            store[store_rows, columns] = total.astype(jnp.bfloat16)
-
-    def slot(item):
-        return pl.ds(item * TILE, TILE)
-
-    def pair_copy(item):
-        return send(x_ref.at[rows(item, 1 - y), :], y_got.at[slot(item), :], item, y_side)
-
-    def up_copy(item, to_z):
-        return send(z_sent.at[slot(item), :], z_got.at[slot(item), :], firsts + item, 2 * to_z + y)
-
-    def end_copy(item):
-        return send(
-            z_sent.at[slot(item), :],
-            e_got.at[slot(item - firsts), :],
-            firsts + every + item - firsts,
-            y_side,
-        )
-
-    def down_copy(item, to_z):
-        here = rows(item, y)
-        return send(
-            o_ref.at[here, :], o_ref.at[here, :], firsts + every + lasts + item, 2 * to_z + y
-        )
-
-    def back_copy(item):
-        here = rows(item, y)
-        return send(
-            o_ref.at[here, :], o_ref.at[here, :], firsts + 2 * every + lasts + item, y_side
-        )
-
-    barrier = pltpu.get_barrier_semaphore()
-    pl.semaphore_signal(barrier, inc=1, device_id=(y_side, place), device_id_type=MESH_ID)
-
-    @pl.when(z > 0)
-    def _():
-        pl.semaphore_signal(barrier, inc=1, device_id=(ctx - 2, place), device_id_type=MESH_ID)
-
-    @pl.when(z < 3)
-    def _():
-        pl.semaphore_signal(barrier, inc=1, device_id=(ctx + 2, place), device_id_type=MESH_ID)
-
-    @pl.when((z == 0) | (z == 3))
-    def _():
-        pl.semaphore_wait(barrier, 2)
-
-    @pl.when((z > 0) & (z < 3))
-    def _():
-        pl.semaphore_wait(barrier, 3)
-
-    for turn in range(pair):
-        for end in range(2):
-            pair_copy(end * pair + turn).start()
-
-    def steps(my_z):
-        depth = lambda item: 3 - my_z if end_of(item) == 0 else my_z
-        toward = lambda item: my_z - 1 if end_of(item) == 0 else my_z + 1
-        away = lambda item: my_z + 1 if end_of(item) == 0 else my_z - 1
-        events = []
-        for item in range(every):
-            wait = 1 if item < firsts else 0
-            late = 0 if item < firsts else 1
-            at = 2 * turn_of(item) + depth(item) + wait
-            events.append((at, item, "up"))
-            if depth(item) == 3 and late:
-                events.append((at + 1, item, "meet"))
-            if depth(item) < 3:
-                events.append(
-                    (2 * turn_of(item) + 3 + wait + late + 3 - depth(item), item, "down")
-                )
-        pending = []
-
-        def start(copy):
-            copy.start()
-            pending.append(copy)
-
-        def finish(item):
-            if depth(item) > 0:
-                start(down_copy(item, away(item)))
-            if item < firsts:
-                start(back_copy(item))
-
-        for _, item, kind in sorted(events):
-            if kind == "up":
-                terms = [(x_ref, rows(item, y))]
-                if item < firsts:
-                    pair_copy(item).wait_recv()
-                    terms.append((y_got, slot(item)))
-                if depth(item) > 0:
-                    up_copy(item, away(item)).wait_recv()
-                    terms.append((z_got, slot(item)))
-                if depth(item) == 3 and item < firsts:
-                    add(o_ref, rows(item, y), terms)
-                    finish(item)
-                else:
-                    add(z_sent, slot(item), terms)
-                    if depth(item) == 3:
-                        start(end_copy(item))
-                    else:
-                        start(up_copy(item, toward(item)))
-            elif kind == "meet":
-                end_copy(item).wait_recv()
-                add(
-                    o_ref,
-                    rows(item, y),
-                    [(z_sent, slot(item)), (e_got, slot(item - firsts))],
-                )
-                finish(item)
-            else:
-                down_copy(item, toward(item)).wait_recv()
-                finish(item)
-        for copy in pending:
-            copy.wait_send()
-
-    for my_z in range(4):
-        pl.when(z == my_z)(functools.partial(steps, my_z))
-
-    for item in range(firsts):
-        pair_copy(item).wait_send()
-        send(
-            o_ref.at[rows(item, y), :],
-            o_ref.at[rows(item, 1 - y), :],
-            firsts + 2 * every + lasts + item,
-            y_side,
-        ).wait_recv()
-
-
-def total_over_ctx(grads, collective_id):
-    rows, width = grads.shape
-    chunks = rows // TILE
-    pair, lone = chunks // 8, chunks // 4
-    items = 2 * pair + 2 * lone
-    sems = 4 * pair + 2 * items + 2 * lone
-    low = lambda count: pltpu.VMEM((count * TILE, width), jnp.bfloat16)
-    return pl.pallas_call(
-        functools.partial(total_kernel, pair, lone),
-        out_shape=jax.ShapeDtypeStruct((rows, width), jnp.bfloat16),
-        in_specs=[pl.BlockSpec(memory_space=pltpu.VMEM)],
-        out_specs=pl.BlockSpec(memory_space=pltpu.VMEM),
-        scratch_shapes=[
-            low(2 * pair),
-            low(items),
-            low(items),
-            low(2 * lone),
-            pltpu.SemaphoreType.DMA((sems,)),
-            pltpu.SemaphoreType.DMA((sems,)),
-        ],
-        compiler_params=pltpu.CompilerParams(
-            collective_id=collective_id,
-            has_side_effects=True,
-            vmem_limit_bytes=48 * 1024 * 1024,
-        ),
-    )(grads)
-
-
 def pack(blocks):
     half = blocks.shape[-2] // 2
     return jnp.concatenate([blocks[..., :half, :], blocks[..., half:, :]], axis=-1)
@@ -623,7 +427,8 @@
         ],
         axis=1,
     )
-    sent, after = lax.optimization_barrier((sent, after))
+    if after:
+        sent, after = lax.optimization_barrier((sent, after))
     got = exchange(sent, ctx_count, fsdp_count, 4)
     parts = jnp.stack(
         [got[:, :row_count, :head_size], got[:, :row_count, head_size:], unpack(got[:, row_count:])]
@@ -735,6 +540,279 @@
     return jnp.einsum("tw,tf->wf", left, right, preferred_element_type=jnp.float32)
 
 
+def mesh_place():
+    ctx, place = lax.axis_index("ctx"), lax.axis_index("fsdp")
+    return ctx // 2, lax.rem(ctx, 2), place // 2, lax.rem(place, 2)
+
+
+def device_at(z, y, x, core):
+    return (2 * z + y, 2 * x + core)
+
+
+def greet(barrier, devices):
+    for device in devices:
+        pl.semaphore_signal(barrier, inc=1, device_id=device, device_id_type=MESH_ID)
+    pl.semaphore_wait(barrier, len(devices))
+
+
+def spans(total, count):
+    edges = [total * i // (count * 16) * 16 for i in range(count)] + [total]
+    return list(zip(edges[:-1], edges[1:]))
+
+
+def plane_kernel(kinds, cuts, *refs):
+    count = len(kinds)
+    ins, outs = refs[:count], refs[count : 2 * count]
+    send_sem, recv_sem, own_sem = refs[2 * count :]
+    z, y, x, core = mesh_place()
+    to_x, to_y = device_at(z, y, 1 - x, core), device_at(z, 1 - y, x, core)
+    greet(pltpu.get_barrier_semaphore(), (to_x, to_y))
+    serial = iter(range(send_sem.shape[0]))
+
+    def send(src, dst, device):
+        sem = next(serial)
+        copy = pltpu.make_async_remote_copy(
+            src_ref=src,
+            dst_ref=dst,
+            send_sem=send_sem.at[sem],
+            recv_sem=recv_sem.at[sem],
+            device_id=device,
+            device_id_type=MESH_ID,
+        )
+        copy.start()
+        return copy
+
+    def block(ref, out, index):
+        width = out.shape[2]
+        if len(ref.shape) == 3:
+            return ref.at[index]
+        step = ref.shape[1] - width
+        return ref.at[:, pl.ds(pl.multiple_of(index * step, 128), width)]
+
+    owns = []
+    for i in range(count):
+        own = block(ins[i], outs[i], y if kinds[i] else x)
+        copy = pltpu.make_async_copy(own, outs[i].at[0], own_sem.at[i])
+        copy.start()
+        owns.append(copy)
+    firsts, seconds = [], []
+    for i in range(count):
+        own = block(ins[i], outs[i], y if kinds[i] else x)
+        away = block(ins[i], outs[i], 1 - y if kinds[i] else 1 - x)
+        for low, high in spans(outs[i].shape[1], cuts[i]):
+            rows = pl.ds(low, high - low)
+            by_x = send((own if kinds[i] else away).at[rows], outs[i].at[1, rows], to_x)
+            by_y = send((away if kinds[i] else own).at[rows], outs[i].at[2, rows], to_y)
+            firsts.append((i, rows, by_x, by_y))
+    for i, rows, by_x, by_y in firsts:
+        if kinds[i]:
+            by_y.wait_recv()
+            seconds.append(send(outs[i].at[2, rows], outs[i].at[3, rows], to_x))
+        else:
+            by_x.wait_recv()
+            seconds.append(send(outs[i].at[1, rows], outs[i].at[3, rows], to_y))
+    for i, rows, by_x, by_y in firsts:
+        (by_x if kinds[i] else by_y).wait_recv()
+        by_x.wait_send()
+        by_y.wait_send()
+    for copy in seconds:
+        copy.wait()
+    for copy in owns:
+        copy.wait()
+
+
+def plane(parts, kinds, widths, cuts, collective_id):
+    rows = parts[0].shape[-2]
+    sems = 3 * sum(cuts)
+    outs = pl.pallas_call(
+        functools.partial(plane_kernel, kinds, cuts),
+        out_shape=[jax.ShapeDtypeStruct((4, rows, width), jnp.bfloat16) for width in widths],
+        in_specs=[pl.BlockSpec(memory_space=pl.ANY)] * len(parts),
+        out_specs=[pl.BlockSpec(memory_space=pl.ANY)] * len(parts),
+        scratch_shapes=[
+            pltpu.SemaphoreType.DMA((sems,)),
+            pltpu.SemaphoreType.DMA((sems,)),
+            pltpu.SemaphoreType.DMA((len(parts),)),
+        ],
+        compiler_params=pltpu.CompilerParams(collective_id=collective_id, has_side_effects=True),
+    )(*parts)
+    return [out.reshape(4 * rows, width) for out, width in zip(outs, widths)]
+
+
+def finish_kernel(chunks, count, *refs):
+    parts, gains = refs[:count], refs[count]
+    outs, gain_got = refs[count + 1 : 2 * count + 1], refs[2 * count + 1]
+    scratch = refs[2 * count + 2 :]
+    core_got, z_got, mid_got, z_sent = (scratch[i * count : (i + 1) * count] for i in range(4))
+    send_sem, recv_sem, gain_send, gain_recv, own_sem = scratch[4 * count :]
+    z, y, x, core = mesh_place()
+    me = lax.axis_index("ctx") * 4 + lax.axis_index("fsdp")
+    total = len(chunks)
+    barrier = pltpu.get_barrier_semaphore()
+
+    def other(step):
+        place = lax.rem(me + step, 32)
+        return place, (place // 4, lax.rem(place, 4))
+
+    @pl.loop(1, 32)
+    def _(step):
+        pl.semaphore_signal(barrier, inc=1, device_id=other(step)[1], device_id_type=MESH_ID)
+
+    pl.semaphore_wait(barrier, 31)
+
+    def send(stage, k, src, dst, device):
+        return pltpu.make_async_remote_copy(
+            src_ref=src,
+            dst_ref=dst,
+            send_sem=send_sem.at[stage * total + k],
+            recv_sem=recv_sem.at[stage * total + k],
+            device_id=device,
+            device_id_type=MESH_ID,
+        )
+
+    def at(k):
+        i, low, high = chunks[k]
+        return i, pl.ds(low, high - low)
+
+    def core_copy(k):
+        i, rows = at(k)
+        return send(
+            0, k, parts[i].at[1 - core, rows], core_got[i].at[rows], device_at(z, y, x, 1 - core)
+        )
+
+    def inward(k):
+        i, rows = at(k)
+        return send(
+            1, k, z_sent[i].at[rows], z_got[i].at[rows], device_at(1 + z // 2, y, x, core)
+        )
+
+    def middle(k):
+        i, rows = at(k)
+        return send(2, k, z_sent[i].at[rows], mid_got[i].at[rows], device_at(3 - z, y, x, core))
+
+    def outward(k):
+        i, rows = at(k)
+        here = outs[i].at[y, rows]
+        return send(3, k, here, here, device_at(3 * (z // 2), y, x, core))
+
+    def across(k):
+        i, rows = at(k)
+        here = outs[i].at[y, rows]
+        return send(4, k, here, here, device_at(z, 1 - y, x, core))
+
+    def gain_copy(step):
+        place, device = other(step)
+        return pltpu.make_async_remote_copy(
+            src_ref=gains.at[lax.rem(place, 4)],
+            dst_ref=gain_got.at[me],
+            send_sem=gain_send.at[step],
+            recv_sem=gain_recv.at[step],
+            device_id=device,
+            device_id_type=MESH_ID,
+        )
+
+    def wide(value):
+        return value.astype(jnp.float32)
+
+    for k in range(total):
+        core_copy(k).start()
+    own = pltpu.make_async_copy(gains.at[lax.rem(me, 4)], gain_got.at[me], own_sem)
+    own.start()
+
+    @pl.loop(1, 32)
+    def _(step):
+        gain_copy(step).start()
+
+    @pl.when((z == 0) | (z == 3))
+    def _():
+        for k in range(total):
+            i, rows = at(k)
+            core_copy(k).wait_recv()
+            value = wide(parts[i][core, rows]) + wide(core_got[i][rows])
+            z_sent[i][rows] = value.astype(jnp.bfloat16)
+            inward(k).start()
+        for k in range(total):
+            outward(k).wait_recv()
+            across(k).start()
+        for k in range(total):
+            inward(k).wait_send()
+
+    @pl.when((z == 1) | (z == 2))
+    def _():
+        def meet(k):
+            i, rows = at(k)
+            middle(k).wait_recv()
+            value = wide(z_sent[i][rows]) + wide(mid_got[i][rows])
+            outs[i][y, rows] = value.astype(jnp.bfloat16)
+            outward(k).start()
+            across(k).start()
+
+        for k in range(total):
+            i, rows = at(k)
+            core_copy(k).wait_recv()
+            inward(k).wait_recv()
+            value = wide(parts[i][core, rows]) + wide(core_got[i][rows]) + wide(z_got[i][rows])
+            z_sent[i][rows] = value.astype(jnp.bfloat16)
+            middle(k).start()
+            if k > 0:
+                meet(k - 1)
+        meet(total - 1)
+        for k in range(total):
+            middle(k).wait_send()
+            outward(k).wait_send()
+
+    for k in range(total):
+        i, rows = at(k)
+        there = outs[i].at[1 - y, rows]
+        send(4, k, there, there, device_at(z, 1 - y, x, core)).wait_recv()
+        across(k).wait_send()
+        core_copy(k).wait_send()
+    own.wait()
+
+    @pl.loop(1, 32)
+    def _(step):
+        gain_copy(step).wait()
+
+
+def finish(parts, gains, cuts, collective_id):
+    chunks = [
+        (i, low, high) for i, cut in enumerate(cuts) for low, high in spans(parts[i].shape[1], cut)
+    ]
+    shapes = [part.shape for part in parts]
+    buffers = [pltpu.VMEM(shape[1:], jnp.bfloat16) for shape in shapes]
+    in_vmem = pl.BlockSpec(memory_space=pltpu.VMEM)
+    return pl.pallas_call(
+        functools.partial(finish_kernel, chunks, len(parts)),
+        out_shape=[jax.ShapeDtypeStruct(shape, jnp.bfloat16) for shape in shapes]
+        + [jax.ShapeDtypeStruct((32, 8, gains.shape[2]), jnp.float32)],
+        in_specs=[in_vmem] * (len(parts) + 1),
+        out_specs=[in_vmem] * (len(parts) + 1),
+        scratch_shapes=buffers * 4
+        + [
+            pltpu.SemaphoreType.DMA((5 * len(chunks),)),
+            pltpu.SemaphoreType.DMA((5 * len(chunks),)),
+            pltpu.SemaphoreType.DMA((32,)),
+            pltpu.SemaphoreType.DMA((32,)),
+            pltpu.SemaphoreType.DMA,
+        ],
+        compiler_params=pltpu.CompilerParams(
+            collective_id=collective_id,
+            has_side_effects=True,
+            vmem_limit_bytes=48 * 1024 * 1024,
+        ),
+    )(*parts, gains)
+
+
+def core_blocks(left, right):
+    both = weight_grad(left, right).astype(jnp.bfloat16)
+    return both.reshape(2, both.shape[0] // 2, both.shape[1])
+
+
+def joined_halves(out, full):
+    skip = 2 * out.shape[2] - full
+    return jnp.concatenate([out[0], out[1][:, skip:]], axis=1).astype(jnp.float32)
+
+
 def on_device(inputs, attn_gain, attn_proj, attn_out, mlp_gain, mlp_in, mlp_out, cotangent):
     seq_count, row_count, model_width = inputs.shape
     head_size = HEAD_DIM
@@ -801,51 +879,59 @@
         .astype(jnp.bfloat16)
         .reshape(seq_count, row_count, head_count, head_size)
     )
-    normed_two_part, gate_part, context_part, normed_part = group_columns(
-        (normed_two_low, gate_low, context_low, normed_low)
-    )
-    seed_group = group_rows(seed_rows)
-    joined = group_rows(jnp.concatenate([lifted_grad, middle_low], axis=1))
-    lift_grad = weight_grad(normed_two_part, joined[:, : lifted_grad.shape[1]])
-    out_grad = weight_grad(context_part, joined[:, lifted_grad.shape[1] :])
-    down_grad = weight_grad(gate_part, seed_group)
-    first_grads = tuple(grad.astype(jnp.bfloat16) for grad in (lift_grad, down_grad, out_grad))
-    mixed_grad, first_grads = attention_back(context_grad, saved, scaling, first_grads)
+    if small:
+        width, lifted_width = model_width // 2, lifted_grad.shape[1]
+        hidden = gate_low.shape[1] // 2
+        lift_half = -(-lifted_width // 256) * 128
+        gate_halves = jnp.stack([gate_low[:, :hidden], gate_low[:, hidden:]])
+        normed_two_left, context_left, normed_left, gate_left, seed_right, middle_right, lift_right = (
+            plane(
+                (normed_two_low, context_low, normed_low, gate_halves, seed_rows, middle_low, lifted_grad),
+                (0, 0, 0, 0, 1, 1, 1),
+                (width, width, width, hidden, width, width, lift_half),
+                (1, 1, 1, 2, 1, 1, 4),
+                5,
+            )
+        )
+        mixed_grad, _ = attention_back(context_grad, saved, scaling, ())
+        (mixed_right,) = plane((mixed_grad,), (1,), (mixed_grad.shape[1] // 2,), (4,), 7)
+        lift_part = core_blocks(normed_two_left, lift_right)
+        down_part = core_blocks(gate_left, seed_right)
+        out_part = core_blocks(context_left, middle_right)
+        proj_part = core_blocks(normed_left, mixed_right)
+    else:
+        normed_two_part, gate_part, context_part, normed_part = group_columns(
+            (normed_two_low, gate_low, context_low, normed_low)
+        )
+        seed_group = group_rows(seed_rows)
+        joined = group_rows(jnp.concatenate([lifted_grad, middle_low], axis=1))
+        lift_grad = weight_grad(normed_two_part, joined[:, : lifted_grad.shape[1]])
+        out_grad = weight_grad(context_part, joined[:, lifted_grad.shape[1] :])
+        down_grad = weight_grad(gate_part, seed_group)
+        first_grads = tuple(grad.astype(jnp.bfloat16) for grad in (lift_grad, down_grad, out_grad))
+        mixed_grad, first_grads = attention_back(context_grad, saved, scaling, first_grads)
+        mixed_group = group_rows(mixed_grad)
+        proj_grad = weight_grad(normed_part, mixed_group).astype(jnp.bfloat16)
+        lift_sum, down_sum, out_sum, proj_sum = (
+            total.astype(jnp.float32) for total in lax.psum((*first_grads, proj_grad), "ctx")
+        )
     normed_grad = jnp.einsum(
         "tm,wm->tw", mixed_grad, proj_full, preferred_element_type=jnp.float32
     ).reshape(seq_count, row_count, model_width)
     state_part, gain_one_grad = norm_back_one(normed_grad)
     input_grad = middle_grad + state_part
-    mixed_group = gather(mixed_grad, False, 4, 7) if small else group_rows(mixed_grad)
-    proj_grad = weight_grad(normed_part, mixed_group).astype(jnp.bfloat16)
-    grads = (*first_grads, proj_grad)
-    if small:
-        sheet = [grad.reshape(own_rows, -1) for grad in grads]
-        widths = [grad.shape[1] for grad in sheet]
-        spare = -sum(widths) % SLICE
-        sheet = jnp.concatenate(
-            [sheet[0], sheet[2], sheet[3], sheet[1], jnp.zeros((own_rows, spare), jnp.bfloat16)],
-            axis=1,
-        )
-        sums = total_over_ctx(sheet, 8)
-        edges = [0, widths[0], widths[0] + widths[2], widths[0] + widths[2] + widths[3]]
-        lift_sum, out_sum, proj_sum, down_sum = (
-            sums[:, edges[0] : edges[1]],
-            sums[:, edges[1] : edges[2]],
-            sums[:, edges[2] : edges[3]],
-            sums[:, edges[3] : edges[3] + widths[1]].reshape(mlp_out.shape),
-        )
-    else:
-        lift_sum, down_sum, out_sum, proj_sum = lax.psum(grads, "ctx")
-    lift_sum, down_sum, out_sum, proj_sum = (
-        total.astype(jnp.float32) for total in (lift_sum, down_sum, out_sum, proj_sum)
-    )
     gain_grads = jnp.stack([gain_one_grad, gain_two_grad])
     if small:
         shares = gain_grads.reshape(2, fsdp_count, gain_width).transpose(1, 0, 2)
         shares = jnp.concatenate([shares, jnp.zeros((fsdp_count, 6, gain_width))], axis=1)
-        shares = jnp.concatenate([shares] * ctx_count, axis=0)
-        gain_own = jnp.sum(exchange(shares, ctx_count, fsdp_count, 5), axis=0)
+        lift_sum, down_sum, out_sum, proj_sum, gain_got = finish(
+            (lift_part, down_part, out_part, proj_part), shares, (8, 4, 2, 4), 8
+        )
+        lift_sum = joined_halves(lift_sum, lifted_width)
+        down_sum = joined_halves(down_sum, model_width)
+        out_sum = joined_halves(out_sum, model_width)
+        proj_sum = joined_halves(proj_sum, mixed_grad.shape[1])
+        gain_own = jnp.sum(gain_got, axis=0)
     else:
         gain_sums = lax.psum(gain_grads, ("ctx", "fsdp"))
         gain_own = lax.dynamic_slice_in_dim(gain_sums, fsdp_place * gain_width, gain_width, axis=1)

time: 578 us -> 494 us (0.85)
  Pallas kernels: 353 us -> 322 us
  local copies, waits for them, and re-layouts: 70.5 us -> 44.6 us
  other arithmetic: 50.5 us -> 40.3 us
  matrix products: 50.9 us -> 43.8 us
    pallas_call x5 -> x4, Pallas kernels: 94.6 us -> 65.2 us  [exchange(): pl.pallas_call(functools.partial(exchange_kernel, ctx_count, fsdp_count),...]
    pallas_call x2 -> x1, Pallas kernels: 77.7 us -> 52 us  [gather(): pl.pallas_call(functools.partial(gather_kernel, spread, chunks), out_shap...]
    pallas_call x1 -> x3, Pallas kernels: 158 us -> 183 us  [the longest x1 101 us: finish(): pl.pallas_call(functools.partial(finish_kernel, chunks, len(parts)), out_...]
    concatenate x6 -> x1, local copies, waits for them, and re-layouts: 18.3 us -> 0.01 us  [on_device(): jnp.concatenate([shares, jnp.zeros((fsdp_count, 6, gain_width))], axis=1)]
    dot_general x4, matrix products: 14.7 us -> 7.88 us  [weight_grad(): jnp.einsum('tw,tf->wf', left, right, preferred_element_type=jnp.float32)]
  transfers between devices with their start and end apart: 6 -> 3, of which waited for: 1 -> 1; matrix products, arithmetic and copies ran while one was open for 18% -> 9% of each run, Pallas kernels for 25% -> 19%
where the time goes in v2:
time: 494 us; the launch traced here: 488 us
  Pallas kernels  322 us (65%)
  local copies, waits for them, and re-layouts  44.6 us (9%)
  matrix products  43.8 us (9%)
  other arithmetic  40.3 us (8%)
  waiting for transfers between devices  17.3 us (4%)
  between operations  14.9 us (3%)
  blocking collectives  5.07 us (1%)
    pallas_call x1, Pallas kernels, finish(): pl.pallas_call(functools.partial(finish_kernel, chunks, len(parts)), out_...  101 us
    pallas_call x2, Pallas kernels, plane(): pl.pallas_call(functools.partial(plane_kernel, kinds, cuts), out_shape=[j...  82 us
    pallas_call x4, Pallas kernels, exchange(): pl.pallas_call(functools.partial(exchange_kernel, ctx_count, fsdp_count),...  65.2 us
    pallas_call x1, Pallas kernels, gather(): pl.pallas_call(functools.partial(gather_kernel, spread, chunks), out_shap...  52 us
    all_gather x1, waiting for transfers between devices, on_device(): lax.all_gather(mlp_out, 'fsdp', axis=0, tiled=True)  15.2 us
    pallas_call x1, Pallas kernels, attend_back(): pl.pallas_call(attend_back_kernel, grid=(rows // block,), out_shape=(jax....  14.1 us
  transfers between devices with their start and end apart: 3, of which 1 were waited for; matrix products, arithmetic and copies ran while one was open for 9% of the time, Pallas kernels for 19%

profile of v2, /device:TPU:0, one launch (start us, length us, event | category | flops | bytes accessed | tf_op | source)
XLA Modules:
  0.0 488.4 jit_solution(7656259629622597589)
XLA Ops:
  9.5 52.0 %shard_map.143 = bf16[4,256,3072]{2,1,0:T(8,128)(2,1)} custom-call(bf16[256,3072]{1,0:T(8,128)(2,1)} %x_ref.1), custom_call_target="tpu_custom_call" | custom-call | tf_op jit(solution)/shard_map/pallas_call | solution.py:260
  61.5 8.7 %copy.32 = bf16[1024,3072]{0,1:T(8,128)(2,1)} copy(bf16[1024,3072]{1,0:T(8,128)(2,1)} %bitcast.154) | data formatting | bytes 12582912 | tf_op jit(solution)/shard_map/reshape | solution.py:271
  70.2 5.1 %all_gather.12 = bf16[2,1024]{1,0:T(2,128)(2,1)S(1)} all-gather(bf16[2,256]{1,0:T(2,128)(2,1)S(1)} %pad_maximum_fusion.9), channel_id=1, replica_groups=mesh['ctx'=8,'fsdp'=4] {'fsdp'}, dimensions={1}, use_global_device_ids=true | all-gather | bytes 5120 | tf_op jit(solution)/shard_map/all_gather | solution.py:829
  76.1 4.5 fusion.40
  93.0 18.6 %shard_map.144 = bf16[32,96,128]{2,1,0:T(8,128)(2,1)} custom-call(bf16[32,96,128]{2,1,0:T(8,128)(2,1)} %maximum_maximum_fusion.x_ref), custom_call_target="tpu_custom_call" | custom-call | tf_op jit(solution)/shard_map/pallas_call | solution.py:171
  113.2 8.5 %shard_map.145 = (f32[2048,64]{1,0:T(8,128)S(1)}, f32[2048,1]{1,0:T(8,128)S(1)}) custom-call(bf16[2048,64]{1,0:T(8,128)(2,1)S(1)} %bitcast.149, bf16[2048,64]{1,0:T(8,128)(2,1)S(1)} %bitcast.147, bf16[2048,64]{1,0:T(8,128)(2,1)S(1)} %bitcast.145), custom_call_target="tpu_custom_call" | custom-call | tf_op jit(solution)/shard_map/pallas_call | solution.py:304
  123.7 15.7 %shard_map.146 = bf16[32,32,128]{2,1,0:T(8,128)(2,1)} custom-call(bf16[32,32,128]{2,1,0:T(8,128)(2,1)} %pad_maximum_fusion.6.x_ref), custom_call_target="tpu_custom_call" | custom-call | tf_op jit(solution)/shard_map/pallas_call | solution.py:171
  146.9 7.3 %fusion.63 = f32[128,5248]{1,0:T(8,128)} fusion(bf16[128,1024]{1,0:T(8,128)(2,1)} %bitcast.161, bf16[1024,5248]{1,0:T(8,128)(2,1)} %all-gather.6.cloned.1.call-done), kind=kOutput, calls=%fused_computation.143 | convolution fusion | flops 1375731712 | bytes 13697024 | tf_op jit(solution)/shard_map/dot_general | solution.py:859
  154.2 15.2 %all-gather.8.cloned.1.call-done = bf16[2624,1024]{1,0:T(8,128)(2,1)} async-done(((bf16[656,1024]{1,0:T(8,128)(2,1)}), bf16[2624,1024]{1,0:T(8,128)(2,1)}) %all-gather.8.cloned.1.call-update) | async-done | bytes 5373968 | tf_op jit(solution)/shard_map/all_gather | solution.py:841
  169.4 7.1 %fusion.38 = (f32[128,2624]{1,0:T(8,128)S(1)}, f32[128,2624]{1,0:T(8,128)S(1)}, f32[128,2624]{1,0:T(8,128)S(1)}) fusion(f32[128,5248]{1,0:T(8,128)} %fusion.63, bf16[128,1024]{1,0:T(8,128)(2,1)} %bitcast.165, bf16[2624,1024]{1,0:T(8,128)(2,1)} %all-gather.8.cloned.1.call-done), kind=kOutput, calls=%fused_computation.98 | convolution fusion | flops 709697536 | bytes 11010048 | tf_op jit(solution)/shard_map/td,fd->tf/dot_general | solution.py:869
  180.8 3.6 fusion.65
  184.6 3.5 fusion.64
  197.6 10.9 %shard_map.147 = bf16[32,32,128]{2,1,0:T(8,128)(2,1)} custom-call(bf16[32,32,128]{2,1,0:T(8,128)(2,1)} %pad_maximum_fusion.7.x_ref), custom_call_target="tpu_custom_call" | custom-call | tf_op jit(solution)/shard_map/pallas_call | solution.py:171
  209.8 14.1 %shard_map.148 = (f32[2048,64]{1,0:T(8,128)S(1)}, f32[2048,64]{1,0:T(8,128)S(1)}, f32[2048,64]{1,0:T(8,128)S(1)}) custom-call(bf16[2048,64]{1,0:T(8,128)(2,1)S(1)} %bitcast.150, bf16[2048,64]{1,0:T(8,128)(2,1)S(1)} %bitcast.148, bf16[2048,64]{1,0:T(8,128)(2,1)S(1)} %bitcast.146, f32[2048,64]{1,0:T(8,128)} %copy-done, f32[2048,1]{1,0:T(8,128)} %copy-done.1, ...), custom_call_target="tpu_custom_call" | custom-call | tf_op jit(solution)/shard_map/pallas_call | solution.py:355
  223.9 3.8 multiply_multiply_fusion.5
  228.1 4.8 fusion.19
  233.3 4.0 fusion.20
  238.7 20.1 %shard_map.149 = bf16[32,96,128]{2,1,0:T(8,128)(2,1)} custom-call(bf16[32,96,128]{2,1,0:T(8,128)(2,1)} %maximum_maximum_fusion.1.x_ref), custom_call_target="tpu_custom_call" | custom-call | tf_op jit(solution)/shard_map/pallas_call | solution.py:171
  266.2 5.1 %fusion.33 = (f32[2,64]{1,0:T(2,128)S(1)}, f32[2,64,1024]{2,1,0:T(8,128)S(1)}) fusion(bf16[2,64,1024]{2,1,0:T(8,128)(2,1)S(1)} %copy-done.3, f32[1024]{0:T(1024)S(1)} %bitcast.183, f32[2,64]{1,0:T(2,128)S(1)} %broadcast_multiply_fusion.3, bf16[2,64,3072]{2,1,0:T(8,128)(2,1)S(1)} %dot_general.54, bf16[1024,3072,1]{1,0,2:T(8,128)(2,1)} %bitcast.155), kind=kOutput, calls=%fused_computation.77 | convolution fusion | flops 805961600 | bytes 7869440 | tf_op jit(solution)/shard_map/tm,wm->tw/dot_general | solution.py:918
  271.6 22.3 %shard_map.151 = bf16[4,128,1536]{2,1,0:T(8,128)(2,1)} custom-call(bf16[128,3072]{1,0:T(8,128)(2,1)} %reshape.276.refs_0_), custom_call_target="tpu_custom_call" | custom-call | tf_op jit(solution)/shard_map/pallas_call | solution.py:627
  294.9 59.7 %shard_map.150 = (bf16[4,128,512]{2,1,0:T(8,128)(2,1)}, bf16[4,128,512]{2,1,0:T(8,128)(2,1)}, bf16[4,128,512]{2,1,0:T(8,128)(2,1)}, bf16[4,128,1312]{2,1,0:T(8,1...) custom-call(bf16[128,1024]{1,0:T(8,128)(2,1)} %bitcast.162, ...), custom_call_target="tpu_custom_call" | custom-call | tf_op jit(solution)/shard_map/pallas_call | solution.py:627
  354.6 3.3 fusion.1
  361.2 3.2 bitcast_convert_fusion
  364.4 100.5 %shard_map.152 = (bf16[2,256,2688]{2,1,0:T(8,128)(2,1)}, bf16[2,656,512]{2,1,0:T(8,128)(2,1)S(1)}, bf16[2,256,512]{2,1,0:T(8,128)(2,1)S(1)}, bf16[2,256,1536]{2,1,0:T(8,128)(2,1)S(1)}, f32[32,8,256]{2,1,0:T(8,128)S(1)}) custom-call(bf16[2,256,2688]{2,1,0:T(8,128)(2,1)} %bitcast.156, bf16[2,656,512]{2,1,0:T(8,128)(2,1)S(1)} %bitcast.152, ...), custom_call_target="tpu_custom_call" | custom-call | tf_op jit(solution)/shard_map/pallas_call | solution.py:784
  (165 shorter events, 72.1 us)
Async XLA Ops:
  7.2 136.4 %all-gather.4.cloned.1.call-start = ((), (), s32[]{:S(2)}) async-start(), calls=%async_computation | async-start | bytes 2621440 | tf_op jit(solution)/shard_map/all_gather | solution.py:839
  7.9 138.9 %all-gather.6.cloned.1.call-start = ((), (), s32[]{:S(2)}) async-start(), calls=%async_computation.1 | async-start | bytes 13434880 | tf_op jit(solution)/shard_map/all_gather | solution.py:840
  8.7 160.7 %all-gather.8.cloned.1.call-start = ((), (), s32[]{:S(2)}) async-start(), calls=%async_computation.2 | async-start | bytes 6717440 | tf_op jit(solution)/shard_map/all_gather | solution.py:841
  61.5 14.0 %copy-start.3 = (bf16[2,64,1024]{2,1,0:T(8,128)(2,1)S(1)}, bf16[2,64,1024]{2,1,0:T(8,128)(2,1)}, u32[]{:S(2)}) copy-start(bf16[2,64,1024]{2,1,0:T(8,128)(2,1)} %param.8) | copy-start | bytes 786436
  76.0 4.5 copy-start.23
  169.4 7.1 %copy-start.5 = (f32[128,5248]{1,0:T(8,128)S(1)}, f32[128,5248]{1,0:T(8,128)}, u32[]{:S(2)}) copy-start(f32[128,5248]{1,0:T(8,128)} %fusion.63) | copy-start | bytes 8060932
  176.5 4.3 copy-start.2
  177.3 7.3 %copy-start.9 = (bf16[128,2624]{1,0:T(8,128)(2,1)}, bf16[128,2624]{1,0:T(8,128)(2,1)S(1)}, u32[]{:S(2)}) copy-start(bf16[128,2624]{1,0:T(8,128)(2,1)S(1)} %get-tuple-element.49) | copy-start | bytes 2015236
  180.8 3.6 copy-start.4
  191.6 3.9 copy-start.17
  258.7 1.7 copy-start.10
  271.6 22.4 %copy-start.22 = (bf16[1,128,1312]{2,1,0:T(8,128)(2,1)S(1)}, bf16[1,128,1312]{2,1,0:T(8,128)(2,1)}, u32[]{:S(2)}) copy-start(bf16[1,128,1312]{2,1,0:T(8,128)(2,1)} %get-tuple-element.77) | copy-start | bytes 1007620
  294.9 59.7 %copy-start.21 = (bf16[4,128,1536]{2,1,0:T(8,128)(2,1)S(1)}, bf16[4,128,1536]{2,1,0:T(8,128)(2,1)}, u32[]{:S(2)}) copy-start(bf16[4,128,1536]{2,1,0:T(8,128)(2,1)} %shard_map.151) | copy-start | bytes 4718596
  354.6 3.3 copy-start.29
  354.6 3.3 copy-start.30
  354.6 3.8 copy-start.28
  359.3 1.8 copy-start.14
  359.3 1.9 copy-start.26
  470.0 1.9 copy-start.6
  470.0 1.9 copy-start.18
  473.0 1.9 copy-start.11
  474.9 2.8 copy-start.24
  474.9 2.8 copy-start.25
  477.7 1.7 copy-start.13
  (12 other events, 17.0 us)
Sparse Core Ops, SparseCore 0:
  9.6 34.5 all-gather.3
  45.7 80.5 all-gather.5
  127.9 41.4 all-gather.7

commit v3 on v2

--- a/solution.py
+++ b/solution.py
@@ -281,6 +281,7 @@
     return jnp.concatenate([blocks[..., :half], blocks[..., half:]], axis=-2)
 
 
+CUTS = ((False, 1), (True, 4), (False, 2))
 CONTRACT_LAST = (((1,), (1,)), ((), ()))
 CONTRACT_FIRST = (((0,), (0,)), ((), ()))
 
@@ -369,7 +370,227 @@
     )(queries, key_rows, value_rows, context, log_total, grad)
 
 
-def by_head_forward(mixed_rows, cos_table, sin_table, scaling):
+def whole_mesh(me):
+    def other(step):
+        place = lax.rem(me + step, 32)
+        return place, (place // 4, lax.rem(place, 4))
+
+    return other
+
+
+def greet_all(other):
+    barrier = pltpu.get_barrier_semaphore()
+
+    @pl.loop(1, 32)
+    def _(step):
+        pl.semaphore_signal(barrier, inc=1, device_id=other(step)[1], device_id_type=MESH_ID)
+
+    pl.semaphore_wait(barrier, 31)
+
+
+def swap_lanes(value):
+    return pltpu.roll(value.astype(jnp.float32), 64, 1)
+
+
+def low_lanes(value):
+    return lax.broadcasted_iota(jnp.int32, value.shape, 1) < 64
+
+
+def weight_piece(ref, by_rows, half, index, count):
+    if by_rows:
+        size = ref.shape[0] // (2 * count)
+        start = pl.multiple_of((half * count + index) * size, 16)
+        return ref.at[pl.ds(start, size), :]
+    size = ref.shape[1] // (2 * count)
+    start = pl.multiple_of((half * count + index) * size, 128)
+    return ref.at[:, pl.ds(start, size)]
+
+
+def forward_kernel(cuts, *refs):
+    count = len(cuts)
+    sent, shards = refs[0], refs[1 : 1 + count]
+    got, context, log_ref, back = refs[1 + count : 5 + count]
+    fulls = refs[5 + count : 5 + 2 * count]
+    (keys, values, packed, head_send, head_recv, back_send, back_recv, own_sem) = refs[
+        5 + 2 * count : 13 + 2 * count
+    ]
+    w_send, w_recv = refs[13 + 2 * count :]
+    z, y, x, core = mesh_place()
+    place = 2 * x + core
+    me = 4 * (2 * z + y) + place
+    across = lax.rem(place + 2, 4)
+    other = whole_mesh(me)
+    sibling, partner = device_at(z, y, x, 1 - core), device_at(z, y, 1 - x, core)
+    neighbour = device_at(z, 1 - y, x, core)
+    greet_all(other)
+
+    def head_copy(step):
+        to, device = other(step)
+        return pltpu.make_async_remote_copy(
+            src_ref=sent.at[to],
+            dst_ref=got.at[me],
+            send_sem=head_send.at[step],
+            recv_sem=head_recv.at[step],
+            device_id=device,
+            device_id_type=MESH_ID,
+        )
+
+    def back_copy(to):
+        step = lax.rem(to - me + 32, 32)
+        return pltpu.make_async_remote_copy(
+            src_ref=packed.at[to],
+            dst_ref=back.at[me],
+            send_sem=back_send.at[step],
+            recv_sem=back_recv.at[step],
+            device_id=(to // 4, lax.rem(to, 4)),
+            device_id_type=MESH_ID,
+        )
+
+    serial = iter(range(w_send.shape[0]))
+
+    def send(src, dst, device):
+        sem = next(serial)
+        copy = pltpu.make_async_remote_copy(
+            src_ref=src,
+            dst_ref=dst,
+            send_sem=w_send.at[sem],
+            recv_sem=w_recv.at[sem],
+            device_id=device,
+            device_id_type=MESH_ID,
+        )
+        copy.start()
+        return copy
+
+    @pl.loop(1, 32)
+    def _(step):
+        head_copy(step).start()
+
+    own = [pltpu.make_async_copy(sent.at[me], got.at[me], own_sem.at[count])]
+    own[0].start()
+    crossing, handed, turned = [], [], []
+    for i, (by_rows, pieces) in enumerate(cuts):
+        for c in range(pieces):
+            src = weight_piece(shards[i], by_rows, y, c, pieces)
+            dst = weight_piece(fulls[i].at[place], by_rows, y, c, pieces)
+            crossing.append((i, c, send(src, dst, partner)))
+    for i in range(count):
+        copy = pltpu.make_async_copy(shards[i], fulls[i].at[place], own_sem.at[i])
+        copy.start()
+        own.append(copy)
+        handed.append(send(shards[i], fulls[i].at[place], sibling))
+
+    def turn(entry):
+        i, c, copy = entry
+        copy.wait_recv()
+        here = weight_piece(fulls[i].at[across], cuts[i][0], y, c, cuts[i][1])
+        turned.append((i, c, send(here, here, neighbour)))
+        handed.append(send(here, here, sibling))
+
+    def hand(entry):
+        i, c, copy = entry
+        copy.wait_recv()
+        here = weight_piece(fulls[i].at[across], cuts[i][0], 1 - y, c, cuts[i][1])
+        handed.append(send(here, here, sibling))
+
+    turn(crossing[0])
+    own[0].wait()
+
+    @pl.loop(1, 32)
+    def _(step):
+        head_copy(step).wait()
+
+    keys[0:1024] = got[:, 0:32, :].reshape(1024, 128)
+    keys[1024:2048] = got[:, 32:64, :].reshape(1024, 128)
+    values[...] = got[:, 64:96, :].reshape(1024, 128)
+
+    def attend_block(b):
+        block = lax.rem(b + me // 4, 8)
+        low_rows = pl.ds(pl.multiple_of(block * 128, 128), 128)
+        high_rows = pl.ds(pl.multiple_of(1024 + block * 128, 128), 128)
+        queries = swap_lanes(jnp.concatenate([keys[low_rows], keys[high_rows]], axis=0))
+        queries = jnp.where(low_lanes(queries), 0.0, queries).astype(jnp.bfloat16)
+        scores = lax.dot_general(
+            queries, keys[...], CONTRACT_LAST, preferred_element_type=jnp.float32
+        )
+        top = jnp.max(scores, axis=-1, keepdims=True)
+        weights = jnp.exp(scores - top)
+        total = jnp.sum(weights, axis=-1, keepdims=True)
+        weights = weights.astype(jnp.bfloat16)
+        first = jnp.dot(weights[:, :1024], values[...], preferred_element_type=jnp.float32)
+        second = jnp.dot(weights[:, 1024:], values[...], preferred_element_type=jnp.float32)
+        outcome = (first + pltpu.roll(second, 64, 1)) / total
+        side = pltpu.roll(outcome[128:], 64, 1)
+        outcome = jnp.where(low_lanes(side), outcome[:128], side)
+        context[low_rows] = outcome
+        log_total = top + jnp.log(total)
+        log_ref[0, low_rows] = log_total[:128]
+        log_ref[1, low_rows] = log_total[128:]
+        packed[pl.ds(4 * block, 4)] = outcome.astype(jnp.bfloat16).reshape(4, 32, 128)
+
+        @pl.loop(4 * block, 4 * block + 4)
+        def _(to):
+            @pl.when(to != me)
+            def _():
+                back_copy(to).start()
+
+    @pl.loop(0, 8)
+    def _(b):
+        attend_block(b)
+
+    mine = pltpu.make_async_copy(packed.at[me], back.at[me], own_sem.at[count + 1])
+    mine.start()
+    own.append(mine)
+    for index in range(1, len(crossing)):
+        turn(crossing[index])
+        hand(turned[index - 1])
+    hand(turned[-1])
+
+    @pl.loop(1, 32)
+    def _(step):
+        back_copy(lax.rem(me + step, 32)).wait()
+
+    for copy in handed:
+        copy.wait()
+    for _, _, copy in crossing + turned:
+        copy.wait_send()
+    for copy in own[1:]:
+        copy.wait()
+
+
+def forward_heads(sent, shards, cuts, collective_id):
+    in_vmem, anywhere = pl.BlockSpec(memory_space=pltpu.VMEM), pl.BlockSpec(memory_space=pl.ANY)
+    copies = len(shards) + sum(4 * pieces for _, pieces in cuts)
+    low, full = jnp.bfloat16, jnp.float32
+    sems = [pltpu.SemaphoreType.DMA((32,))] * 4
+    return pl.pallas_call(
+        functools.partial(forward_kernel, cuts),
+        out_shape=[
+            jax.ShapeDtypeStruct((32, 96, 128), low),
+            jax.ShapeDtypeStruct((1024, 128), full),
+            jax.ShapeDtypeStruct((2, 1024, 1), full),
+            jax.ShapeDtypeStruct((32, 32, 128), low),
+        ]
+        + [jax.ShapeDtypeStruct((4, *shard.shape), low) for shard in shards],
+        in_specs=[in_vmem] + [anywhere] * len(shards),
+        out_specs=[in_vmem] * 4 + [anywhere] * len(shards),
+        scratch_shapes=[
+            pltpu.VMEM((2048, 128), low),
+            pltpu.VMEM((1024, 128), low),
+            pltpu.VMEM((32, 32, 128), low),
+            *sems,
+            pltpu.SemaphoreType.DMA((len(shards) + 2,)),
+            pltpu.SemaphoreType.DMA((copies,)),
+            pltpu.SemaphoreType.DMA((copies,)),
+        ],
+        compiler_params=pltpu.CompilerParams(
+            collective_id=collective_id,
+            has_side_effects=True,
+            vmem_limit_bytes=48 * 1024 * 1024,
+        ),
+    )(sent, *shards)
+
+
+def by_head_forward(mixed_rows, cos_table, sin_table, scaling, shards=()):
     seq_count, row_count, _, head_count, head_size = mixed_rows.shape
     ctx_count, fsdp_count = lax.axis_size("ctx"), lax.axis_size("fsdp")
     count = ctx_count * fsdp_count
@@ -384,6 +605,21 @@
         ],
         axis=1,
     )
+    if shards:
+        got, context, log_total, back, *fulls = forward_heads(sent, shards, CUTS, 1)
+        context_low = (
+            unpack(back)
+            .reshape(seq_count, head_count, row_count, head_size)
+            .transpose(0, 2, 1, 3)
+            .reshape(seq_count * row_count, head_count * head_size)
+        )
+        flat = lambda rows: rows.reshape(count * row_count, head_size)
+        queries = flat(got[:, :row_count, :head_size])
+        key_rows = flat(got[:, :row_count, head_size:])
+        value_rows = flat(unpack(got[:, row_count:]))
+        context = flat(unpack(context.reshape(32, 32, 128)))
+        log_total = log_total.reshape(2, 32, 32).transpose(1, 0, 2).reshape(2048, 1)
+        return context_low, (queries, key_rows, value_rows, context, log_total), fulls
     got = exchange(sent, ctx_count, fsdp_count, 1)
     flat = lambda rows: rows.reshape(count * row_count, head_size)
     queries = flat(got[:, :row_count, :head_size])
@@ -402,7 +638,7 @@
         .transpose(0, 2, 1, 3)
         .reshape(seq_count * row_count, head_count * head_size)
     )
-    return context_low, (queries, key_rows, value_rows, context, log_total)
+    return context_low, (queries, key_rows, value_rows, context, log_total), ()
 
 
 def by_head_back(context_grad, saved, scaling, after):
@@ -440,7 +676,7 @@
     ), after
 
 
-def by_block_forward(mixed_rows, cos_table, sin_table, scaling):
+def by_block_forward(mixed_rows, cos_table, sin_table, scaling, shards=()):
     seq_count, row_count, _, head_count, head_size = mixed_rows.shape
     width = head_count * head_size
     queries = rotate(mixed_rows[:, :, 0], cos_table, sin_table).astype(jnp.bfloat16)
@@ -467,7 +703,8 @@
     context = (weighted / denominator[..., None]).transpose(0, 2, 1, 3)
     log_total = running_max + jnp.log(denominator)
     context_low = context.reshape(seq_count * row_count, width).astype(jnp.bfloat16)
-    return context_low, (queries, key_block, value_block, context, log_total, cos_table, sin_table)
+    saved = queries, key_block, value_block, context, log_total, cos_table, sin_table
+    return context_low, saved, ()
 
 
 def by_block_back(context_grad, saved, scaling, after):
@@ -832,14 +1069,15 @@
     gain_one, gain_two = gains[0], gains[1]
     ctx_count = lax.axis_size("ctx")
     small = one_head_each and fsdp_count == 4 and ctx_count == 8
-    proj_full, out_full, lift_full, down_full = (
-        gather(attn_proj, True, 3, 6)
-        if small
-        else lax.all_gather(attn_proj, "fsdp", axis=0, tiled=True),
-        lax.all_gather(attn_out, "fsdp", axis=0, tiled=True),
-        lax.all_gather(mlp_in, "fsdp", axis=0, tiled=True),
-        lax.all_gather(mlp_out, "fsdp", axis=0, tiled=True),
-    )
+    if small:
+        proj_full = gather(attn_proj, True, 3, 6)
+        shards = attn_out, mlp_in, mlp_out
+    else:
+        shards = ()
+        proj_full, out_full, lift_full, down_full = (
+            lax.all_gather(rows, "fsdp", axis=0, tiled=True)
+            for rows in (attn_proj, attn_out, mlp_in, mlp_out)
+        )
     states = inputs.astype(jnp.float32)
     normed, norm_back_one = jax.vjp(layer_norm, states, gain_one)
     normed_low = normed.astype(jnp.bfloat16).reshape(tokens, model_width)
@@ -849,7 +1087,11 @@
     attention, attention_back = (
         (by_head_forward, by_head_back) if one_head_each else (by_block_forward, by_block_back)
     )
-    context_low, saved = attention(mixed_rows, cos_table, sin_table, scaling)
+    context_low, saved, fulls = attention(mixed_rows, cos_table, sin_table, scaling, shards)
+    if small:
+        out_full, lift_full, down_full = (
+            full.reshape(4 * full.shape[1], full.shape[2]) for full in fulls
+        )
     branch = jnp.dot(context_low, out_full, preferred_element_type=jnp.float32).reshape(
         seq_count, row_count, model_width
     )

time: 494 us -> 501 us (1.014)
  Pallas kernels: 322 us -> 366 us
  waiting for transfers between devices: 17.3 us -> 0 us
  between operations: 14.9 us -> 1.92 us
    pallas_call x1, Pallas kernels: 8.48 us -> 89 us  [forward_heads(): pl.pallas_call(functools.partial(forward_kernel, cuts), out_shape=[jax.Sh...]
    pallas_call x4 -> x2, Pallas kernels: 65.2 us -> 28.9 us  [exchange(): pl.pallas_call(functools.partial(exchange_kernel, ctx_count, fsdp_count),...]
    all_gather x3 -> x0, waiting for transfers between devices: 15.2 us -> none  [the longest x1 15.2 us: on_device(): lax.all_gather(mlp_out, 'fsdp', axis=0, tiled=True)]
  transfers between devices with their start and end apart: 3 -> 0, of which waited for: 1 -> 0; matrix products, arithmetic and copies ran while one was open for 9% -> 0% of each run, Pallas kernels for 19% -> 0%
where the time goes in v3:
time: 501 us; the launch traced here: 496 us
  Pallas kernels  366 us (73%)
  local copies, waits for them, and re-layouts  41.6 us (8%)
  other arithmetic  40.9 us (8%)
  matrix products  39.5 us (8%)
  blocking collectives  5.98 us (1%)
    pallas_call x1, Pallas kernels, finish(): pl.pallas_call(functools.partial(finish_kernel, chunks, len(parts)), out_...  101 us
    pallas_call x1, Pallas kernels, forward_heads(): pl.pallas_call(functools.partial(forward_kernel, cuts), out_shape=[jax.Sh...  89 us
    pallas_call x2, Pallas kernels, plane(): pl.pallas_call(functools.partial(plane_kernel, kinds, cuts), out_shape=[j...  82.7 us
    pallas_call x1, Pallas kernels, gather(): pl.pallas_call(functools.partial(gather_kernel, spread, chunks), out_shap...  51.1 us
    pallas_call x2, Pallas kernels, exchange(): pl.pallas_call(functools.partial(exchange_kernel, ctx_count, fsdp_count),...  28.9 us
    pallas_call x1, Pallas kernels, attend_back(): pl.pallas_call(attend_back_kernel, grid=(rows // block,), out_shape=(jax....  14.1 us

profile of v3, /device:TPU:0, one launch (start us, length us, event | category | flops | bytes accessed | tf_op | source)
XLA Modules:
  0.0 496.2 jit_solution(17458963953486996232)
XLA Ops:
  4.2 6.0 %all_gather.3 = bf16[2,1024]{1,0:T(2,128)(2,1)S(1)} all-gather(bf16[2,256]{1,0:T(2,128)(2,1)S(1)} %pad_maximum_fusion.9), channel_id=1, replica_groups=mesh['ctx'=8,'fsdp'=4] {'fsdp'}, dimensions={1}, use_global_device_ids=true | all-gather | bytes 5120 | tf_op jit(solution)/shard_map/all_gather | solution.py:1066
  11.4 51.1 %shard_map.143 = bf16[4,256,3072]{2,1,0:T(8,128)(2,1)} custom-call(bf16[256,3072]{1,0:T(8,128)(2,1)} %x_ref.1), custom_call_target="tpu_custom_call" | custom-call | tf_op jit(solution)/shard_map/pallas_call | solution.py:260
  62.5 8.6 %copy.32 = bf16[1024,3072]{0,1:T(8,128)(2,1)} copy(bf16[1024,3072]{1,0:T(8,128)(2,1)} %bitcast.157) | data formatting | bytes 12582912 | tf_op jit(solution)/shard_map/reshape | solution.py:271
  71.1 4.3 fusion.36
  77.3 2.2 fusion.32
  89.6 89.0 %shard_map.144 = (bf16[32,96,128]{2,1,0:T(8,128)(2,1)S(1)}, f32[1024,128]{1,0:T(8,128)S(1)}, f32[2,1024,1]{2,1,0:T(8,128)S(1)}, bf16[32,32,128]{2,1,0:T(8,128)(2...) custom-call(bf16[32,96,128]{2,1,0:T(8,128)(2,1)S(1)} %maximum_maximum_fusion.re, ...), custom_call_target="tpu_custom_call" | custom-call | tf_op jit(solution)/shard_map/pallas_call | solution.py:565
  180.4 2.2 fusion.59
  183.0 5.9 %fusion.60 = f32[128,5248]{1,0:T(8,128)S(1)} fusion(bf16[128,1024]{1,0:T(8,128)(2,1)S(1)} %bitcast.176, bf16[1024,5248]{1,0:T(8,128)(2,1)} %bitcast.159), kind=kOutput, calls=%fused_computation.144 | convolution fusion | flops 1375731712 | bytes 13697024 | tf_op jit(solution)/shard_map/dot_general | solution.py:1101
  188.9 3.9 fusion.34
  194.9 3.7 multiply_reduce_fusion
  206.2 9.0 %shard_map.145 = bf16[32,32,128]{2,1,0:T(8,128)(2,1)} custom-call(bf16[32,32,128]{2,1,0:T(8,128)(2,1)} %pad_maximum_fusion.7.x_ref), custom_call_target="tpu_custom_call" | custom-call | tf_op jit(solution)/shard_map/pallas_call | solution.py:171
  220.9 14.1 %shard_map.146 = (f32[2048,64]{1,0:T(8,128)S(1)}, f32[2048,64]{1,0:T(8,128)S(1)}, f32[2048,64]{1,0:T(8,128)S(1)}) custom-call(bf16[2048,64]{1,0:T(8,128)(2,1)S(1)} %bitcast.154, bf16[2048,64]{1,0:T(8,128)(2,1)S(1)} %bitcast.153, bf16[2048,64]{1,0:T(8,128)(2,1)S(1)} %bitcast.152, f32[2048,64]{1,0:T(8,128)} %bitcast.175, f32[2048,1]{1,0:T(8,128)} %reshape.309.log_ref, ...), custom_call_target="tpu_custom_call" | custom-call | tf_op jit(solution)/shard_map/pallas_call | solution.py:356
  235.3 3.8 multiply_multiply_fusion.5
  239.5 4.8 fusion.15
  244.6 4.0 fusion.16
  250.1 19.9 %shard_map.147 = bf16[32,96,128]{2,1,0:T(8,128)(2,1)} custom-call(bf16[32,96,128]{2,1,0:T(8,128)(2,1)} %maximum_maximum_fusion.1.x_ref), custom_call_target="tpu_custom_call" | custom-call | tf_op jit(solution)/shard_map/pallas_call | solution.py:171
  275.7 5.4 %fusion.29 = (f32[2,64]{1,0:T(2,128)S(1)}, f32[2,64,1024]{2,1,0:T(8,128)S(1)}) fusion(bf16[2,64,1024]{2,1,0:T(8,128)(2,1)S(1)} %copy-done.4, f32[1024]{0:T(1024)S(1)} %bitcast.197, f32[2,64]{1,0:T(2,128)S(1)} %broadcast_multiply_fusion.3, bf16[2,64,3072]{2,1,0:T(8,128)(2,1)} %dot_general.63, bf16[1024,3072,1]{1,0,2:T(8,128)(2,1)} %bitcast.158), kind=kOutput, calls=%fused_computation.79 | convolution fusion | flops 805961600 | bytes 7869440 | tf_op jit(solution)/shard_map/tm,wm->tw/dot_general | solution.py:1160
  285.2 63.2 %shard_map.148 = (bf16[4,128,512]{2,1,0:T(8,128)(2,1)}, bf16[4,128,512]{2,1,0:T(8,128)(2,1)}, bf16[4,128,512]{2,1,0:T(8,128)(2,1)}, bf16[4,128,1312]{2,1,0:T(8,1...) custom-call(bf16[128,1024]{1,0:T(8,128)(2,1)} %bitcast.177, ...), custom_call_target="tpu_custom_call" | custom-call | tf_op jit(solution)/shard_map/pallas_call | solution.py:864
  350.3 19.5 %shard_map.149 = bf16[4,128,1536]{2,1,0:T(8,128)(2,1)} custom-call(bf16[128,3072]{1,0:T(8,128)(2,1)} %reshape.297.refs_0_), custom_call_target="tpu_custom_call" | custom-call | tf_op jit(solution)/shard_map/pallas_call | solution.py:864
  369.8 3.8 fusion.1
  376.9 3.2 bitcast_convert_fusion
  380.1 100.5 %shard_map.150 = (bf16[2,256,2688]{2,1,0:T(8,128)(2,1)}, bf16[2,656,512]{2,1,0:T(8,128)(2,1)S(1)}, bf16[2,256,512]{2,1,0:T(8,128)(2,1)S(1)}, bf16[2,256,1536]{2,1,0:T(8,128)(2,1)S(1)}, f32[32,8,256]{2,1,0:T(8,128)S(1)}) custom-call(bf16[2,256,2688]{2,1,0:T(8,128)(2,1)} %bitcast.164, bf16[2,656,512]{2,1,0:T(8,128)(2,1)S(1)} %bitcast.155, ...), custom_call_target="tpu_custom_call" | custom-call | tf_op jit(solution)/shard_map/pallas_call | solution.py:1021
  483.8 2.7 maximum_convert_fusion
  491.6 4.1 fusion.10
  (155 shorter events, 59.1 us)
Async XLA Ops:
  11.4 59.8 %copy-start.21 = (bf16[2,64,1024]{2,1,0:T(8,128)(2,1)}, bf16[2,64,1024]{2,1,0:T(8,128)(2,1)S(1)}, u32[]{:S(2)}) copy-start(bf16[2,64,1024]{2,1,0:T(8,128)(2,1)S(1)} %fusion.26) | copy-start | bytes 786436
  86.7 1.5 copy-start.20
  178.8 1.6 copy-start.3
  182.8 6.1 %slice-start.3 = ((s8[5373952]{0:T(1024)(128)(4,1)}), s8[4194304]{0:T(1024)(128)(4,1)S(1)}, s32[]{:S(2)}) async-start(s8[5373952]{0:T(1024)(128)(4,1)} %bitcast.170), calls=%async_computation.3 | async-start | bytes 8388608
  183.0 5.9 %copy-start.13 = (bf16[2,64,1024]{2,1,0:T(8,128)(2,1)}, bf16[2,64,1024]{2,1,0:T(8,128)(2,1)S(1)}, u32[]{:S(2)}) copy-start(bf16[2,64,1024]{2,1,0:T(8,128)(2,1)S(1)} %multiply_convert_fusion.1) | copy-start | bytes 786436
  183.0 5.9 %slice-start.4 = ((s8[5373952]{0:T(1024)(128)(4,1)}), s8[1179648]{0:T(1024)(128)(4,1)S(1)}, s32[]{:S(2)}) async-start(s8[5373952]{0:T(1024)(128)(4,1)} %bitcast.170), calls=%async_computation.4 | async-start | bytes 2359296
  183.0 5.9 %copy-start.17 = (bf16[2,64,1024]{2,1,0:T(8,128)(2,1)S(1)}, bf16[2,64,1024]{2,1,0:T(8,128)(2,1)}, u32[]{:S(2)}) copy-start(bf16[2,64,1024]{2,1,0:T(8,128)(2,1)} %param.15) | copy-start | bytes 786436
  183.0 11.8 %slice-start = ((s8[10747904]{0:T(1024)(128)(4,1)}), s8[4194304]{0:T(1024)(128)(4,1)S(1)}, s32[]{:S(2)}) async-start(s8[10747904]{0:T(1024)(128)(4,1)} %bitcast.160), calls=%async_computation | async-start | bytes 8388608
  188.9 5.9 %slice-start.1 = ((s8[10747904]{0:T(1024)(128)(4,1)}), s8[4194304]{0:T(1024)(128)(4,1)S(1)}, s32[]{:S(2)}) async-start(s8[10747904]{0:T(1024)(128)(4,1)} %bitcast.160), calls=%async_computation.1 | async-start | bytes 8388608
  188.9 5.9 %slice-start.2 = ((s8[10747904]{0:T(1024)(128)(4,1)}), s8[2359296]{0:T(1024)(128)(4,1)S(1)}, s32[]{:S(2)}) async-start(s8[10747904]{0:T(1024)(128)(4,1)} %bitcast.160), calls=%async_computation.2 | async-start | bytes 4718592
  194.8 3.7 copy-start.2
  198.5 1.9 copy-start.5
  198.8 3.1 copy-start.8
  273.6 2.1 copy-start.4
  275.7 6.2 %copy-start.7 = (bf16[128,2624]{1,0:T(8,128)(2,1)S(1)}, bf16[128,2624]{1,0:T(8,128)(2,1)}, u32[]{:S(2)}) copy-start(bf16[128,2624]{1,0:T(8,128)(2,1)} %get-tuple-element.61) | copy-start | bytes 2015236
  369.8 3.9 copy-start.25
  369.8 3.9 copy-start.26
  369.8 4.3 copy-start.24
  375.0 1.8 copy-start.14
  375.0 1.9 copy-start.22
  480.8 2.7 copy-start.15
  487.8 2.7 copy-start.9
  487.8 2.7 copy-start.12
  487.8 2.7 copy-start.18
  (8 other events, 9.3 us)

commit v4 on v3

--- a/solution.py
+++ b/solution.py
@@ -260,7 +260,7 @@
     return pl.pallas_call(
         functools.partial(gather_kernel, spread, chunks),
         out_shape=jax.ShapeDtypeStruct((4, rows, width), block.dtype),
-        in_specs=[pl.BlockSpec(memory_space=pl.ANY)],
+        in_specs=[pl.BlockSpec(memory_space=pltpu.VMEM)],
         out_specs=pl.BlockSpec(memory_space=pl.ANY),
         scratch_shapes=[
             pltpu.SemaphoreType.DMA((count,)),
@@ -281,7 +281,7 @@
     return jnp.concatenate([blocks[..., :half], blocks[..., half:]], axis=-2)
 
 
-CUTS = ((False, 1), (True, 4), (False, 2))
+CUTS = ((False, 1), (True, 4), (False, 4))
 CONTRACT_LAST = (((1,), (1,)), ((), ()))
 CONTRACT_FIRST = (((0,), (0,)), ((), ()))
 
@@ -493,6 +493,7 @@
         handed.append(send(here, here, sibling))
 
     turn(crossing[0])
+    turn(crossing[1])
     own[0].wait()
 
     @pl.loop(1, 32)
@@ -533,16 +534,27 @@
             def _():
                 back_copy(to).start()
 
-    @pl.loop(0, 8)
+    turn(crossing[2])
+    hand(turned[0])
+
+    @pl.loop(0, 4)
+    def _(b):
+        attend_block(b)
+
+    turn(crossing[3])
+    hand(turned[1])
+
+    @pl.loop(4, 8)
     def _(b):
         attend_block(b)
 
     mine = pltpu.make_async_copy(packed.at[me], back.at[me], own_sem.at[count + 1])
     mine.start()
     own.append(mine)
-    for index in range(1, len(crossing)):
+    for index in range(4, len(crossing)):
         turn(crossing[index])
-        hand(turned[index - 1])
+        hand(turned[index - 2])
+    hand(turned[-2])
     hand(turned[-1])
 
     @pl.loop(1, 32)
@@ -571,7 +583,7 @@
             jax.ShapeDtypeStruct((32, 32, 128), low),
         ]
         + [jax.ShapeDtypeStruct((4, *shard.shape), low) for shard in shards],
-        in_specs=[in_vmem] + [anywhere] * len(shards),
+        in_specs=[in_vmem] * (1 + len(shards)),
         out_specs=[in_vmem] * 4 + [anywhere] * len(shards),
         scratch_shapes=[
             pltpu.VMEM((2048, 128), low),
@@ -590,6 +602,190 @@
     )(sent, *shards)
 
 
+def back_kernel(kinds, cuts, scaling, *refs):
+    count = len(kinds)
+    sent, got, context, log_ref, cos_ref, sin_ref = refs[:6]
+    parts, result = refs[6 : 6 + count], refs[6 + count]
+    outs = refs[7 + count : 7 + 2 * count]
+    (grads, keys, values, dq, dk, dv, packed, go_send, go_recv, back_send, back_recv, mine_sem) = refs[
+        7 + 2 * count : 19 + 2 * count
+    ]
+    me = lax.axis_index("ctx") * 4 + lax.axis_index("fsdp")
+    other = whole_mesh(me)
+    greet_all(other)
+
+    def go_copy(step):
+        to, device = other(step)
+        return pltpu.make_async_remote_copy(
+            src_ref=sent.at[to],
+            dst_ref=grads.at[me],
+            send_sem=go_send.at[step],
+            recv_sem=go_recv.at[step],
+            device_id=device,
+            device_id_type=MESH_ID,
+        )
+
+    def back_copy(to):
+        step = lax.rem(to - me + 32, 32)
+        return pltpu.make_async_remote_copy(
+            src_ref=packed.at[to],
+            dst_ref=result.at[me],
+            send_sem=back_send.at[step],
+            recv_sem=back_recv.at[step],
+            device_id=(to // 4, lax.rem(to, 4)),
+            device_id_type=MESH_ID,
+        )
+
+    @pl.loop(1, 32)
+    def _(step):
+        go_copy(step).start()
+
+    mine = pltpu.make_async_copy(sent.at[me], grads.at[me], mine_sem.at[0])
+    mine.start()
+    start, turn, end = plane_moves(kinds, cuts, parts, outs, *refs[19 + 2 * count :])
+    start()
+    keys[0:1024] = got[:, 0:32, :].reshape(1024, 128)
+    keys[1024:2048] = got[:, 32:64, :].reshape(1024, 128)
+    values[...] = got[:, 64:96, :].reshape(1024, 128)
+    dk[...] = jnp.zeros_like(dk)
+    dv[...] = jnp.zeros_like(dv)
+    mine.wait()
+
+    @pl.loop(1, 32)
+    def _(step):
+        go_copy(step).wait()
+
+    def rows_of(block):
+        return (
+            pl.ds(pl.multiple_of(block * 128, 128), 128),
+            pl.ds(pl.multiple_of(1024 + block * 128, 128), 128),
+        )
+
+    def grad_block(block):
+        low_rows, high_rows = rows_of(block)
+        queries = swap_lanes(jnp.concatenate([keys[low_rows], keys[high_rows]], axis=0))
+        queries = jnp.where(low_lanes(queries), 0.0, queries).astype(jnp.bfloat16)
+        pair = grads[pl.ds(4 * block, 4)].reshape(128, 128).astype(jnp.float32)
+        side = pltpu.roll(pair, 64, 1)
+        first = low_lanes(pair)
+        grad = jnp.concatenate([jnp.where(first, pair, 0.0), jnp.where(first, side, 0.0)], axis=0)
+        above = jnp.concatenate([jnp.where(first, 0.0, side), jnp.where(first, 0.0, pair)], axis=0)
+        grad, above = grad.astype(jnp.bfloat16), above.astype(jnp.bfloat16)
+        product = pair * context[low_rows]
+        inner = jnp.concatenate(
+            [
+                jnp.sum(jnp.where(first, product, 0.0), axis=-1, keepdims=True),
+                jnp.sum(jnp.where(first, 0.0, product), axis=-1, keepdims=True),
+            ],
+            axis=0,
+        )
+        log_total = jnp.concatenate([log_ref[0, low_rows], log_ref[1, low_rows]], axis=0)
+        scores = lax.dot_general(
+            queries, keys[...], CONTRACT_LAST, preferred_element_type=jnp.float32
+        )
+        probs = jnp.exp(scores - log_total)
+        prob_grad = jnp.concatenate(
+            [
+                lax.dot_general(
+                    side_grad, values[...], CONTRACT_LAST, preferred_element_type=jnp.float32
+                )
+                for side_grad in (grad, above)
+            ],
+            axis=1,
+        )
+        score_grad = (probs * (prob_grad - inner)).astype(jnp.bfloat16)
+        dv[...] += lax.dot_general(
+            probs.astype(jnp.bfloat16), grad, CONTRACT_FIRST, preferred_element_type=jnp.float32
+        )
+        dk[...] += lax.dot_general(
+            score_grad, queries, CONTRACT_FIRST, preferred_element_type=jnp.float32
+        )
+        query_grad = jnp.dot(score_grad, keys[...], preferred_element_type=jnp.float32)
+        dq[low_rows] = query_grad[:128]
+        dq[high_rows] = query_grad[128:]
+
+    @pl.loop(0, 4)
+    def _(block):
+        grad_block(block)
+
+    turn(4)
+
+    @pl.loop(4, 8)
+    def _(block):
+        grad_block(block)
+
+    turn(3)
+
+    def unrotated(rows):
+        both = jnp.where(
+            low_lanes(dk[rows]), pltpu.roll(dq[rows] * scaling, 64, 1), dk[rows]
+        )
+        sined = both * sin_ref[rows]
+        lane = lax.rem(lax.broadcasted_iota(jnp.int32, both.shape, 1), 64)
+        turned = jnp.where(lane < 32, pltpu.roll(sined, 96, 1), -pltpu.roll(sined, 32, 1))
+        return (both * cos_ref[rows] + turned).astype(jnp.bfloat16).reshape(4, 32, 128)
+
+    @pl.loop(0, 8)
+    def _(b):
+        block = lax.rem(b + me // 4, 8)
+        low_rows, high_rows = rows_of(block)
+        places = pl.ds(4 * block, 4)
+        packed[places, 0:32, :] = unrotated(low_rows)
+        packed[places, 32:64, :] = unrotated(high_rows)
+        side = pltpu.roll(dv[high_rows], 64, 1)
+        value_pair = jnp.where(low_lanes(side), dv[low_rows], side)
+        packed[places, 64:96, :] = value_pair.astype(jnp.bfloat16).reshape(4, 32, 128)
+
+        @pl.loop(4 * block, 4 * block + 4)
+        def _(to):
+            @pl.when(to != me)
+            def _():
+                back_copy(to).start()
+
+    own = pltpu.make_async_copy(packed.at[me], result.at[me], mine_sem.at[1])
+    own.start()
+    turn(64)
+
+    @pl.loop(1, 32)
+    def _(step):
+        back_copy(lax.rem(me + step, 32)).wait()
+
+    own.wait()
+    end()
+
+
+def back_heads(sent, saved, tables, parts, kinds, widths, cuts, scaling, collective_id):
+    in_vmem, anywhere = pl.BlockSpec(memory_space=pltpu.VMEM), pl.BlockSpec(memory_space=pl.ANY)
+    low, full, rows = jnp.bfloat16, jnp.float32, parts[0].shape[-2]
+    result, *outs = pl.pallas_call(
+        functools.partial(back_kernel, kinds, cuts, scaling),
+        out_shape=[jax.ShapeDtypeStruct((32, 96, 128), low)]
+        + [jax.ShapeDtypeStruct((4, rows, width), low) for width in widths],
+        in_specs=[in_vmem] * (6 + len(parts)),
+        out_specs=[in_vmem] + [anywhere] * len(parts),
+        scratch_shapes=[
+            pltpu.VMEM((32, 32, 128), low),
+            pltpu.VMEM((2048, 128), low),
+            pltpu.VMEM((1024, 128), low),
+            pltpu.VMEM((2048, 128), full),
+            pltpu.VMEM((2048, 128), full),
+            pltpu.VMEM((2048, 128), full),
+            pltpu.VMEM((32, 96, 128), low),
+            *[pltpu.SemaphoreType.DMA((32,))] * 4,
+            pltpu.SemaphoreType.DMA((2,)),
+            pltpu.SemaphoreType.DMA((3 * sum(cuts),)),
+            pltpu.SemaphoreType.DMA((3 * sum(cuts),)),
+            pltpu.SemaphoreType.DMA((len(parts),)),
+        ],
+        compiler_params=pltpu.CompilerParams(
+            collective_id=collective_id,
+            has_side_effects=True,
+            vmem_limit_bytes=56 * 1024 * 1024,
+        ),
+    )(sent, *saved, *tables, *parts)
+    return result, [out.reshape(4 * rows, width) for out, width in zip(outs, widths)]
+
+
 def by_head_forward(mixed_rows, cos_table, sin_table, scaling, shards=()):
     seq_count, row_count, _, head_count, head_size = mixed_rows.shape
     ctx_count, fsdp_count = lax.axis_size("ctx"), lax.axis_size("fsdp")
@@ -613,13 +809,7 @@
             .transpose(0, 2, 1, 3)
             .reshape(seq_count * row_count, head_count * head_size)
         )
-        flat = lambda rows: rows.reshape(count * row_count, head_size)
-        queries = flat(got[:, :row_count, :head_size])
-        key_rows = flat(got[:, :row_count, head_size:])
-        value_rows = flat(unpack(got[:, row_count:]))
-        context = flat(unpack(context.reshape(32, 32, 128)))
-        log_total = log_total.reshape(2, 32, 32).transpose(1, 0, 2).reshape(2048, 1)
-        return context_low, (queries, key_rows, value_rows, context, log_total), fulls
+        return context_low, (got, context, log_total), fulls
     got = exchange(sent, ctx_count, fsdp_count, 1)
     flat = lambda rows: rows.reshape(count * row_count, head_size)
     queries = flat(got[:, :row_count, :head_size])
@@ -641,10 +831,28 @@
     return context_low, (queries, key_rows, value_rows, context, log_total), ()
 
 
-def by_head_back(context_grad, saved, scaling, after):
+def by_head_back(context_grad, saved, scaling, after, planes=()):
     seq_count, row_count, head_count, head_size = context_grad.shape
     ctx_count, fsdp_count = lax.axis_size("ctx"), lax.axis_size("fsdp")
     count = ctx_count * fsdp_count
+    if planes:
+        sent = pack(context_grad.transpose(0, 2, 1, 3).reshape(count, row_count, head_size))
+        order = jnp.arange(count * row_count, dtype=jnp.int32)
+        order = order.reshape(count, 2, row_count // 2).transpose(1, 0, 2).reshape(-1)
+        tables = [jnp.tile(table[:, 0], (1, 2)) for table in angles(order, head_size)]
+        got, lefts = back_heads(sent, saved, tables, *planes, scaling, 2)
+        parts = jnp.stack(
+            [
+                got[:, :row_count, :head_size],
+                got[:, :row_count, head_size:],
+                unpack(got[:, row_count:]),
+            ]
+        )
+        return (
+            parts.reshape(3, seq_count, head_count, row_count, head_size)
+            .transpose(1, 3, 0, 2, 4)
+            .reshape(seq_count * row_count, 3 * head_count * head_size)
+        ), lefts
     queries, key_rows, value_rows, context, log_total = saved
     sent = pack(context_grad.transpose(0, 2, 1, 3).reshape(count, row_count, head_size))
     grad = unpack(exchange(sent, ctx_count, fsdp_count, 3)).reshape(count * row_count, head_size)
@@ -707,7 +915,7 @@
     return context_low, saved, ()
 
 
-def by_block_back(context_grad, saved, scaling, after):
+def by_block_back(context_grad, saved, scaling, after, planes=()):
     seq_count, row_count, head_count, head_size = context_grad.shape
     width = head_count * head_size
     queries, key_block, value_block, context, log_total, cos_table, sin_table = saved
@@ -797,13 +1005,7 @@
     return list(zip(edges[:-1], edges[1:]))
 
 
-def plane_kernel(kinds, cuts, *refs):
-    count = len(kinds)
-    ins, outs = refs[:count], refs[count : 2 * count]
-    send_sem, recv_sem, own_sem = refs[2 * count :]
-    z, y, x, core = mesh_place()
-    to_x, to_y = device_at(z, y, 1 - x, core), device_at(z, 1 - y, x, core)
-    greet(pltpu.get_barrier_semaphore(), (to_x, to_y))
+def sender(send_sem, recv_sem):
     serial = iter(range(send_sem.shape[0]))
 
     def send(src, dst, device):
@@ -819,43 +1021,72 @@
         copy.start()
         return copy
 
-    def block(ref, out, index):
-        width = out.shape[2]
+    return send
+
+
+def plane_moves(kinds, cuts, ins, outs, send_sem, recv_sem, own_sem):
+    z, y, x, core = mesh_place()
+    to_x, to_y = device_at(z, y, 1 - x, core), device_at(z, 1 - y, x, core)
+    send = sender(send_sem, recv_sem)
+    firsts, seconds, owns = [], [], []
+
+    def block(i, index):
+        ref, width = ins[i], outs[i].shape[2]
         if len(ref.shape) == 3:
             return ref.at[index]
         step = ref.shape[1] - width
         return ref.at[:, pl.ds(pl.multiple_of(index * step, 128), width)]
 
-    owns = []
-    for i in range(count):
-        own = block(ins[i], outs[i], y if kinds[i] else x)
-        copy = pltpu.make_async_copy(own, outs[i].at[0], own_sem.at[i])
-        copy.start()
-        owns.append(copy)
-    firsts, seconds = [], []
-    for i in range(count):
-        own = block(ins[i], outs[i], y if kinds[i] else x)
-        away = block(ins[i], outs[i], 1 - y if kinds[i] else 1 - x)
-        for low, high in spans(outs[i].shape[1], cuts[i]):
-            rows = pl.ds(low, high - low)
-            by_x = send((own if kinds[i] else away).at[rows], outs[i].at[1, rows], to_x)
-            by_y = send((away if kinds[i] else own).at[rows], outs[i].at[2, rows], to_y)
-            firsts.append((i, rows, by_x, by_y))
-    for i, rows, by_x, by_y in firsts:
-        if kinds[i]:
-            by_y.wait_recv()
-            seconds.append(send(outs[i].at[2, rows], outs[i].at[3, rows], to_x))
-        else:
-            by_x.wait_recv()
-            seconds.append(send(outs[i].at[1, rows], outs[i].at[3, rows], to_y))
-    for i, rows, by_x, by_y in firsts:
-        (by_x if kinds[i] else by_y).wait_recv()
-        by_x.wait_send()
-        by_y.wait_send()
-    for copy in seconds:
-        copy.wait()
-    for copy in owns:
-        copy.wait()
+    def start():
+        for i, kind in enumerate(kinds):
+            own = block(i, y if kind else x)
+            away = block(i, 1 - y if kind else 1 - x)
+            for low, high in spans(outs[i].shape[1], cuts[i]):
+                rows = pl.ds(low, high - low)
+                by_x = send((own if kind else away).at[rows], outs[i].at[1, rows], to_x)
+                by_y = send((away if kind else own).at[rows], outs[i].at[2, rows], to_y)
+                firsts.append((i, rows, by_x, by_y))
+        for i, kind in enumerate(kinds):
+            own = block(i, y if kind else x)
+            copy = pltpu.make_async_copy(own, outs[i].at[0], own_sem.at[i])
+            copy.start()
+            owns.append(copy)
+
+    def turn(count):
+        for i, rows, by_x, by_y in firsts[len(seconds) :][:count]:
+            if kinds[i]:
+                by_y.wait_recv()
+                seconds.append(send(outs[i].at[2, rows], outs[i].at[3, rows], to_x))
+            else:
+                by_x.wait_recv()
+                seconds.append(send(outs[i].at[1, rows], outs[i].at[3, rows], to_y))
+
+    def end():
+        turn(len(firsts))
+        for i, rows, by_x, by_y in firsts:
+            (by_x if kinds[i] else by_y).wait_recv()
+            by_x.wait_send()
+            by_y.wait_send()
+        for copy in seconds:
+            copy.wait()
+        for copy in owns:
+            copy.wait()
+
+    return start, turn, end
+
+
+def plane_kernel(kinds, cuts, *refs):
+    count = len(kinds)
+    z, y, x, core = mesh_place()
+    greet(
+        pltpu.get_barrier_semaphore(),
+        (device_at(z, y, 1 - x, core), device_at(z, 1 - y, x, core)),
+    )
+    start, turn, end = plane_moves(
+        kinds, cuts, refs[:count], refs[count : 2 * count], *refs[2 * count :]
+    )
+    start()
+    end()
 
 
 def plane(parts, kinds, widths, cuts, collective_id):
@@ -864,7 +1095,7 @@
     outs = pl.pallas_call(
         functools.partial(plane_kernel, kinds, cuts),
         out_shape=[jax.ShapeDtypeStruct((4, rows, width), jnp.bfloat16) for width in widths],
-        in_specs=[pl.BlockSpec(memory_space=pl.ANY)] * len(parts),
+        in_specs=[pl.BlockSpec(memory_space=pltpu.VMEM)] * len(parts),
         out_specs=[pl.BlockSpec(memory_space=pl.ANY)] * len(parts),
         scratch_shapes=[
             pltpu.SemaphoreType.DMA((sems,)),
@@ -1070,7 +1301,7 @@
     ctx_count = lax.axis_size("ctx")
     small = one_head_each and fsdp_count == 4 and ctx_count == 8
     if small:
-        proj_full = gather(attn_proj, True, 3, 6)
+        proj_full = gather(attn_proj, True, 6, 6)
         shards = attn_out, mlp_in, mlp_out
     else:
         shards = ()
@@ -1126,16 +1357,16 @@
         hidden = gate_low.shape[1] // 2
         lift_half = -(-lifted_width // 256) * 128
         gate_halves = jnp.stack([gate_low[:, :hidden], gate_low[:, hidden:]])
-        normed_two_left, context_left, normed_left, gate_left, seed_right, middle_right, lift_right = (
-            plane(
-                (normed_two_low, context_low, normed_low, gate_halves, seed_rows, middle_low, lifted_grad),
-                (0, 0, 0, 0, 1, 1, 1),
-                (width, width, width, hidden, width, width, lift_half),
-                (1, 1, 1, 2, 1, 1, 4),
-                5,
-            )
-        )
-        mixed_grad, _ = attention_back(context_grad, saved, scaling, ())
+        planes = (
+            (lifted_grad, normed_two_low, gate_halves, context_low, normed_low, seed_rows, middle_low),
+            (1, 0, 0, 0, 0, 1, 1),
+            (lift_half, width, hidden, width, width, width, width),
+            (4, 1, 2, 1, 1, 1, 1),
+        )
+        mixed_grad, sides = attention_back(context_grad, saved, scaling, (), planes)
+        lift_right, normed_two_left, gate_left, context_left, normed_left, seed_right, middle_right = (
+            sides
+        )
         (mixed_right,) = plane((mixed_grad,), (1,), (mixed_grad.shape[1] // 2,), (4,), 7)
         lift_part = core_blocks(normed_two_left, lift_right)
         down_part = core_blocks(gate_left, seed_right)

time: 501 us -> 418 us (0.83)
  Pallas kernels: 366 us -> 308 us
  other arithmetic: 40.9 us -> 22.9 us
  local copies, waits for them, and re-layouts: 41.6 us -> 34.9 us
    pallas_call x2 -> x1, Pallas kernels: 82.7 us -> 20.6 us  [plane(): pl.pallas_call(functools.partial(plane_kernel, kinds, cuts), out_shape=[j...]
    pallas_call x3 -> x1, Pallas kernels: 42.9 us -> 77.8 us  [back_heads(): pl.pallas_call(functools.partial(back_kernel, kinds, cuts, scaling), out_...]
    pallas_call x1, Pallas kernels: 51.1 us -> 29.1 us  [gather(): pl.pallas_call(functools.partial(gather_kernel, spread, chunks), out_shap...]
    convert_element_type x3 -> x0, other arithmetic: 8.84 us -> none  [the longest x1 4.75 us: by_head_back(): unrotate(query_grad * scaling, cos_all, sin_all).astype(jnp.bfloat16)]
    pallas_call x1, Pallas kernels: 89 us -> 81.7 us  [forward_heads(): pl.pallas_call(functools.partial(forward_kernel, cuts), out_shape=[jax.Sh...]
where the time goes in v4:
time: 418 us; the launch traced here: 412 us
  Pallas kernels  308 us (74%)
  matrix products  38.4 us (9%)
  local copies, waits for them, and re-layouts  34.9 us (8%)
  other arithmetic  22.9 us (5%)
  blocking collectives  5.98 us (1%)
    pallas_call x1, Pallas kernels, finish(): pl.pallas_call(functools.partial(finish_kernel, chunks, len(parts)), out_...  98.8 us
    pallas_call x1, Pallas kernels, forward_heads(): pl.pallas_call(functools.partial(forward_kernel, cuts), out_shape=[jax.Sh...  81.7 us
    pallas_call x1, Pallas kernels, back_heads(): pl.pallas_call(functools.partial(back_kernel, kinds, cuts, scaling), out_...  77.8 us
    pallas_call x1, Pallas kernels, gather(): pl.pallas_call(functools.partial(gather_kernel, spread, chunks), out_shap...  29.1 us
    pallas_call x1, Pallas kernels, plane(): pl.pallas_call(functools.partial(plane_kernel, kinds, cuts), out_shape=[j...  20.6 us
    reshape x1, local copies, waits for them, and re-layouts, gather(): return pl.pallas_call(functools.partial(gather_kernel, spread, chunks), o...  8.65 us
    unnamed x68, local copies, waits for them, and re-layouts  8.49 us

profile of v4, /device:TPU:0, one launch (start us, length us, event | category | flops | bytes accessed | tf_op | source)
XLA Modules:
  0.0 412.0 jit_solution(9959584899804966925)
XLA Ops:
  4.2 6.0 %all_gather.3 = bf16[2,1024]{1,0:T(2,128)(2,1)S(1)} all-gather(bf16[2,256]{1,0:T(2,128)(2,1)S(1)} %pad_maximum_fusion.6), channel_id=1, replica_groups=mesh['ctx'=8,'fsdp'=4] {'fsdp'}, dimensions={1}, use_global_device_ids=true | all-gather | bytes 5120 | tf_op jit(solution)/shard_map/all_gather | solution.py:1297
  11.4 29.1 %shard_map.143 = bf16[4,256,3072]{2,1,0:T(8,128)(2,1)} custom-call(bf16[256,3072]{1,0:T(8,128)(2,1)} %x_ref.1), custom_call_target="tpu_custom_call" | custom-call | tf_op jit(solution)/shard_map/pallas_call | solution.py:260
  40.5 8.6 %copy.31 = bf16[1024,3072]{0,1:T(8,128)(2,1)} copy(bf16[1024,3072]{1,0:T(8,128)(2,1)} %bitcast.144) | data formatting | bytes 12582912 | tf_op jit(solution)/shard_map/reshape | solution.py:271
  49.1 4.5 %fusion.33 = f32[2,64,3,16,64]{1,4,3,2,0:T(8,128)S(1)} fusion(bf16[3,16,64,1024,1]{3,2,1,0,4:T(8,128)(2,1)} %bitcast.155, bf16[2,64,1024]{2,1,0:T(8,128)(2,1)S(1)} %fusion.21), kind=kOutput, calls=%fused_computation.91 | convolution fusion | flops 805306368 | bytes 8126464 | tf_op jit(solution)/shard_map/dot_general | solution.py:1315
  53.8 1.5 copy-done.8
  62.3 81.7 %shard_map.144 = (bf16[32,96,128]{2,1,0:T(8,128)(2,1)S(1)}, f32[1024,128]{1,0:T(8,128)S(1)}, f32[2,1024,1]{2,1,0:T(8,128)S(1)}, bf16[32,32,128]{2,1,0:T(8,128)(2...) custom-call(bf16[32,96,128]{2,1,0:T(8,128)(2,1)S(1)} %maximum_maximum_fusion.re, ...), custom_call_target="tpu_custom_call" | custom-call | tf_op jit(solution)/shard_map/pallas_call | solution.py:577
  146.5 1.5 fusion.49
  148.4 5.9 %fusion.50 = f32[128,5248]{1,0:T(8,128)S(1)} fusion(bf16[128,1024]{1,0:T(8,128)(2,1)S(1)} %bitcast.164, bf16[1024,5248]{1,0:T(8,128)(2,1)} %bitcast.146), kind=kOutput, calls=%fused_computation.125 | convolution fusion | flops 1375731712 | bytes 13697024 | tf_op jit(solution)/shard_map/dot_general | solution.py:1332
  154.3 3.9 fusion.31
  160.6 3.7 multiply_reduce_fusion
  166.2 1.5 convolution_convert_fusion
  171.5 1.9 fusion.29
  176.2 77.8 %shard_map.145 = (bf16[32,96,128]{2,1,0:T(8,128)(2,1)}, bf16[4,128,2688]{2,1,0:T(8,128)(2,1)}, bf16[4,128,512]{2,1,0:T(8,128)(2,1)}, bf16[4,128,1312]{2,1,0:T(8,...) custom-call(bf16[32,32,128]{2,1,0:T(8,128)(2,1)} %pad_maximum_fusion, ...), custom_call_target="tpu_custom_call" | custom-call | tf_op jit(solution)/shard_map/pallas_call | solution.py:760
  254.0 1.5 fusion.42
  258.8 5.1 %fusion.24 = (f32[2,64]{1,0:T(2,128)S(1)}, f32[2,64,1024]{2,1,0:T(8,128)S(1)}) fusion(bf16[2,64,1024]{2,1,0:T(8,128)(2,1)S(1)} %copy-done.6, f32[1024]{0:T(1024)S(1)} %bitcast.181, f32[2,64]{1,0:T(2,128)S(1)} %broadcast_multiply_fusion.3, bf16[2,64,3072]{2,1,0:T(8,128)(2,1)S(1)} %dot_general.63, bf16[1024,3072,1]{1,0,2:T(8,128)(2,1)} %bitcast.145), kind=kOutput, calls=%fused_computation.66 | convolution fusion | flops 805961600 | bytes 7869440 | tf_op jit(solution)/shard_map/tm,wm->tw/dot_general | solution.py:1391
  264.7 2.1 reshape.362.refs_0_
  266.9 20.6 %shard_map.146 = bf16[4,128,1536]{2,1,0:T(8,128)(2,1)} custom-call(bf16[128,3072]{1,0:T(8,128)(2,1)} %reshape.362.refs_0_), custom_call_target="tpu_custom_call" | custom-call | tf_op jit(solution)/shard_map/pallas_call | solution.py:1095
  287.5 3.7 fusion.1
  294.4 3.2 bitcast_convert_fusion
  297.7 98.8 %shard_map.147 = (bf16[2,256,2688]{2,1,0:T(8,128)(2,1)}, bf16[2,656,512]{2,1,0:T(8,128)(2,1)S(1)}, bf16[2,256,512]{2,1,0:T(8,128)(2,1)S(1)}, bf16[2,256,1536]{2,1,0:T(8,128)(2,1)S(1)}, f32[32,8,256]{2,1,0:T(8,128)S(1)}) custom-call(bf16[2,256,2688]{2,1,0:T(8,128)(2,1)} %bitcast.151, bf16[2,656,512]{2,1,0:T(8,128)(2,1)S(1)} %bitcast.142, ...), custom_call_target="tpu_custom_call" | custom-call | tf_op jit(solution)/shard_map/pallas_call | solution.py:1252
  396.6 1.9 maximum_convert_fusion.2
  399.6 2.7 maximum_convert_fusion
  403.6 2.0 maximum_convert_fusion.1
  407.4 4.1 %fusion.10 = bf16[2,64,1024]{2,1,0:T(8,128)(2,1)} fusion(f32[2,64,1024]{2,1,0:T(8,128)S(1)} %get-tuple-element.93, bf16[2,64,2624]{2,1,0:T(8,128)(2,1)S(1)} %bitcast.154, bf16[2624,1024,1]{1,0,2:T(8,128)(2,1)} %bitcast.156), kind=kOutput, calls=%fused_computation.36 | convolution fusion | flops 688128000 | bytes 6832128 | tf_op jit(solution)/shard_map/dot_general | solution.py:1337
  (143 shorter events, 36.8 us)
Async XLA Ops:
  11.4 37.7 %copy-start.22 = (bf16[2,64,1024]{2,1,0:T(8,128)(2,1)}, bf16[2,64,1024]{2,1,0:T(8,128)(2,1)S(1)}, u32[]{:S(2)}) copy-start(bf16[2,64,1024]{2,1,0:T(8,128)(2,1)S(1)} %fusion.21) | copy-start | bytes 786436
  53.6 1.7 copy-start.8
  60.8 1.4 copy-start.4
  144.1 2.3 copy-start.6
  144.2 2.3 copy-start.7
  148.2 6.1 %slice-start.3 = ((s8[5373952]{0:T(1024)(128)(4,1)}), s8[4194304]{0:T(1024)(128)(4,1)S(1)}, s32[]{:S(2)}) async-start(s8[5373952]{0:T(1024)(128)(4,1)} %bitcast.157), calls=%async_computation.3 | async-start | bytes 8388608
  148.4 5.9 %copy-start.16 = (bf16[2,64,1024]{2,1,0:T(8,128)(2,1)}, bf16[2,64,1024]{2,1,0:T(8,128)(2,1)S(1)}, u32[]{:S(2)}) copy-start(bf16[2,64,1024]{2,1,0:T(8,128)(2,1)S(1)} %multiply_convert_fusion.1) | copy-start | bytes 786436
  148.4 5.9 %slice-start.4 = ((s8[5373952]{0:T(1024)(128)(4,1)}), s8[1179648]{0:T(1024)(128)(4,1)S(1)}, s32[]{:S(2)}) async-start(s8[5373952]{0:T(1024)(128)(4,1)} %bitcast.157), calls=%async_computation.4 | async-start | bytes 2359296
  148.4 5.9 %copy-start.20 = (bf16[2,64,1024]{2,1,0:T(8,128)(2,1)S(1)}, bf16[2,64,1024]{2,1,0:T(8,128)(2,1)}, u32[]{:S(2)}) copy-start(bf16[2,64,1024]{2,1,0:T(8,128)(2,1)} %param.15) | copy-start | bytes 786436
  148.4 12.2 %slice-start = ((s8[10747904]{0:T(1024)(128)(4,1)}), s8[4194304]{0:T(1024)(128)(4,1)S(1)}, s32[]{:S(2)}) async-start(s8[10747904]{0:T(1024)(128)(4,1)} %bitcast.147), calls=%async_computation | async-start | bytes 8388608
  154.3 6.2 %slice-start.1 = ((s8[10747904]{0:T(1024)(128)(4,1)}), s8[4194304]{0:T(1024)(128)(4,1)S(1)}, s32[]{:S(2)}) async-start(s8[10747904]{0:T(1024)(128)(4,1)} %bitcast.147), calls=%async_computation.1 | async-start | bytes 8388608
  154.3 6.2 %slice-start.2 = ((s8[10747904]{0:T(1024)(128)(4,1)}), s8[2359296]{0:T(1024)(128)(4,1)S(1)}, s32[]{:S(2)}) async-start(s8[10747904]{0:T(1024)(128)(4,1)} %bitcast.147), calls=%async_computation.2 | async-start | bytes 4718592
  160.5 3.7 copy-start.5
  266.8 20.6 %copy-start.28 = (bf16[4,128,512]{2,1,0:T(8,128)(2,1)S(1)}, bf16[4,128,512]{2,1,0:T(8,128)(2,1)}, u32[]{:S(2)}) copy-start(bf16[4,128,512]{2,1,0:T(8,128)(2,1)} %get-tuple-element.42) | copy-start | bytes 1572868
  287.5 3.7 copy-start.26
  287.5 3.7 copy-start.27
  287.5 4.2 %copy-start.25 = (bf16[4,128,512]{2,1,0:T(8,128)(2,1)S(1)}, bf16[4,128,512]{2,1,0:T(8,128)(2,1)}, u32[]{:S(2)}) copy-start(bf16[4,128,512]{2,1,0:T(8,128)(2,1)} %get-tuple-element.39) | copy-start | bytes 1572868
  292.6 1.8 copy-start.17
  292.6 1.9 copy-start.23
  396.6 2.7 copy-start.18
  403.6 2.7 copy-start.12
  403.6 2.7 copy-start.14
  403.6 2.7 copy-start.21
  405.7 1.7 copy-start.10
  (10 other events, 11.0 us)

commit v5 on v4

--- a/solution.py
+++ b/solution.py
@@ -182,95 +182,6 @@
     )(blocks)
 
 
-def gather_kernel(spread, chunks, x_ref, o_ref, send_sem, recv_sem, own_sem):
-    ctx, place = lax.axis_index("ctx"), lax.axis_index("fsdp")
-    across = lax.rem(place + 2, 4)
-    beside = place + 1 - 2 * lax.rem(place, 2)
-    half = lax.rem(ctx, 2)
-    other_ctx = ctx + 1 - 2 * half
-    sibling, partner, neighbour = (ctx, beside), (ctx, across), (other_ctx, place)
-    width = x_ref.shape[-1] // (2 * chunks if spread else chunks)
-    mine = half * chunks if spread else 0
-    theirs = (1 - half) * chunks
-
-    def columns(index):
-        return pl.ds(pl.multiple_of(index * width, 128), width)
-
-    def send(src, dst, sem, device):
-        return pltpu.make_async_remote_copy(
-            src_ref=src,
-            dst_ref=dst,
-            send_sem=send_sem.at[sem],
-            recv_sem=recv_sem.at[sem],
-            device_id=device,
-            device_id_type=MESH_ID,
-        )
-
-    def piece(index):
-        return o_ref.at[across, :, columns(index)]
-
-    barrier = pltpu.get_barrier_semaphore()
-    partners = (sibling, partner, neighbour) if spread else (sibling, partner)
-    for device in partners:
-        pl.semaphore_signal(barrier, inc=1, device_id=device, device_id_type=MESH_ID)
-    pl.semaphore_wait(barrier, len(partners))
-    crossing = [
-        send(
-            x_ref.at[:, columns(mine + c)],
-            o_ref.at[place, :, columns(mine + c)],
-            c,
-            partner,
-        )
-        for c in range(chunks)
-    ]
-    for copy in crossing:
-        copy.start()
-    started = list(crossing)
-    whole = send(x_ref, o_ref.at[place], chunks, sibling)
-    whole.start()
-    own = pltpu.make_async_copy(x_ref, o_ref.at[place], own_sem)
-    own.start()
-    turned = []
-    for c in range(chunks):
-        crossing[c].wait_recv()
-        if spread:
-            turn = send(piece(mine + c), piece(mine + c), chunks + 1 + c, neighbour)
-            turn.start()
-            turned.append(turn)
-        hand = send(piece(mine + c), piece(mine + c), 2 * chunks + 1 + c, sibling)
-        hand.start()
-        started.append(hand)
-    handed = started[chunks:]
-    for c in range(len(turned)):
-        turned[c].wait_recv()
-        hand = send(piece(theirs + c), piece(theirs + c), 3 * chunks + 1 + c, sibling)
-        hand.start()
-        handed.append(hand)
-    whole.wait_recv()
-    own.wait()
-    for hand in handed:
-        hand.wait_recv()
-    for copy in crossing + turned + handed + [whole]:
-        copy.wait_send()
-
-
-def gather(block, spread, chunks, collective_id):
-    rows, width = block.shape
-    count = 4 * chunks + 1
-    return pl.pallas_call(
-        functools.partial(gather_kernel, spread, chunks),
-        out_shape=jax.ShapeDtypeStruct((4, rows, width), block.dtype),
-        in_specs=[pl.BlockSpec(memory_space=pltpu.VMEM)],
-        out_specs=pl.BlockSpec(memory_space=pl.ANY),
-        scratch_shapes=[
-            pltpu.SemaphoreType.DMA((count,)),
-            pltpu.SemaphoreType.DMA((count,)),
-            pltpu.SemaphoreType.DMA,
-        ],
-        compiler_params=pltpu.CompilerParams(collective_id=collective_id, has_side_effects=True),
-    )(block).reshape(4 * rows, width)
-
-
 def pack(blocks):
     half = blocks.shape[-2] // 2
     return jnp.concatenate([blocks[..., :half, :], blocks[..., half:, :]], axis=-1)
@@ -281,7 +192,8 @@
     return jnp.concatenate([blocks[..., :half], blocks[..., half:]], axis=-2)
 
 
-CUTS = ((False, 1), (True, 4), (False, 4))
+AHEAD = 3
+CUTS = ((False, 6), (False, 1), (True, 4), (False, 4))
 CONTRACT_LAST = (((1,), (1,)), ((), ()))
 CONTRACT_FIRST = (((0,), (0,)), ((), ()))
 
@@ -406,21 +318,24 @@
     return ref.at[:, pl.ds(start, size)]
 
 
-def forward_kernel(cuts, *refs):
+def forward_kernel(cuts, scaling, *refs):
     count = len(cuts)
-    sent, shards = refs[0], refs[1 : 1 + count]
-    got, context, log_ref, back = refs[1 + count : 5 + count]
-    fulls = refs[5 + count : 5 + 2 * count]
-    (keys, values, packed, head_send, head_recv, back_send, back_recv, own_sem) = refs[
-        5 + 2 * count : 13 + 2 * count
+    x_ref, cos_ref, sin_ref, gain_ref = refs[:4]
+    shards = refs[4 : 4 + count]
+    normed_ref, gains, got, context, log_ref, back = refs[4 + count : 10 + count]
+    fulls = refs[10 + count : 10 + 2 * count]
+    (sent, keys, values, packed, head_send, head_recv, back_send, back_recv, own_sem) = refs[
+        10 + 2 * count : 19 + 2 * count
     ]
-    w_send, w_recv = refs[13 + 2 * count :]
+    w_send, w_recv = refs[19 + 2 * count :]
+    targets, proj = fulls, fulls[0]
     z, y, x, core = mesh_place()
     place = 2 * x + core
     me = 4 * (2 * z + y) + place
     across = lax.rem(place + 2, 4)
     other = whole_mesh(me)
     sibling, partner = device_at(z, y, x, 1 - core), device_at(z, y, 1 - x, core)
+    corner = device_at(z, y, 1 - x, 1 - core)
     neighbour = device_at(z, 1 - y, x, core)
     greet_all(other)
 
@@ -446,55 +361,121 @@
             device_id_type=MESH_ID,
         )
 
-    serial = iter(range(w_send.shape[0]))
-
-    def send(src, dst, device):
-        sem = next(serial)
-        copy = pltpu.make_async_remote_copy(
-            src_ref=src,
-            dst_ref=dst,
-            send_sem=w_send.at[sem],
-            recv_sem=w_recv.at[sem],
-            device_id=device,
-            device_id_type=MESH_ID,
-        )
+    send = sender(w_send, w_recv)
+    crossing, handed, turned = [], [], []
+
+    todo = [(i, c) for i in range(count) for c in range(cuts[i][1])]
+    first = cuts[0][1]
+
+    def cross(pieces=1):
+        for i, c in todo[len(crossing) :][:pieces]:
+            src = weight_piece(shards[i], cuts[i][0], y, c, cuts[i][1])
+            dst = weight_piece(targets[i].at[place], cuts[i][0], y, c, cuts[i][1])
+            crossing.append((i, c, send(src, dst, partner)))
+
+    def keep(i):
+        copy = pltpu.make_async_copy(shards[i], targets[i].at[place], own_sem.at[i])
         copy.start()
         return copy
+
+    def turn(entry):
+        i, c, copy = entry
+        copy.wait_recv()
+        here = weight_piece(targets[i].at[across], cuts[i][0], y, c, cuts[i][1])
+        turned.append((i, c, send(here, here, neighbour)))
+        cross()
+        handed.append(send(here, here, sibling))
+
+    def hand(entry):
+        i, c, copy = entry
+        copy.wait_recv()
+        here = weight_piece(targets[i].at[across], cuts[i][0], 1 - y, c, cuts[i][1])
+        handed.append(send(here, here, sibling))
+
+    gain_moves = [
+        send(gain_ref, gains.at[place], device) for device in (sibling, partner, corner)
+    ]
+    cross(AHEAD)
+    handed.append(send(shards[0], proj.at[place], sibling))
+    kept = pltpu.make_async_copy(gain_ref, gains.at[place], own_sem.at[count])
+    kept.start()
+    owns = [keep(0)]
+    states = x_ref[...].astype(jnp.float32)
+    centred = states - jnp.mean(states, axis=-1, keepdims=True)
+    spread = jnp.mean(centred * centred, axis=-1, keepdims=True)
+    centred = centred * lax.rsqrt(spread + eps)
+    kept.wait()
+    for copy in gain_moves:
+        copy.wait()
+    for f in range(4):
+        part = centred[:, f * 256 : (f + 1) * 256] * gains[f, 0:1, :].astype(jnp.float32)
+        normed_ref[:, f * 256 : (f + 1) * 256] = part.astype(jnp.bfloat16)
+    for c in range(first):
+        turn(crossing[c])
+    for c in range(first):
+        hand(turned[c])
+    owns[0].wait()
+    for copy in handed[: 1 + 2 * first]:
+        copy.wait_recv()
+    cos = jnp.concatenate([cos_ref[...]] * 2, axis=1)
+    sin = jnp.concatenate([sin_ref[...]] * 2, axis=1)
+
+    def turn_heads(value):
+        lane = lax.rem(lax.broadcasted_iota(jnp.int32, value.shape, 1), 64)
+        turned_lanes = jnp.where(lane < 32, -pltpu.roll(value, 224, 1), pltpu.roll(value, 32, 1))
+        return value * cos + turned_lanes * sin
+
+    @pl.loop(0, 4)
+    def _(quad):
+        def product(start):
+            columns = pl.ds(pl.multiple_of(start + quad * 256, 128), 256)
+            total = jnp.dot(
+                normed_ref[:, :256], proj[0, :, columns], preferred_element_type=jnp.float32
+            )
+            for f in range(1, 4):
+                total += jnp.dot(
+                    normed_ref[:, f * 256 : (f + 1) * 256],
+                    proj[f, :, columns],
+                    preferred_element_type=jnp.float32,
+                )
+            return total
+
+        queries = turn_heads(product(0)).astype(jnp.bfloat16).astype(jnp.float32) * scaling
+        key_rows = turn_heads(product(1024))
+        value_rows = product(2048)
+        for pair in range(2):
+            lanes = slice(pair * 128, (pair + 1) * 128)
+            q, k, v = queries[:, lanes], key_rows[:, lanes], value_rows[:, lanes]
+            swapped_q, swapped_k = pltpu.roll(q, 64, 1), pltpu.roll(k, 64, 1)
+            even = jnp.where(low_lanes(q), q, swapped_k).astype(jnp.bfloat16)
+            odd = jnp.where(low_lanes(q), swapped_q, k).astype(jnp.bfloat16)
+            swapped_v = pltpu.roll(v, 64, 1)
+            for seq in range(2):
+                head = seq * 16 + quad * 4 + pair * 2
+                low, mid, high = seq * 64, seq * 64 + 32, seq * 64 + 64
+                sent[head, 0:64] = even[low:high]
+                sent[head + 1, 0:64] = odd[low:high]
+                mask = low_lanes(v[low:mid])
+                sent[head, 64:96] = jnp.where(mask, v[low:mid], swapped_v[mid:high]).astype(
+                    jnp.bfloat16
+                )
+                sent[head + 1, 64:96] = jnp.where(mask, swapped_v[low:mid], v[mid:high]).astype(
+                    jnp.bfloat16
+                )
 
     @pl.loop(1, 32)
     def _(step):
         head_copy(step).start()
 
-    own = [pltpu.make_async_copy(sent.at[me], got.at[me], own_sem.at[count])]
-    own[0].start()
-    crossing, handed, turned = [], [], []
-    for i, (by_rows, pieces) in enumerate(cuts):
-        for c in range(pieces):
-            src = weight_piece(shards[i], by_rows, y, c, pieces)
-            dst = weight_piece(fulls[i].at[place], by_rows, y, c, pieces)
-            crossing.append((i, c, send(src, dst, partner)))
-    for i in range(count):
-        copy = pltpu.make_async_copy(shards[i], fulls[i].at[place], own_sem.at[i])
-        copy.start()
-        own.append(copy)
-        handed.append(send(shards[i], fulls[i].at[place], sibling))
-
-    def turn(entry):
-        i, c, copy = entry
-        copy.wait_recv()
-        here = weight_piece(fulls[i].at[across], cuts[i][0], y, c, cuts[i][1])
-        turned.append((i, c, send(here, here, neighbour)))
-        handed.append(send(here, here, sibling))
-
-    def hand(entry):
-        i, c, copy = entry
-        copy.wait_recv()
-        here = weight_piece(fulls[i].at[across], cuts[i][0], 1 - y, c, cuts[i][1])
-        handed.append(send(here, here, sibling))
-
-    turn(crossing[0])
-    turn(crossing[1])
-    own[0].wait()
+    own_head = pltpu.make_async_copy(sent.at[me], got.at[me], own_sem.at[count + 1])
+    own_head.start()
+    for i in range(1, count):
+        owns.append(keep(i))
+        handed.append(send(shards[i], targets[i].at[place], sibling))
+    for c in range(first, first + 3):
+        turn(crossing[c])
+    hand(turned[first])
+    own_head.wait()
 
     @pl.loop(1, 32)
     def _(step):
@@ -534,24 +515,24 @@
             def _():
                 back_copy(to).start()
 
-    turn(crossing[2])
-    hand(turned[0])
+    turn(crossing[first + 3])
+    hand(turned[first + 1])
 
     @pl.loop(0, 4)
     def _(b):
         attend_block(b)
 
-    turn(crossing[3])
-    hand(turned[1])
+    turn(crossing[first + 4])
+    hand(turned[first + 2])
 
     @pl.loop(4, 8)
     def _(b):
         attend_block(b)
 
-    mine = pltpu.make_async_copy(packed.at[me], back.at[me], own_sem.at[count + 1])
+    mine = pltpu.make_async_copy(packed.at[me], back.at[me], own_sem.at[count + 2])
     mine.start()
-    own.append(mine)
-    for index in range(4, len(crossing)):
+    owns.append(mine)
+    for index in range(first + 5, len(todo)):
         turn(crossing[index])
         hand(turned[index - 2])
     hand(turned[-2])
@@ -561,45 +542,51 @@
     def _(step):
         back_copy(lax.rem(me + step, 32)).wait()
 
+    for copy in handed[1 + 2 * first :]:
+        copy.wait_recv()
     for copy in handed:
-        copy.wait()
+        copy.wait_send()
     for _, _, copy in crossing + turned:
         copy.wait_send()
-    for copy in own[1:]:
+    for copy in owns[1:]:
         copy.wait()
 
 
-def forward_heads(sent, shards, cuts, collective_id):
+def forward_heads(rows, cos_table, sin_table, gain, shards, cuts, scaling, collective_id):
     in_vmem, anywhere = pl.BlockSpec(memory_space=pltpu.VMEM), pl.BlockSpec(memory_space=pl.ANY)
-    copies = len(shards) + sum(4 * pieces for _, pieces in cuts)
+    copies = 3 + len(shards) + sum(4 * pieces for _, pieces in cuts)
     low, full = jnp.bfloat16, jnp.float32
     sems = [pltpu.SemaphoreType.DMA((32,))] * 4
+    proj, *rest = shards
     return pl.pallas_call(
-        functools.partial(forward_kernel, cuts),
+        functools.partial(forward_kernel, cuts, scaling),
         out_shape=[
+            jax.ShapeDtypeStruct(rows.shape, low),
+            jax.ShapeDtypeStruct((4, *gain.shape), low),
             jax.ShapeDtypeStruct((32, 96, 128), low),
             jax.ShapeDtypeStruct((1024, 128), full),
             jax.ShapeDtypeStruct((2, 1024, 1), full),
             jax.ShapeDtypeStruct((32, 32, 128), low),
         ]
         + [jax.ShapeDtypeStruct((4, *shard.shape), low) for shard in shards],
-        in_specs=[in_vmem] * (1 + len(shards)),
-        out_specs=[in_vmem] * 4 + [anywhere] * len(shards),
+        in_specs=[in_vmem] * (4 + len(shards)),
+        out_specs=[in_vmem] * 7 + [anywhere] * len(rest),
         scratch_shapes=[
+            pltpu.VMEM((32, 96, 128), low),
             pltpu.VMEM((2048, 128), low),
             pltpu.VMEM((1024, 128), low),
             pltpu.VMEM((32, 32, 128), low),
             *sems,
-            pltpu.SemaphoreType.DMA((len(shards) + 2,)),
+            pltpu.SemaphoreType.DMA((len(shards) + 3,)),
             pltpu.SemaphoreType.DMA((copies,)),
             pltpu.SemaphoreType.DMA((copies,)),
         ],
         compiler_params=pltpu.CompilerParams(
             collective_id=collective_id,
             has_side_effects=True,
-            vmem_limit_bytes=48 * 1024 * 1024,
+            vmem_limit_bytes=56 * 1024 * 1024,
         ),
-    )(sent, *shards)
+    )(rows, cos_table, sin_table, gain, *shards)
 
 
 def back_kernel(kinds, cuts, scaling, *refs):
@@ -786,7 +773,7 @@
     return result, [out.reshape(4 * rows, width) for out, width in zip(outs, widths)]
 
 
-def by_head_forward(mixed_rows, cos_table, sin_table, scaling, shards=()):
+def by_head_forward(mixed_rows, cos_table, sin_table, scaling):
     seq_count, row_count, _, head_count, head_size = mixed_rows.shape
     ctx_count, fsdp_count = lax.axis_size("ctx"), lax.axis_size("fsdp")
     count = ctx_count * fsdp_count
@@ -801,15 +788,6 @@
         ],
         axis=1,
     )
-    if shards:
-        got, context, log_total, back, *fulls = forward_heads(sent, shards, CUTS, 1)
-        context_low = (
-            unpack(back)
-            .reshape(seq_count, head_count, row_count, head_size)
-            .transpose(0, 2, 1, 3)
-            .reshape(seq_count * row_count, head_count * head_size)
-        )
-        return context_low, (got, context, log_total), fulls
     got = exchange(sent, ctx_count, fsdp_count, 1)
     flat = lambda rows: rows.reshape(count * row_count, head_size)
     queries = flat(got[:, :row_count, :head_size])
@@ -828,7 +806,7 @@
         .transpose(0, 2, 1, 3)
         .reshape(seq_count * row_count, head_count * head_size)
     )
-    return context_low, (queries, key_rows, value_rows, context, log_total), ()
+    return context_low, (queries, key_rows, value_rows, context, log_total)
 
 
 def by_head_back(context_grad, saved, scaling, after, planes=()):
@@ -884,7 +862,7 @@
     ), after
 
 
-def by_block_forward(mixed_rows, cos_table, sin_table, scaling, shards=()):
+def by_block_forward(mixed_rows, cos_table, sin_table, scaling):
     seq_count, row_count, _, head_count, head_size = mixed_rows.shape
     width = head_count * head_size
     queries = rotate(mixed_rows[:, :, 0], cos_table, sin_table).astype(jnp.bfloat16)
@@ -912,7 +890,7 @@
     log_total = running_max + jnp.log(denominator)
     context_low = context.reshape(seq_count * row_count, width).astype(jnp.bfloat16)
     saved = queries, key_block, value_block, context, log_total, cos_table, sin_table
-    return context_low, saved, ()
+    return context_low, saved
 
 
 def by_block_back(context_grad, saved, scaling, after, planes=()):
@@ -1294,35 +1272,54 @@
     cos_table, sin_table = angles(start_row + jnp.arange(row_count, dtype=jnp.int32), head_size)
     tokens = seq_count * row_count
     gain_width = own_rows = attn_gain.shape[0]
-    gains = lax.all_gather(jnp.stack([attn_gain, mlp_gain]), "fsdp", axis=1, tiled=True).astype(
-        jnp.float32
-    )
-    gain_one, gain_two = gains[0], gains[1]
     ctx_count = lax.axis_size("ctx")
     small = one_head_each and fsdp_count == 4 and ctx_count == 8
+    states = inputs.astype(jnp.float32)
+    attention, attention_back = (
+        (by_head_forward, by_head_back) if one_head_each else (by_block_forward, by_block_back)
+    )
     if small:
-        proj_full = gather(attn_proj, True, 6, 6)
-        shards = attn_out, mlp_in, mlp_out
+        gain_rows = jnp.concatenate(
+            [attn_gain[None], mlp_gain[None], jnp.zeros((14, gain_width), attn_gain.dtype)], axis=0
+        )
+        normed_low, gains, got, context, log_total, back, *fulls = forward_heads(
+            inputs.reshape(tokens, model_width),
+            *(
+                jnp.tile(table.reshape(row_count, head_size), (seq_count, 2))
+                for table in (cos_table, sin_table)
+            ),
+            gain_rows,
+            (attn_proj, attn_out, mlp_in, mlp_out),
+            CUTS,
+            scaling,
+            1,
+        )
+        saved = got, context, log_total
+        context_low = (
+            unpack(back)
+            .reshape(seq_count, head_count, row_count, head_size)
+            .transpose(0, 2, 1, 3)
+            .reshape(tokens, head_count * head_size)
+        )
+        proj_full, out_full, lift_full, down_full = (
+            full.reshape(4 * full.shape[1], full.shape[2]) for full in fulls
+        )
+        gain_one = gains[:, 0, :].reshape(model_width).astype(jnp.float32)
+        gain_two = gains[:, 1, :].reshape(model_width).astype(jnp.float32)
+        _, norm_back_one = jax.vjp(layer_norm, states, gain_one)
     else:
-        shards = ()
+        gains = lax.all_gather(jnp.stack([attn_gain, mlp_gain]), "fsdp", axis=1, tiled=True)
+        gain_one, gain_two = gains.astype(jnp.float32)
         proj_full, out_full, lift_full, down_full = (
             lax.all_gather(rows, "fsdp", axis=0, tiled=True)
             for rows in (attn_proj, attn_out, mlp_in, mlp_out)
         )
-    states = inputs.astype(jnp.float32)
-    normed, norm_back_one = jax.vjp(layer_norm, states, gain_one)
-    normed_low = normed.astype(jnp.bfloat16).reshape(tokens, model_width)
-    mixed_rows = jnp.dot(normed_low, proj_full, preferred_element_type=jnp.float32).reshape(
-        seq_count, row_count, 3, head_count, head_size
-    )
-    attention, attention_back = (
-        (by_head_forward, by_head_back) if one_head_each else (by_block_forward, by_block_back)
-    )
-    context_low, saved, fulls = attention(mixed_rows, cos_table, sin_table, scaling, shards)
-    if small:
-        out_full, lift_full, down_full = (
-            full.reshape(4 * full.shape[1], full.shape[2]) for full in fulls
-        )
+        normed, norm_back_one = jax.vjp(layer_norm, states, gain_one)
+        normed_low = normed.astype(jnp.bfloat16).reshape(tokens, model_width)
+        mixed_rows = jnp.dot(normed_low, proj_full, preferred_element_type=jnp.float32).reshape(
+            seq_count, row_count, 3, head_count, head_size
+        )
+        context_low, saved = attention(mixed_rows, cos_table, sin_table, scaling)
     branch = jnp.dot(context_low, out_full, preferred_element_type=jnp.float32).reshape(
         seq_count, row_count, model_width
     )

time: 418 us -> 383 us (0.916)
  local copies, waits for them, and re-layouts: 34.9 us -> 23.5 us
  blocking collectives: 5.98 us -> 0 us
  other arithmetic: 22.9 us -> 17.4 us
  Pallas kernels: 308 us -> 303 us
  matrix products: 38.4 us -> 33.9 us
    reshape x3 -> x2, local copies, waits for them, and re-layouts: 10 us -> 1.4 us  [on_device(): context_low = unpack(back).reshape(seq_count, head_count, row_count, head...]
    all_gather x1 -> x0, blocking collectives: 5.98 us -> none  [on_device(): lax.all_gather(jnp.stack([attn_gain, mlp_gain]), 'fsdp', axis=1, tiled=True)]
    pallas_call x2 -> x1, Pallas kernels: 111 us -> 106 us  [forward_heads(): pl.pallas_call(functools.partial(forward_kernel, cuts, scaling), out_shap...]
    dot_general x1 -> x0, matrix products: 4.49 us -> none  [on_device(): jnp.dot(normed_low, proj_full, preferred_element_type=jnp.float32)]
    unnamed x68 -> x54, local copies, waits for them, and re-layouts: 8.49 us -> 5.15 us
where the time goes in v5:
time: 383 us; the launch traced here: 379 us
  Pallas kernels  303 us (79%)
  matrix products  33.9 us (9%)
  local copies, waits for them, and re-layouts  23.5 us (6%)
  other arithmetic  17.4 us (5%)
    pallas_call x1, Pallas kernels, forward_heads(): pl.pallas_call(functools.partial(forward_kernel, cuts, scaling), out_shap...  106 us
    pallas_call x1, Pallas kernels, finish(): pl.pallas_call(functools.partial(finish_kernel, chunks, len(parts)), out_...  98 us
    pallas_call x1, Pallas kernels, back_heads(): pl.pallas_call(functools.partial(back_kernel, kinds, cuts, scaling), out_...  77.8 us
    pallas_call x1, Pallas kernels, plane(): pl.pallas_call(functools.partial(plane_kernel, kinds, cuts), out_shape=[j...  21.4 us
    dot_general x4, matrix products, weight_grad(): jnp.einsum('tw,tf->wf', left, right, preferred_element_type=jnp.float32)  8.24 us
    convert_element_type x4, other arithmetic, joined_halves(): jnp.concatenate([out[0], out[1][:, skip:]], axis=1).astype(jnp.float32)  7.75 us

profile of v5, /device:TPU:0, one launch (start us, length us, event | category | flops | bytes accessed | tf_op | source)
XLA Modules:
  0.0 379.4 jit_solution(7014636622694254614)
XLA Ops:
  4.6 105.7 %shard_map.143 = (bf16[128,1024]{1,0:T(8,128)(2,1)}, bf16[4,16,256]{2,1,0:T(8,128)(2,1)}, bf16[32,96,128]{2,1,0:T(8,128)(2,1)}, f32[1024,128]{1,0:T(8,128)}, f32...) custom-call(bf16[128,1024]{1,0:T(8,128)(2,1)} %bitcast.119, ...), custom_call_target="tpu_custom_call" | custom-call | tf_op jit(solution)/shard_map/pallas_call | solution.py:561
  110.4 1.2 fusion.33
  113.2 1.5 fusion.35
  116.0 5.9 %fusion.36 = f32[128,5248]{1,0:T(8,128)S(1)} fusion(bf16[128,1024]{1,0:T(8,128)(2,1)S(1)} %bitcast.131, bf16[1024,5248]{1,0:T(8,128)(2,1)} %bitcast.112), kind=kOutput, calls=%fused_computation.105 | convolution fusion | flops 1375731712 | bytes 13697024 | tf_op jit(solution)/shard_map/dot_general | solution.py:1329
  121.9 3.9 %fusion.21 = (f32[128,2624]{1,0:T(8,128)S(1)}, f32[128,2624]{1,0:T(8,128)S(1)}, f32[128,2624]{1,0:T(8,128)S(1)}) fusion(f32[128,5248]{1,0:T(8,128)S(1)} %fusion.36, bf16[2624,1024]{1,0:T(8,128)(2,1)S(1)} %bitcast.126, bf16[128,1024]{1,0:T(8,128)(2,1)S(1)} %bitcast.136), kind=kOutput, calls=%fused_computation.68 | convolution fusion | flops 709697536 | bytes 11010048 | tf_op jit(solution)/shard_map/td,fd->tf/dot_general | solution.py:1339
  128.2 3.7 multiply_reduce_fusion
  133.7 1.5 convolution_convert_fusion
  135.3 1.3 reshape.344
  139.1 1.9 fusion.19
  141.1 1.3 copy.29.refs_4_
  142.5 1.3 copy.30.refs_5_
  143.8 77.8 %shard_map.144 = (bf16[32,96,128]{2,1,0:T(8,128)(2,1)}, bf16[4,128,2688]{2,1,0:T(8,128)(2,1)}, bf16[4,128,512]{2,1,0:T(8,128)(2,1)}, bf16[4,128,1312]{2,1,0:T(8,...) custom-call(bf16[32,32,128]{2,1,0:T(8,128)(2,1)} %pad_maximum_fusion, ...), custom_call_target="tpu_custom_call" | custom-call | tf_op jit(solution)/shard_map/pallas_call | solution.py:747
  221.6 1.5 fusion.30
  225.2 1.1 dot_general.53
  226.3 5.1 %fusion.15 = (f32[2,64]{1,0:T(2,128)S(1)}, f32[2,64]{1,0:T(2,128)S(1)}, f32[2,64,1024]{2,1,0:T(8,128)S(1)}) fusion(bf16[2,64,1024]{2,1,0:T(8,128)(2,1)S(1)} %copy-done.1, f32[2,64]{1,0:T(2,128)S(1)} %get-tuple-element.100, f32[1024]{0:T(1024)S(1)} %bitcast.143, bf16[2,64,3072]{2,1,0:T(8,128)(2,1)S(1)} %dot_general.53, bf16[1024,3072,1]{1,0,2:T(8,128)(2,1)} %bitcast.117), kind=kOutput, calls=%fused_computation.51 | convolution fusion | flops 806223616 | bytes 7869952 | tf_op jit(solution)/shard_map/tm,wm->tw/dot_general | solution.py:1388
  232.2 2.1 reshape.357.refs_0_
  234.3 21.4 %shard_map.145 = bf16[4,128,1536]{2,1,0:T(8,128)(2,1)} custom-call(bf16[128,3072]{1,0:T(8,128)(2,1)} %reshape.357.refs_0_), custom_call_target="tpu_custom_call" | custom-call | tf_op jit(solution)/shard_map/pallas_call | solution.py:1073
  255.8 3.7 fusion.1
  262.7 3.2 bitcast_convert_fusion
  265.9 98.0 %shard_map.146 = (bf16[2,256,2688]{2,1,0:T(8,128)(2,1)}, bf16[2,656,512]{2,1,0:T(8,128)(2,1)S(1)}, bf16[2,256,512]{2,1,0:T(8,128)(2,1)S(1)}, bf16[2,256,1536]{2,1,0:T(8,128)(2,1)S(1)}, f32[32,8,256]{2,1,0:T(8,128)S(1)}) custom-call(bf16[2,256,2688]{2,1,0:T(8,128)(2,1)} %bitcast.118, bf16[2,656,512]{2,1,0:T(8,128)(2,1)S(1)} %bitcast.110, ...), custom_call_target="tpu_custom_call" | custom-call | tf_op jit(solution)/shard_map/pallas_call | solution.py:1230
  364.0 1.9 maximum_convert_fusion.2
  367.1 2.7 maximum_convert_fusion
  371.1 2.0 maximum_convert_fusion.1
  374.8 4.1 %fusion.10 = bf16[2,64,1024]{2,1,0:T(8,128)(2,1)} fusion(f32[2,64,1024]{2,1,0:T(8,128)S(1)} %get-tuple-element.95, bf16[2,64,2624]{2,1,0:T(8,128)(2,1)S(1)} %bitcast.122, bf16[2624,1024,1]{1,0,2:T(8,128)(2,1)} %bitcast.123), kind=kOutput, calls=%fused_computation.36 | convolution fusion | flops 688128000 | bytes 6832128 | tf_op jit(solution)/shard_map/dot_general | solution.py:1334
  (117 shorter events, 23.9 us)
Async XLA Ops:
  111.6 1.6 copy-start.1
  111.6 1.7 copy-start.2
  115.8 6.1 %slice-start.3 = ((s8[5373952]{0:T(1024)(128)(4,1)}), s8[4194304]{0:T(1024)(128)(4,1)S(1)}, s32[]{:S(2)}) async-start(s8[5373952]{0:T(1024)(128)(4,1)} %bitcast.124), calls=%async_computation.3 | async-start | bytes 8388608
  115.9 5.9 %copy-start.10 = (bf16[2,64,1024]{2,1,0:T(8,128)(2,1)}, bf16[2,64,1024]{2,1,0:T(8,128)(2,1)S(1)}, u32[]{:S(2)}) copy-start(bf16[2,64,1024]{2,1,0:T(8,128)(2,1)S(1)} %multiply_convert_fusion.1) | copy-start | bytes 786436
  115.9 5.9 %slice-start.4 = ((s8[5373952]{0:T(1024)(128)(4,1)}), s8[1179648]{0:T(1024)(128)(4,1)S(1)}, s32[]{:S(2)}) async-start(s8[5373952]{0:T(1024)(128)(4,1)} %bitcast.124), calls=%async_computation.4 | async-start | bytes 2359296
  115.9 5.9 %copy-start.14 = (bf16[2,64,1024]{2,1,0:T(8,128)(2,1)S(1)}, bf16[2,64,1024]{2,1,0:T(8,128)(2,1)}, u32[]{:S(2)}) copy-start(bf16[2,64,1024]{2,1,0:T(8,128)(2,1)} %param.15) | copy-start | bytes 786436
  115.9 12.2 %slice-start = ((s8[10747904]{0:T(1024)(128)(4,1)}), s8[4194304]{0:T(1024)(128)(4,1)S(1)}, s32[]{:S(2)}) async-start(s8[10747904]{0:T(1024)(128)(4,1)} %bitcast.113), calls=%async_computation | async-start | bytes 8388608
  121.9 6.2 %slice-start.1 = ((s8[10747904]{0:T(1024)(128)(4,1)}), s8[4194304]{0:T(1024)(128)(4,1)S(1)}, s32[]{:S(2)}) async-start(s8[10747904]{0:T(1024)(128)(4,1)} %bitcast.113), calls=%async_computation.1 | async-start | bytes 8388608
  121.9 6.2 %slice-start.2 = ((s8[10747904]{0:T(1024)(128)(4,1)}), s8[2359296]{0:T(1024)(128)(4,1)S(1)}, s32[]{:S(2)}) async-start(s8[10747904]{0:T(1024)(128)(4,1)} %bitcast.113), calls=%async_computation.2 | async-start | bytes 4718592
  126.7 1.1 copy-start.3
  128.1 3.7 copy-start
  223.0 1.1 copy-start.9
  234.3 21.5 %copy-start.21 = (bf16[4,128,512]{2,1,0:T(8,128)(2,1)S(1)}, bf16[4,128,512]{2,1,0:T(8,128)(2,1)}, u32[]{:S(2)}) copy-start(bf16[4,128,512]{2,1,0:T(8,128)(2,1)} %get-tuple-element.48) | copy-start | bytes 1572868
  255.8 3.7 copy-start.19
  255.8 3.7 copy-start.20
  255.8 4.2 %copy-start.18 = (bf16[4,128,512]{2,1,0:T(8,128)(2,1)S(1)}, bf16[4,128,512]{2,1,0:T(8,128)(2,1)}, u32[]{:S(2)}) copy-start(bf16[4,128,512]{2,1,0:T(8,128)(2,1)} %get-tuple-element.45) | copy-start | bytes 1572868
  259.5 1.4 copy-start.17
  260.8 1.8 copy-start.11
  260.8 1.9 copy-start.16
  364.0 2.7 copy-start.12
  371.0 2.7 copy-start.6
  371.1 2.7 copy-start.8
  371.1 2.7 copy-start.15
  373.1 1.7 copy-start.4
  (3 other events, 2.3 us)

commit v6 on v5

--- a/solution.py
+++ b/solution.py
@@ -193,6 +193,7 @@
 
 
 AHEAD = 3
+LAG = 6
 CUTS = ((False, 6), (False, 1), (True, 4), (False, 4))
 CONTRACT_LAST = (((1,), (1,)), ((), ()))
 CONTRACT_FIRST = (((0,), (0,)), ((), ()))
@@ -1053,44 +1054,15 @@
     return start, turn, end
 
 
-def plane_kernel(kinds, cuts, *refs):
-    count = len(kinds)
-    z, y, x, core = mesh_place()
-    greet(
-        pltpu.get_barrier_semaphore(),
-        (device_at(z, y, 1 - x, core), device_at(z, 1 - y, x, core)),
-    )
-    start, turn, end = plane_moves(
-        kinds, cuts, refs[:count], refs[count : 2 * count], *refs[2 * count :]
-    )
-    start()
-    end()
-
-
-def plane(parts, kinds, widths, cuts, collective_id):
-    rows = parts[0].shape[-2]
-    sems = 3 * sum(cuts)
-    outs = pl.pallas_call(
-        functools.partial(plane_kernel, kinds, cuts),
-        out_shape=[jax.ShapeDtypeStruct((4, rows, width), jnp.bfloat16) for width in widths],
-        in_specs=[pl.BlockSpec(memory_space=pltpu.VMEM)] * len(parts),
-        out_specs=[pl.BlockSpec(memory_space=pl.ANY)] * len(parts),
-        scratch_shapes=[
-            pltpu.SemaphoreType.DMA((sems,)),
-            pltpu.SemaphoreType.DMA((sems,)),
-            pltpu.SemaphoreType.DMA((len(parts),)),
-        ],
-        compiler_params=pltpu.CompilerParams(collective_id=collective_id, has_side_effects=True),
-    )(*parts)
-    return [out.reshape(4 * rows, width) for out, width in zip(outs, widths)]
-
-
 def finish_kernel(chunks, count, *refs):
-    parts, gains = refs[:count], refs[count]
-    outs, gain_got = refs[count + 1 : 2 * count + 1], refs[2 * count + 1]
-    scratch = refs[2 * count + 2 :]
+    mixed, left, gains = refs[count - 1 : count + 2]
+    outs, gain_got = refs[count + 2 : 2 * count + 2], refs[2 * count + 2]
+    scratch = refs[2 * count + 3 :]
     core_got, z_got, mid_got, z_sent = (scratch[i * count : (i + 1) * count] for i in range(4))
-    send_sem, recv_sem, gain_send, gain_recv, own_sem = scratch[4 * count :]
+    send_sem, recv_sem, gain_send, gain_recv, own_sem, last, right = scratch[
+        4 * count : 4 * count + 7
+    ]
+    parts = (*refs[: count - 1], last)
     z, y, x, core = mesh_place()
     me = lax.axis_index("ctx") * 4 + lax.axis_index("fsdp")
     total = len(chunks)
@@ -1160,8 +1132,12 @@
     def wide(value):
         return value.astype(jnp.float32)
 
-    for k in range(total):
+    outer = (z == 0) | (z == 3)
+    late = [k for k in range(total) if chunks[k][0] == count - 1][0]
+    start, turn, end = plane_moves((1,), (4,), (mixed,), (right,), *scratch[4 * count + 7 :])
+    for k in range(AHEAD):
         core_copy(k).start()
+    start()
     own = pltpu.make_async_copy(gains.at[lax.rem(me, 4)], gain_got.at[me], own_sem)
     own.start()
 
@@ -1169,40 +1145,77 @@
     def _(step):
         gain_copy(step).start()
 
-    @pl.when((z == 0) | (z == 3))
+    def meet(k):
+        @pl.when(outer)
+        def _():
+            if k >= LAG:
+                outward(k - LAG).wait_recv()
+                across(k - LAG).start()
+
+        if k < 1 or k > total:
+            return
+        i, rows = at(k - 1)
+
+        @pl.when(jnp.logical_not(outer))
+        def _():
+            middle(k - 1).wait_recv()
+            value = wide(z_sent[i][rows]) + wide(mid_got[i][rows])
+            outs[i][y, rows] = value.astype(jnp.bfloat16)
+            outward(k - 1).start()
+            across(k - 1).start()
+
+    for k in range(total):
+        i, rows = at(k)
+        if 2 <= k < 6:
+            turn(1)
+        if k == late - AHEAD:
+            end()
+            for half in range(2):
+                block = left[0:128, half * 256 : (half + 1) * 256]
+                value = lax.dot_general(
+                    block, right[0], CONTRACT_FIRST, preferred_element_type=jnp.float32
+                )
+                for source in range(1, 4):
+                    block = left[source * 128 : (source + 1) * 128, half * 256 : (half + 1) * 256]
+                    value += lax.dot_general(
+                        block, right[source], CONTRACT_FIRST, preferred_element_type=jnp.float32
+                    )
+                last[half] = value.astype(jnp.bfloat16)
+        if k + AHEAD < total:
+            core_copy(k + AHEAD).start()
+        core_copy(k).wait_recv()
+        value = wide(parts[i][core, rows]) + wide(core_got[i][rows])
+
+        @pl.when(outer)
+        def _():
+            z_sent[i][rows] = value.astype(jnp.bfloat16)
+            inward(k).start()
+
+        @pl.when(jnp.logical_not(outer))
+        def _():
+            inward(k).wait_recv()
+            z_sent[i][rows] = (value + wide(z_got[i][rows])).astype(jnp.bfloat16)
+            middle(k).start()
+
+        meet(k)
+
+    for k in range(total, total + LAG):
+        if k > total:
+
+            @pl.when(outer)
+            def _():
+                outward(k - LAG).wait_recv()
+                across(k - LAG).start()
+        else:
+            meet(k)
+
+    @pl.when(outer)
     def _():
         for k in range(total):
-            i, rows = at(k)
-            core_copy(k).wait_recv()
-            value = wide(parts[i][core, rows]) + wide(core_got[i][rows])
-            z_sent[i][rows] = value.astype(jnp.bfloat16)
-            inward(k).start()
-        for k in range(total):
-            outward(k).wait_recv()
-            across(k).start()
-        for k in range(total):
             inward(k).wait_send()
 
-    @pl.when((z == 1) | (z == 2))
+    @pl.when(jnp.logical_not(outer))
     def _():
-        def meet(k):
-            i, rows = at(k)
-            middle(k).wait_recv()
-            value = wide(z_sent[i][rows]) + wide(mid_got[i][rows])
-            outs[i][y, rows] = value.astype(jnp.bfloat16)
-            outward(k).start()
-            across(k).start()
-
-        for k in range(total):
-            i, rows = at(k)
-            core_copy(k).wait_recv()
-            inward(k).wait_recv()
-            value = wide(parts[i][core, rows]) + wide(core_got[i][rows]) + wide(z_got[i][rows])
-            z_sent[i][rows] = value.astype(jnp.bfloat16)
-            middle(k).start()
-            if k > 0:
-                meet(k - 1)
-        meet(total - 1)
         for k in range(total):
             middle(k).wait_send()
             outward(k).wait_send()
@@ -1220,19 +1233,22 @@
         gain_copy(step).wait()
 
 
-def finish(parts, gains, cuts, collective_id):
+def finish(parts, mixed, left, gains, cuts, collective_id):
+    tokens, width = mixed.shape
+    shapes = [part.shape for part in parts]
+    shapes.append((2, left.shape[1] // 2, width // 2))
+    count = len(shapes)
     chunks = [
-        (i, low, high) for i, cut in enumerate(cuts) for low, high in spans(parts[i].shape[1], cut)
+        (i, low, high) for i, cut in enumerate(cuts) for low, high in spans(shapes[i][1], cut)
     ]
-    shapes = [part.shape for part in parts]
     buffers = [pltpu.VMEM(shape[1:], jnp.bfloat16) for shape in shapes]
     in_vmem = pl.BlockSpec(memory_space=pltpu.VMEM)
     return pl.pallas_call(
-        functools.partial(finish_kernel, chunks, len(parts)),
+        functools.partial(finish_kernel, chunks, count),
         out_shape=[jax.ShapeDtypeStruct(shape, jnp.bfloat16) for shape in shapes]
         + [jax.ShapeDtypeStruct((32, 8, gains.shape[2]), jnp.float32)],
-        in_specs=[in_vmem] * (len(parts) + 1),
-        out_specs=[in_vmem] * (len(parts) + 1),
+        in_specs=[in_vmem] * (count + 2),
+        out_specs=[in_vmem] * (count + 1),
         scratch_shapes=buffers * 4
         + [
             pltpu.SemaphoreType.DMA((5 * len(chunks),)),
@@ -1240,13 +1256,18 @@
             pltpu.SemaphoreType.DMA((32,)),
             pltpu.SemaphoreType.DMA((32,)),
             pltpu.SemaphoreType.DMA,
+            pltpu.VMEM(shapes[-1], jnp.bfloat16),
+            pltpu.VMEM((4, tokens, width // 2), jnp.bfloat16),
+            pltpu.SemaphoreType.DMA((12,)),
+            pltpu.SemaphoreType.DMA((12,)),
+            pltpu.SemaphoreType.DMA((1,)),
         ],
         compiler_params=pltpu.CompilerParams(
             collective_id=collective_id,
             has_side_effects=True,
-            vmem_limit_bytes=48 * 1024 * 1024,
+            vmem_limit_bytes=56 * 1024 * 1024,
         ),
-    )(*parts, gains)
+    )(*parts, mixed, left, gains)
 
 
 def core_blocks(left, right):
@@ -1364,11 +1385,9 @@
         lift_right, normed_two_left, gate_left, context_left, normed_left, seed_right, middle_right = (
             sides
         )
-        (mixed_right,) = plane((mixed_grad,), (1,), (mixed_grad.shape[1] // 2,), (4,), 7)
         lift_part = core_blocks(normed_two_left, lift_right)
         down_part = core_blocks(gate_left, seed_right)
         out_part = core_blocks(context_left, middle_right)
-        proj_part = core_blocks(normed_left, mixed_right)
     else:
         normed_two_part, gate_part, context_part, normed_part = group_columns(
             (normed_two_low, gate_low, context_low, normed_low)
@@ -1395,7 +1414,7 @@
         shares = gain_grads.reshape(2, fsdp_count, gain_width).transpose(1, 0, 2)
         shares = jnp.concatenate([shares, jnp.zeros((fsdp_count, 6, gain_width))], axis=1)
         lift_sum, down_sum, out_sum, proj_sum, gain_got = finish(
-            (lift_part, down_part, out_part, proj_part), shares, (8, 4, 2, 4), 8
+            (lift_part, down_part, out_part), mixed_grad, normed_left, shares, (8, 4, 2, 4), 8
         )
         lift_sum = joined_halves(lift_sum, lifted_width)
         down_sum = joined_halves(down_sum, model_width)

time: 383 us -> 363 us (0.948)
  Pallas kernels: 303 us -> 284 us
    pallas_call x2 -> x1, Pallas kernels: 119 us -> 100 us  [finish(): pl.pallas_call(functools.partial(finish_kernel, chunks, count), out_shape...]
    dot_general x4 -> x3, matrix products: 8.24 us -> 6.45 us  [weight_grad(): jnp.einsum('tw,tf->wf', left, right, preferred_element_type=jnp.float32)]
where the time goes in v6:
time: 363 us; the launch traced here: 359 us
  Pallas kernels  284 us (78%)
  matrix products  32.2 us (9%)
  local copies, waits for them, and re-layouts  23.7 us (7%)
  other arithmetic  17.4 us (5%)
    pallas_call x1, Pallas kernels, forward_heads(): pl.pallas_call(functools.partial(forward_kernel, cuts, scaling), out_shap...  106 us
    pallas_call x1, Pallas kernels, finish(): pl.pallas_call(functools.partial(finish_kernel, chunks, count), out_shape...  100 us
    pallas_call x1, Pallas kernels, back_heads(): pl.pallas_call(functools.partial(back_kernel, kinds, cuts, scaling), out_...  77.8 us
    convert_element_type x4, other arithmetic, joined_halves(): jnp.concatenate([out[0], out[1][:, skip:]], axis=1).astype(jnp.float32)  7.74 us

profile of v6, /device:TPU:0, one launch (start us, length us, event | category | flops | bytes accessed | tf_op | source)
XLA Modules:
  0.0 358.7 jit_solution(8543944779892349517)
XLA Ops:
  4.6 105.7 %shard_map.143 = (bf16[128,1024]{1,0:T(8,128)(2,1)}, bf16[4,16,256]{2,1,0:T(8,128)(2,1)}, bf16[32,96,128]{2,1,0:T(8,128)(2,1)}, f32[1024,128]{1,0:T(8,128)}, f32...) custom-call(bf16[128,1024]{1,0:T(8,128)(2,1)} %bitcast.111, ...), custom_call_target="tpu_custom_call" | custom-call | tf_op jit(solution)/shard_map/pallas_call | solution.py:562
  113.2 1.5 fusion.34
  115.9 5.9 %fusion.35 = f32[128,5248]{1,0:T(8,128)S(1)} fusion(bf16[128,1024]{1,0:T(8,128)(2,1)S(1)} %bitcast.123, bf16[1024,5248]{1,0:T(8,128)(2,1)} %bitcast.104), kind=kOutput, calls=%fused_computation.103 | convolution fusion | flops 1375731712 | bytes 13697024 | tf_op jit(solution)/shard_map/dot_general | solution.py:1350
  121.9 3.9 %fusion.20 = (f32[128,2624]{1,0:T(8,128)S(1)}, f32[128,2624]{1,0:T(8,128)S(1)}, f32[128,2624]{1,0:T(8,128)S(1)}) fusion(f32[128,5248]{1,0:T(8,128)S(1)} %fusion.35, bf16[2624,1024]{1,0:T(8,128)(2,1)S(1)} %bitcast.118, bf16[128,1024]{1,0:T(8,128)(2,1)S(1)} %bitcast.128), kind=kOutput, calls=%fused_computation.66 | convolution fusion | flops 709697536 | bytes 11010048 | tf_op jit(solution)/shard_map/td,fd->tf/dot_general | solution.py:1360
  128.1 3.7 %multiply_reduce_fusion = (f32[1024]{0:T(1024)S(1)}, f32[2,64]{1,0:T(2,128)S(1)}, f32[2,64,1024]{2,1,0:T(8,128)S(1)}) fusion(f32[2,64,1024]{2,1,0:T(8,128)S(1)} %get-tuple-element.95, f32[2,64]{1,0:T(2,128)S(1)} %fusion.25, f32[2,64]{1,0:T(2,128)S(1)} %broadcast_multiply_fusion.3, f32[1024]{0:T(1024)S(1)} %bitcast.141, ...), kind=kOutput, calls=%fused_computation.60 | convolution fusion | flops 1376648064 | bytes 13149696 | tf_op jit(solution)/shard_map/tf,wf->tw/dot_general | solution.py:1362
  133.7 1.5 convolution_convert_fusion
  135.3 1.3 reshape.342
  139.1 1.9 fusion.18
  141.0 1.3 copy.28.refs_4_
  142.4 1.3 copy.29.refs_5_
  143.8 77.8 %shard_map.144 = (bf16[32,96,128]{2,1,0:T(8,128)(2,1)}, bf16[4,128,2688]{2,1,0:T(8,128)(2,1)}, bf16[4,128,512]{2,1,0:T(8,128)(2,1)}, bf16[4,128,1312]{2,1,0:T(8,...) custom-call(bf16[32,32,128]{2,1,0:T(8,128)(2,1)} %pad_maximum_fusion, ...), custom_call_target="tpu_custom_call" | custom-call | tf_op jit(solution)/shard_map/pallas_call | solution.py:748
  221.5 1.5 fusion.29
  225.1 1.3 dot_general.50
  226.5 5.1 %fusion.14 = (f32[2,64]{1,0:T(2,128)S(1)}, f32[2,64]{1,0:T(2,128)S(1)}, f32[2,64,1024]{2,1,0:T(8,128)S(1)}) fusion(bf16[2,64,1024]{2,1,0:T(8,128)(2,1)S(1)} %copy-done.1, f32[2,64]{1,0:T(2,128)S(1)} %get-tuple-element.100, f32[1024]{0:T(1024)S(1)} %bitcast.137, bf16[2,64,3072]{2,1,0:T(8,128)(2,1)S(1)} %dot_general.50, bf16[1024,3072,1]{1,0,2:T(8,128)(2,1)} %bitcast.109), kind=kOutput, calls=%fused_computation.49 | convolution fusion | flops 806223616 | bytes 7869952 | tf_op jit(solution)/shard_map/tm,wm->tw/dot_general | solution.py:1407
  232.7 1.3 fusion.7
  233.9 2.0 fusion
  236.0 3.2 bitcast_convert_fusion
  239.2 1.8 reshape.355.refs_3_
  241.1 100.4 %shard_map.145 = (bf16[2,256,2688]{2,1,0:T(8,128)(2,1)}, bf16[2,656,512]{2,1,0:T(8,128)(2,1)}, bf16[2,256,512]{2,1,0:T(8,128)(2,1)}, bf16[2,256,1536]{2,1,0:T(8,128)(2,1)}, f32[32,8,256]{2,1,0:T(8,128)}) custom-call(bf16[2,256,2688]{2,1,0:T(8,128)(2,1)} %bitcast.110, bf16[2,656,512]{2,1,0:T(8,128)(2,1)} %bitcast.134, bf16[2,256,512]{2,1,0:T(8,128)(2,1)} %bitcast.136, ...), custom_call_target="tpu_custom_call" | custom-call | tf_op jit(solution)/shard_map/pallas_call | solution.py:1246
  341.4 1.4 slice_bitcast_fusion.5
  342.8 1.9 maximum_convert_fusion.2
  345.9 2.7 maximum_convert_fusion
  350.6 2.0 maximum_convert_fusion.1
  354.3 4.1 %fusion.9 = bf16[2,64,1024]{2,1,0:T(8,128)(2,1)} fusion(f32[2,64,1024]{2,1,0:T(8,128)S(1)} %get-tuple-element.95, bf16[2,64,2624]{2,1,0:T(8,128)(2,1)S(1)} %bitcast.114, bf16[2624,1024,1]{1,0,2:T(8,128)(2,1)} %bitcast.115), kind=kOutput, calls=%fused_computation.34 | convolution fusion | flops 688128000 | bytes 6832128 | tf_op jit(solution)/shard_map/dot_general | solution.py:1355
  (119 shorter events, 22.6 us)
Async XLA Ops:
  111.5 1.7 copy-start.2
  115.7 6.1 %slice-start.3 = ((s8[5373952]{0:T(1024)(128)(4,1)}), s8[4194304]{0:T(1024)(128)(4,1)S(1)}, s32[]{:S(2)}) async-start(s8[5373952]{0:T(1024)(128)(4,1)} %bitcast.116), calls=%async_computation.3 | async-start | bytes 8388608
  115.9 5.9 %copy-start.10 = (bf16[2,64,1024]{2,1,0:T(8,128)(2,1)}, bf16[2,64,1024]{2,1,0:T(8,128)(2,1)S(1)}, u32[]{:S(2)}) copy-start(bf16[2,64,1024]{2,1,0:T(8,128)(2,1)S(1)} %multiply_convert_fusion.1) | copy-start | bytes 786436
  115.9 5.9 %slice-start.4 = ((s8[5373952]{0:T(1024)(128)(4,1)}), s8[1179648]{0:T(1024)(128)(4,1)S(1)}, s32[]{:S(2)}) async-start(s8[5373952]{0:T(1024)(128)(4,1)} %bitcast.116), calls=%async_computation.4 | async-start | bytes 2359296
  115.9 5.9 %copy-start.14 = (bf16[2,64,1024]{2,1,0:T(8,128)(2,1)S(1)}, bf16[2,64,1024]{2,1,0:T(8,128)(2,1)}, u32[]{:S(2)}) copy-start(bf16[2,64,1024]{2,1,0:T(8,128)(2,1)} %param.15) | copy-start | bytes 786436
  115.9 12.2 %slice-start = ((s8[10747904]{0:T(1024)(128)(4,1)}), s8[4194304]{0:T(1024)(128)(4,1)S(1)}, s32[]{:S(2)}) async-start(s8[10747904]{0:T(1024)(128)(4,1)} %bitcast.105), calls=%async_computation | async-start | bytes 8388608
  121.9 6.2 %slice-start.1 = ((s8[10747904]{0:T(1024)(128)(4,1)}), s8[4194304]{0:T(1024)(128)(4,1)S(1)}, s32[]{:S(2)}) async-start(s8[10747904]{0:T(1024)(128)(4,1)} %bitcast.105), calls=%async_computation.1 | async-start | bytes 8388608
  121.9 6.2 %slice-start.2 = ((s8[10747904]{0:T(1024)(128)(4,1)}), s8[2359296]{0:T(1024)(128)(4,1)S(1)}, s32[]{:S(2)}) async-start(s8[10747904]{0:T(1024)(128)(4,1)} %bitcast.105), calls=%async_computation.2 | async-start | bytes 4718592
  128.1 3.7 %copy-start = (bf16[128,5248]{1,0:T(8,128)(2,1)}, bf16[128,5248]{1,0:T(8,128)(2,1)S(1)}, u32[]{:S(2)}) copy-start(bf16[128,5248]{1,0:T(8,128)(2,1)S(1)} %add_convert_fusion.refs_6_) | copy-start | bytes 4030468
  226.5 6.2 %copy-start.22 = (bf16[4,128,512]{2,1,0:T(8,128)(2,1)S(1)}, bf16[4,128,512]{2,1,0:T(8,128)(2,1)}, u32[]{:S(2)}) copy-start(bf16[4,128,512]{2,1,0:T(8,128)(2,1)} %get-tuple-element.46) | copy-start | bytes 1572868
  226.5 6.2 %copy-start.23 = (bf16[4,128,512]{2,1,0:T(8,128)(2,1)S(1)}, bf16[4,128,512]{2,1,0:T(8,128)(2,1)}, u32[]{:S(2)}) copy-start(bf16[4,128,512]{2,1,0:T(8,128)(2,1)} %get-tuple-element.47) | copy-start | bytes 1572868
  231.7 4.3 %copy-start.7 = (f32[2,64,1024]{2,1,0:T(8,128)}, f32[2,64,1024]{2,1,0:T(8,128)S(1)}, u32[]{:S(2)}) copy-start(f32[2,64,1024]{2,1,0:T(8,128)S(1)} %get-tuple-element.98) | copy-start | bytes 1572868
  231.7 2.3 copy-start.20
  231.7 2.3 copy-start.21
  233.9 2.0 copy-start.11
  233.9 2.0 copy-start.17
  342.8 2.7 copy-start.12
  345.9 2.8 copy-start.18
  348.6 1.8 copy-start.16
  350.5 2.1 copy-start.19
  350.5 2.7 copy-start.6
  350.5 2.7 copy-start.8
  350.6 2.7 copy-start.15
  352.6 1.7 copy-start.4
  (5 other events, 5.3 us)

commit v7 on v6

--- a/solution.py
+++ b/solution.py
@@ -631,7 +631,7 @@
     mine = pltpu.make_async_copy(sent.at[me], grads.at[me], mine_sem.at[0])
     mine.start()
     start, turn, end = plane_moves(kinds, cuts, parts, outs, *refs[19 + 2 * count :])
-    start()
+    start(0, 1)
     keys[0:1024] = got[:, 0:32, :].reshape(1024, 128)
     keys[1024:2048] = got[:, 32:64, :].reshape(1024, 128)
     values[...] = got[:, 64:96, :].reshape(1024, 128)
@@ -642,6 +642,9 @@
     @pl.loop(1, 32)
     def _(step):
         go_copy(step).wait()
+
+    start(1, 4)
+    turn(2)
 
     def rows_of(block):
         return (
@@ -696,6 +699,7 @@
     def _(block):
         grad_block(block)
 
+    start(4)
     turn(4)
 
     @pl.loop(4, 8)
@@ -1016,8 +1020,8 @@
         step = ref.shape[1] - width
         return ref.at[:, pl.ds(pl.multiple_of(index * step, 128), width)]
 
-    def start():
-        for i, kind in enumerate(kinds):
+    def start(low_part=0, high_part=len(kinds)):
+        for i, kind in list(enumerate(kinds))[low_part:high_part]:
             own = block(i, y if kind else x)
             away = block(i, 1 - y if kind else 1 - x)
             for low, high in spans(outs[i].shape[1], cuts[i]):
@@ -1025,7 +1029,7 @@
                 by_x = send((own if kind else away).at[rows], outs[i].at[1, rows], to_x)
                 by_y = send((away if kind else own).at[rows], outs[i].at[2, rows], to_y)
                 firsts.append((i, rows, by_x, by_y))
-        for i, kind in enumerate(kinds):
+        for i, kind in list(enumerate(kinds))[low_part:high_part]:
             own = block(i, y if kind else x)
             copy = pltpu.make_async_copy(own, outs[i].at[0], own_sem.at[i])
             copy.start()

time: 363 us -> 363 us (level)
  no operation moved by 1% of the time
where the time goes in v7:
time: 363 us; the launch traced here: 359 us
  Pallas kernels  284 us (78%)
  matrix products  32.2 us (9%)
  local copies, waits for them, and re-layouts  23.7 us (7%)
  other arithmetic  17.4 us (5%)
    pallas_call x1, Pallas kernels, forward_heads(): pl.pallas_call(functools.partial(forward_kernel, cuts, scaling), out_shap...  106 us
    pallas_call x1, Pallas kernels, finish(): pl.pallas_call(functools.partial(finish_kernel, chunks, count), out_shape...  100 us
    pallas_call x1, Pallas kernels, back_heads(): pl.pallas_call(functools.partial(back_kernel, kinds, cuts, scaling), out_...  77.8 us
    convert_element_type x4, other arithmetic, joined_halves(): jnp.concatenate([out[0], out[1][:, skip:]], axis=1).astype(jnp.float32)  7.74 us

profile of v7, /device:TPU:0, one launch (start us, length us, event | category | flops | bytes accessed | tf_op | source)
XLA Modules:
  0.0 358.7 jit_solution(3448555278169524571)
XLA Ops:
  4.6 105.7 %shard_map.143 = (bf16[128,1024]{1,0:T(8,128)(2,1)}, bf16[4,16,256]{2,1,0:T(8,128)(2,1)}, bf16[32,96,128]{2,1,0:T(8,128)(2,1)}, f32[1024,128]{1,0:T(8,128)}, f32...) custom-call(bf16[128,1024]{1,0:T(8,128)(2,1)} %bitcast.111, ...), custom_call_target="tpu_custom_call" | custom-call | tf_op jit(solution)/shard_map/pallas_call | solution.py:562
  113.2 1.5 fusion.34
  115.9 5.9 %fusion.35 = f32[128,5248]{1,0:T(8,128)S(1)} fusion(bf16[128,1024]{1,0:T(8,128)(2,1)S(1)} %bitcast.123, bf16[1024,5248]{1,0:T(8,128)(2,1)} %bitcast.104), kind=kOutput, calls=%fused_computation.103 | convolution fusion | flops 1375731712 | bytes 13697024 | tf_op jit(solution)/shard_map/dot_general | solution.py:1354
  121.9 3.9 %fusion.20 = (f32[128,2624]{1,0:T(8,128)S(1)}, f32[128,2624]{1,0:T(8,128)S(1)}, f32[128,2624]{1,0:T(8,128)S(1)}) fusion(f32[128,5248]{1,0:T(8,128)S(1)} %fusion.35, bf16[2624,1024]{1,0:T(8,128)(2,1)S(1)} %bitcast.118, bf16[128,1024]{1,0:T(8,128)(2,1)S(1)} %bitcast.128), kind=kOutput, calls=%fused_computation.66 | convolution fusion | flops 709697536 | bytes 11010048 | tf_op jit(solution)/shard_map/td,fd->tf/dot_general | solution.py:1364
  128.1 3.7 %multiply_reduce_fusion = (f32[1024]{0:T(1024)S(1)}, f32[2,64]{1,0:T(2,128)S(1)}, f32[2,64,1024]{2,1,0:T(8,128)S(1)}) fusion(f32[2,64,1024]{2,1,0:T(8,128)S(1)} %get-tuple-element.95, f32[2,64]{1,0:T(2,128)S(1)} %fusion.25, f32[2,64]{1,0:T(2,128)S(1)} %broadcast_multiply_fusion.3, f32[1024]{0:T(1024)S(1)} %bitcast.141, ...), kind=kOutput, calls=%fused_computation.60 | convolution fusion | flops 1376648064 | bytes 13149696 | tf_op jit(solution)/shard_map/tf,wf->tw/dot_general | solution.py:1366
  133.7 1.5 convolution_convert_fusion
  135.3 1.3 reshape.342
  139.1 1.9 fusion.18
  141.0 1.3 copy.28.refs_4_
  142.4 1.3 copy.29.refs_5_
  143.8 77.8 %shard_map.144 = (bf16[32,96,128]{2,1,0:T(8,128)(2,1)}, bf16[4,128,2688]{2,1,0:T(8,128)(2,1)}, bf16[4,128,512]{2,1,0:T(8,128)(2,1)}, bf16[4,128,1312]{2,1,0:T(8,...) custom-call(bf16[32,32,128]{2,1,0:T(8,128)(2,1)} %pad_maximum_fusion, ...), custom_call_target="tpu_custom_call" | custom-call | tf_op jit(solution)/shard_map/pallas_call | solution.py:752
  221.5 1.5 fusion.29
  225.1 1.3 dot_general.50
  226.5 5.1 %fusion.14 = (f32[2,64]{1,0:T(2,128)S(1)}, f32[2,64]{1,0:T(2,128)S(1)}, f32[2,64,1024]{2,1,0:T(8,128)S(1)}) fusion(bf16[2,64,1024]{2,1,0:T(8,128)(2,1)S(1)} %copy-done.1, f32[2,64]{1,0:T(2,128)S(1)} %get-tuple-element.100, f32[1024]{0:T(1024)S(1)} %bitcast.137, bf16[2,64,3072]{2,1,0:T(8,128)(2,1)S(1)} %dot_general.50, bf16[1024,3072,1]{1,0,2:T(8,128)(2,1)} %bitcast.109), kind=kOutput, calls=%fused_computation.49 | convolution fusion | flops 806223616 | bytes 7869952 | tf_op jit(solution)/shard_map/tm,wm->tw/dot_general | solution.py:1411
  232.7 1.3 fusion.7
  233.9 2.0 fusion
  236.0 3.2 bitcast_convert_fusion
  239.2 1.8 reshape.355.refs_3_
  241.1 100.4 %shard_map.145 = (bf16[2,256,2688]{2,1,0:T(8,128)(2,1)}, bf16[2,656,512]{2,1,0:T(8,128)(2,1)}, bf16[2,256,512]{2,1,0:T(8,128)(2,1)}, bf16[2,256,1536]{2,1,0:T(8,128)(2,1)}, f32[32,8,256]{2,1,0:T(8,128)}) custom-call(bf16[2,256,2688]{2,1,0:T(8,128)(2,1)} %bitcast.110, bf16[2,656,512]{2,1,0:T(8,128)(2,1)} %bitcast.134, bf16[2,256,512]{2,1,0:T(8,128)(2,1)} %bitcast.136, ...), custom_call_target="tpu_custom_call" | custom-call | tf_op jit(solution)/shard_map/pallas_call | solution.py:1250
  341.4 1.4 slice_bitcast_fusion.5
  342.8 1.9 maximum_convert_fusion.2
  345.9 2.7 maximum_convert_fusion
  350.6 2.0 maximum_convert_fusion.1
  354.3 4.1 %fusion.9 = bf16[2,64,1024]{2,1,0:T(8,128)(2,1)} fusion(f32[2,64,1024]{2,1,0:T(8,128)S(1)} %get-tuple-element.95, bf16[2,64,2624]{2,1,0:T(8,128)(2,1)S(1)} %bitcast.114, bf16[2624,1024,1]{1,0,2:T(8,128)(2,1)} %bitcast.115), kind=kOutput, calls=%fused_computation.34 | convolution fusion | flops 688128000 | bytes 6832128 | tf_op jit(solution)/shard_map/dot_general | solution.py:1359
  (119 shorter events, 22.6 us)
Async XLA Ops:
  111.5 1.7 copy-start.2
  115.7 6.1 %slice-start.3 = ((s8[5373952]{0:T(1024)(128)(4,1)}), s8[4194304]{0:T(1024)(128)(4,1)S(1)}, s32[]{:S(2)}) async-start(s8[5373952]{0:T(1024)(128)(4,1)} %bitcast.116), calls=%async_computation.3 | async-start | bytes 8388608
  115.9 5.9 %copy-start.10 = (bf16[2,64,1024]{2,1,0:T(8,128)(2,1)}, bf16[2,64,1024]{2,1,0:T(8,128)(2,1)S(1)}, u32[]{:S(2)}) copy-start(bf16[2,64,1024]{2,1,0:T(8,128)(2,1)S(1)} %multiply_convert_fusion.1) | copy-start | bytes 786436
  115.9 5.9 %slice-start.4 = ((s8[5373952]{0:T(1024)(128)(4,1)}), s8[1179648]{0:T(1024)(128)(4,1)S(1)}, s32[]{:S(2)}) async-start(s8[5373952]{0:T(1024)(128)(4,1)} %bitcast.116), calls=%async_computation.4 | async-start | bytes 2359296
  115.9 5.9 %copy-start.14 = (bf16[2,64,1024]{2,1,0:T(8,128)(2,1)S(1)}, bf16[2,64,1024]{2,1,0:T(8,128)(2,1)}, u32[]{:S(2)}) copy-start(bf16[2,64,1024]{2,1,0:T(8,128)(2,1)} %param.15) | copy-start | bytes 786436
  115.9 12.2 %slice-start = ((s8[10747904]{0:T(1024)(128)(4,1)}), s8[4194304]{0:T(1024)(128)(4,1)S(1)}, s32[]{:S(2)}) async-start(s8[10747904]{0:T(1024)(128)(4,1)} %bitcast.105), calls=%async_computation | async-start | bytes 8388608
  121.9 6.2 %slice-start.1 = ((s8[10747904]{0:T(1024)(128)(4,1)}), s8[4194304]{0:T(1024)(128)(4,1)S(1)}, s32[]{:S(2)}) async-start(s8[10747904]{0:T(1024)(128)(4,1)} %bitcast.105), calls=%async_computation.1 | async-start | bytes 8388608
  121.9 6.2 %slice-start.2 = ((s8[10747904]{0:T(1024)(128)(4,1)}), s8[2359296]{0:T(1024)(128)(4,1)S(1)}, s32[]{:S(2)}) async-start(s8[10747904]{0:T(1024)(128)(4,1)} %bitcast.105), calls=%async_computation.2 | async-start | bytes 4718592
  128.1 3.7 %copy-start = (bf16[128,5248]{1,0:T(8,128)(2,1)}, bf16[128,5248]{1,0:T(8,128)(2,1)S(1)}, u32[]{:S(2)}) copy-start(bf16[128,5248]{1,0:T(8,128)(2,1)S(1)} %add_convert_fusion.refs_6_) | copy-start | bytes 4030468
  226.5 6.2 %copy-start.22 = (bf16[4,128,512]{2,1,0:T(8,128)(2,1)S(1)}, bf16[4,128,512]{2,1,0:T(8,128)(2,1)}, u32[]{:S(2)}) copy-start(bf16[4,128,512]{2,1,0:T(8,128)(2,1)} %get-tuple-element.46) | copy-start | bytes 1572868
  226.5 6.2 %copy-start.23 = (bf16[4,128,512]{2,1,0:T(8,128)(2,1)S(1)}, bf16[4,128,512]{2,1,0:T(8,128)(2,1)}, u32[]{:S(2)}) copy-start(bf16[4,128,512]{2,1,0:T(8,128)(2,1)} %get-tuple-element.47) | copy-start | bytes 1572868
  231.7 4.3 %copy-start.7 = (f32[2,64,1024]{2,1,0:T(8,128)}, f32[2,64,1024]{2,1,0:T(8,128)S(1)}, u32[]{:S(2)}) copy-start(f32[2,64,1024]{2,1,0:T(8,128)S(1)} %get-tuple-element.98) | copy-start | bytes 1572868
  231.7 2.3 copy-start.20
  231.7 2.3 copy-start.21
  233.9 2.0 copy-start.11
  233.9 2.0 copy-start.17
  342.8 2.7 copy-start.12
  345.9 2.8 copy-start.18
  348.6 1.8 copy-start.16
  350.5 2.1 copy-start.19
  350.5 2.7 copy-start.6
  350.5 2.7 copy-start.8
  350.6 2.7 copy-start.15
  352.6 1.7 copy-start.4
  (5 other events, 5.3 us)
